TPU v7x, 32 devices: a whole 2x2x4 slice. The times are simulated.
32 devices in a mesh: dp: 16 (over z, y, core), tensor: 2 (over x).
Axes of the slice: x: 2, y: 2, z: 4, core: 2. Of those that a mesh axis runs over, the one named last changes fastest.
Arguments:
- inputs: bfloat16 [49152, 1024], P('dp'), may hold values from -6 to 6
- segment_ids: int32 [16, 3072], P('dp'), may hold values from 0 to 5, never falling along the last dimension, each value on 1 to 1024 neighbouring positions
- cotangent: bfloat16 [49152, 1024], P('dp', 'tensor'), may hold values from -6 to 6
- ln1_gain: bfloat16 [1024], replicated, may hold values from 0.5 to 1.5
- attention_norm_bias: bfloat16 [1024], replicated, may hold values from -3 to 3
- ln2_gain: bfloat16 [1024], replicated, may hold values from 0.5 to 1.5
- feedforward_norm_bias: bfloat16 [1024], replicated, may hold values from -3 to 3
- w_qkv: bfloat16 [1024, 3, 1024], P(None, None, 'tensor'), may hold values from -0.1875 to 0.1875
- b_qkv: bfloat16 [3, 1024], P(None, 'tensor'), may hold values from -3 to 3
- w_dense: bfloat16 [1024, 1024], P('tensor'), may hold values from -0.75 to 0.75
- b_dense: bfloat16 [1024], P('tensor'), may hold values from -3 to 3
- w_fc1: bfloat16 [1024, 4096], P(None, 'tensor'), may hold values from -0.1875 to 0.1875
- b_fc1: bfloat16 [4096], P('tensor'), may hold values from -3 to 3
- w_fc2: bfloat16 [4096, 1024], P('tensor'), may hold values from -0.09375 to 0.09375
- b_fc2: bfloat16 [1024], P('tensor'), may hold values from -3 to 3
Outputs:
- outputs: bfloat16 [49152, 1024], P('dp', 'tensor')
- input_grad: float32 [49152, 1024], P('dp', 'tensor')
- ln1_gain_grad: float32 [1024], replicated
- ln1_bias_grad: float32 [1024], replicated
- ln2_gain_grad: float32 [1024], replicated
- ln2_bias_grad: float32 [1024], replicated
- qkv_weight_grad: float32 [1024, 3, 1024], P(None, None, 'tensor')
- qkv_bias_grad: float32 [3, 1024], P(None, 'tensor')
- dense_weight_grad: float32 [1024, 1024], P('tensor')
- dense_bias_grad: float32 [1024], P('tensor')
- fc1_weight_grad: float32 [1024, 4096], P(None, 'tensor')
- fc1_bias_grad: float32 [4096], P('tensor')
- fc2_weight_grad: float32 [4096, 1024], P('tensor')
- fc2_bias_grad: float32 [1024], P('tensor')
Inputs may be any that keep to these rules, and one draw needn't show every extreme that they name: `segment_ids`: in each pack of 3072 tokens the segment numbers never fall and run over 0 to 5; every segment has 1 to 1024 tokens, and one has exactly 1024.
All inputs are finite; a program needn't handle non-finite values.
Results may differ from a plain program's by a relative error of at most 0.012.
The roundings to bfloat16 on the way count: a program that leaves them out, or rounds other values in their place, can miss the bound.
Values may be sent and summed in bfloat16 or wider, within the bound.
No kernel may reach another device: no remote copies, remote signals or barrier semaphores. Data moves between devices by JAX's collectives and lax.ppermute only.
A program may use at most 320 MiB of HBM per device.

v0:
```python
import jax
import jax.numpy as jnp
from jax import lax
from jax.sharding import PartitionSpec as P

HEAD_DIM = 64
ROT = 16
MOST = 1024
BLOCK = 512


NORM_EPS = 1e-05
MASKED = -1e30


def apply_layer_norm(values, gain, shift):
    centred = values - jnp.mean(values, axis=-1, keepdims=True)
    root_inv = lax.rsqrt(jnp.mean(centred * centred, axis=-1, keepdims=True) + NORM_EPS)
    normed = centred * root_inv
    return (normed, root_inv, normed * gain + shift)


def layer_norm_backward(normed_grad, normed, root_inv, gain):
    scaled = normed_grad * gain
    inner = jnp.mean(scaled * normed, axis=-1, keepdims=True)
    return root_inv * (scaled - jnp.mean(scaled, axis=-1, keepdims=True) - normed * inner)


def rotary_tables(segments):
    length = segments.shape[0]
    places = jnp.arange(length, dtype=jnp.int32)
    first = jnp.concatenate([jnp.ones((1,), dtype=bool), segments[1:] != segments[:-1]])
    starts = lax.cummax(jnp.where(first, places, jnp.zeros_like(places)), axis=0)
    offsets = (places - starts).astype(jnp.float32)
    inverse = 10000.0 ** (-jnp.arange(0, ROT, 2).astype(jnp.float32) / ROT)
    angles = offsets[:, None] * inverse[None, :]
    cosine = jnp.concatenate([jnp.cos(angles), jnp.cos(angles)], axis=-1)
    sine = jnp.concatenate([jnp.sin(angles), jnp.sin(angles)], axis=-1)
    return (cosine, sine)


def rotate(values, cosine, sine):
    half = ROT // 2
    part = values[..., :ROT]
    turned = jnp.concatenate([-part[..., half:], part[..., :half]], axis=-1)
    moved = part * cosine[:, None, :] + turned * sine[:, None, :]
    return jnp.concatenate([moved, values[..., ROT:]], axis=-1)


def rotate_back(grads, cosine, sine):
    half = ROT // 2
    part = grads[..., :ROT]
    scaled = part * sine[:, None, :]
    turned = jnp.concatenate([scaled[..., half:], -scaled[..., :half]], axis=-1)
    moved = part * cosine[:, None, :] + turned
    return jnp.concatenate([moved, grads[..., ROT:]], axis=-1)


def gelu_slope(hidden):
    cumulative = 0.5 * (1.0 + lax.erf(hidden * 0.7071067811865476))
    density = jnp.exp(-0.5 * hidden * hidden) * 0.3989422804014327
    return cumulative + hidden * density


def on_device(
    inputs,
    segment_ids,
    cotangent,
    ln1_gain,
    attention_norm_bias,
    ln2_gain,
    feedforward_norm_bias,
    w_qkv,
    b_qkv,
    w_dense,
    b_dense,
    w_fc1,
    b_fc1,
    w_fc2,
    b_fc2,
):
    segments = segment_ids[0]
    length = inputs.shape[0]
    width = inputs.shape[1]
    local = w_qkv.shape[2]
    heads = local // HEAD_DIM
    scale = HEAD_DIM ** (-0.5)
    blocks = length // BLOCK
    span = MOST + BLOCK
    cosine, sine = rotary_tables(segments)
    places = jnp.arange(length, dtype=jnp.int32)
    residual_stream = inputs.astype(jnp.float32)
    attention_norm_gain = ln1_gain.astype(jnp.float32)
    feedforward_norm_gain = ln2_gain.astype(jnp.float32)
    attention_standardized, attention_inverse_root, attention_normed = apply_layer_norm(
        residual_stream, attention_norm_gain, attention_norm_bias.astype(jnp.float32)
    )
    feedforward_standardized, feedforward_inverse_root, feedforward_normed = apply_layer_norm(
        residual_stream, feedforward_norm_gain, feedforward_norm_bias.astype(jnp.float32)
    )
    attention_normed = attention_normed.astype(jnp.bfloat16)
    feedforward_normed = feedforward_normed.astype(jnp.bfloat16)
    qkv_matrix = w_qkv.reshape(width, 3 * local)
    qkv = jnp.dot(attention_normed, qkv_matrix, preferred_element_type=jnp.float32) + b_qkv.reshape(
        3 * local
    ).astype(jnp.float32)
    qkv = qkv.reshape(length, 3, heads, HEAD_DIM)
    query = rotate(qkv[:, 0], cosine, sine).astype(jnp.bfloat16)
    key = rotate(qkv[:, 1], cosine, sine).astype(jnp.bfloat16)
    value = qkv[:, 2].astype(jnp.bfloat16)

    def window_of(start):
        return jnp.clip(start - MOST, 0, length - span)

    def scores_for(start):
        first = window_of(start)
        rows_query = lax.dynamic_slice_in_dim(query, start, BLOCK, 0)
        seg_rows = lax.dynamic_slice_in_dim(segments, start, BLOCK, 0)
        pos_rows = lax.dynamic_slice_in_dim(places, start, BLOCK, 0)
        key_rows = lax.dynamic_slice_in_dim(key, first, span, 0)
        seg_keys = lax.dynamic_slice_in_dim(segments, first, span, 0)
        pos_keys = lax.dynamic_slice_in_dim(places, first, span, 0)
        raw = (
            jnp.einsum("qhd,khd->hqk", rows_query, key_rows, preferred_element_type=jnp.float32)
            * scale
        )
        allowed = (seg_rows[:, None] == seg_keys[None, :]) & (
            pos_keys[None, :] <= pos_rows[:, None]
        )
        return (rows_query, key_rows, first, jnp.where(allowed[None], raw, MASKED))

    def attend(start):
        rows_query, key_rows, first, scores = scores_for(start)
        value_rows = lax.dynamic_slice_in_dim(value, first, span, 0)
        peak = jnp.max(scores, axis=-1, keepdims=True)
        log_total = peak + jnp.log(jnp.sum(jnp.exp(scores - peak), axis=-1, keepdims=True))
        probs = jnp.exp(scores - log_total).astype(jnp.bfloat16)
        return (
            jnp.einsum("hqk,khd->qhd", probs, value_rows, preferred_element_type=jnp.float32),
            log_total,
        )

    starts = jnp.arange(blocks, dtype=jnp.int32) * BLOCK
    mixed, totals = lax.map(attend, starts)
    mixed = mixed.reshape(length, local).astype(jnp.bfloat16)
    attention = jnp.dot(mixed, w_dense, preferred_element_type=jnp.float32)
    hidden = jnp.dot(feedforward_normed, w_fc1, preferred_element_type=jnp.float32) + b_fc1.astype(
        jnp.float32
    )
    active = jax.nn.gelu(hidden, approximate=False).astype(jnp.bfloat16)
    feed = jnp.dot(active, w_fc2, preferred_element_type=jnp.float32)
    summed = lax.psum_scatter(
        attention, "tensor", scatter_dimension=1, tiled=True
    ) + lax.psum_scatter(
        feed.astype(jnp.bfloat16), "tensor", scatter_dimension=1, tiled=True
    ).astype(
        jnp.float32
    )
    own_cols = lax.dynamic_slice_in_dim(residual_stream, lax.axis_index("tensor") * local, local, 1)
    outputs = (own_cols + summed + b_dense.astype(jnp.float32) + b_fc2.astype(jnp.float32)).astype(
        jnp.bfloat16
    )
    out_grad = lax.all_gather(cotangent, "tensor", axis=1, tiled=True)
    out_bias_grad = jnp.sum(cotangent.astype(jnp.float32), axis=0)
    dense_weight_grad = jnp.dot(mixed.T, out_grad, preferred_element_type=jnp.float32)
    fc2_weight_grad = jnp.dot(active.T, out_grad, preferred_element_type=jnp.float32)
    active_grad = jnp.dot(out_grad, w_fc2.T, preferred_element_type=jnp.float32)
    hidden_grad = (active_grad * gelu_slope(hidden)).astype(jnp.bfloat16)
    fc1_weight_grad = jnp.dot(feedforward_normed.T, hidden_grad, preferred_element_type=jnp.float32)
    fc1_bias_grad = jnp.sum(hidden_grad.astype(jnp.float32), axis=0)
    feedforward_normed_grad = jnp.dot(hidden_grad, w_fc1.T, preferred_element_type=jnp.float32)
    mixed_grad = jnp.dot(out_grad, w_dense.T, preferred_element_type=jnp.float32).astype(
        jnp.bfloat16
    )

    def back_step(carry, pieces):
        key_grad, value_grad = carry
        start, log_total, grad_rows = pieces
        rows_query, key_rows, first, scores = scores_for(start)
        value_rows = lax.dynamic_slice_in_dim(value, first, span, 0)
        probs = jnp.exp(scores - log_total)
        value_part = lax.dynamic_slice_in_dim(value_grad, first, span, 0)
        value_part = value_part + jnp.einsum(
            "hqk,qhd->khd",
            probs.astype(jnp.bfloat16),
            grad_rows,
            preferred_element_type=jnp.float32,
        )
        prob_grad = jnp.einsum(
            "qhd,khd->hqk", grad_rows, value_rows, preferred_element_type=jnp.float32
        )
        inner = jnp.sum(probs * prob_grad, axis=-1, keepdims=True)
        score_grad = (probs * (prob_grad - inner)).astype(jnp.bfloat16)
        query_rows = (
            jnp.einsum("hqk,khd->qhd", score_grad, key_rows, preferred_element_type=jnp.float32)
            * scale
        )
        key_part = lax.dynamic_slice_in_dim(key_grad, first, span, 0)
        key_part = (
            key_part
            + jnp.einsum("hqk,qhd->khd", score_grad, rows_query, preferred_element_type=jnp.float32)
            * scale
        )
        key_grad = lax.dynamic_update_slice_in_dim(key_grad, key_part, first, 0)
        value_grad = lax.dynamic_update_slice_in_dim(value_grad, value_part, first, 0)
        return ((key_grad, value_grad), query_rows)

    empty = jnp.zeros((length, heads, HEAD_DIM), jnp.float32)
    grad_blocks = mixed_grad.reshape(blocks, BLOCK, heads, HEAD_DIM)
    (key_grad, value_grad), query_grad = lax.scan(
        back_step, (empty, empty), (starts, totals, grad_blocks)
    )
    query_grad = rotate_back(query_grad.reshape(length, heads, HEAD_DIM), cosine, sine)
    key_grad = rotate_back(key_grad, cosine, sine)
    qkv_grad = (
        jnp.stack([query_grad, key_grad, value_grad], axis=1)
        .reshape(length, 3 * local)
        .astype(jnp.bfloat16)
    )
    qkv_weight_grad = jnp.dot(
        attention_normed.T, qkv_grad, preferred_element_type=jnp.float32
    ).reshape(width, 3, local)
    qkv_bias_grad = jnp.sum(qkv_grad.astype(jnp.float32), axis=0).reshape(3, local)
    attention_normed_grad = jnp.dot(qkv_grad, qkv_matrix.T, preferred_element_type=jnp.float32)
    all_sums = lax.psum(
        (
            qkv_weight_grad,
            qkv_bias_grad,
            dense_weight_grad,
            out_bias_grad,
            fc1_weight_grad,
            fc1_bias_grad,
            fc2_weight_grad,
        ),
        "dp",
    )
    (
        qkv_weight_grad,
        qkv_bias_grad,
        dense_weight_grad,
        dense_bias_grad,
        fc1_weight_grad,
        fc1_bias_grad,
        fc2_weight_grad,
    ) = all_sums
    input_partial_grad = layer_norm_backward(
        attention_normed_grad, attention_standardized, attention_inverse_root, attention_norm_gain
    ) + layer_norm_backward(
        feedforward_normed_grad,
        feedforward_standardized,
        feedforward_inverse_root,
        feedforward_norm_gain,
    )
    input_grad = lax.psum_scatter(
        input_partial_grad, "tensor", scatter_dimension=1, tiled=True
    ) + cotangent.astype(jnp.float32)
    norm_terms = (
        jnp.sum(attention_normed_grad * attention_standardized, axis=0),
        jnp.sum(attention_normed_grad, axis=0),
        jnp.sum(feedforward_normed_grad * feedforward_standardized, axis=0),
        jnp.sum(feedforward_normed_grad, axis=0),
    )
    ln1_gain_grad, ln1_bias_grad, ln2_gain_grad, ln2_bias_grad = lax.psum(
        (norm_terms[0], norm_terms[1], norm_terms[2], norm_terms[3]), ("dp", "tensor")
    )
    return (
        outputs,
        input_grad,
        ln1_gain_grad,
        ln1_bias_grad,
        ln2_gain_grad,
        ln2_bias_grad,
        qkv_weight_grad,
        qkv_bias_grad,
        dense_weight_grad,
        dense_bias_grad,
        fc1_weight_grad,
        fc1_bias_grad,
        fc2_weight_grad,
        dense_bias_grad,
    )


def solution(mesh):
    placed = (
        P("dp", None),
        P("dp", None),
        P("dp", "tensor"),
        P(),
        P(),
        P(),
        P(),
        P(None, None, "tensor"),
        P(None, "tensor"),
        P("tensor", None),
        P("tensor"),
        P(None, "tensor"),
        P("tensor"),
        P("tensor", None),
        P("tensor"),
    )
    return jax.shard_map(
        on_device,
        mesh=mesh,
        in_specs=placed,
        out_specs=(
            P("dp", "tensor"),
            P("dp", "tensor"),
            P(),
            P(),
            P(),
            P(),
            P(None, None, "tensor"),
            P(None, "tensor"),
            P("tensor", None),
            P("tensor"),
            P(None, "tensor"),
            P("tensor"),
            P("tensor", None),
            P("tensor"),
        ),
        check_vma=False,
    )
```

profile of v0, /device:TPU:0, one launch (start us, length us, event | category | flops | bytes accessed | tf_op | source)
XLA Modules:
  0.0 2100.0 jit_solution(7724173197933049781)
XLA Ops:
  14.8 70.0 %fusion.47 = (bf16[3072,2048]{1,0:T(8,128)(2,1)}, f32[3072,2048]{1,0:T(8,128)}) fusion(f32[2048]{0:T(1024)S(1)} %convert_element_type.141, bf16[1024,2048]{1,0:T(8,128)(2,1)S(1)} %copy-done.41, bf16[3072,1024]{1,0:T(8,128)(2,1)S(1)} %copy-done.5, f32[1024]{0:T(1024)S(1)} %convert_element_type.139, f32[1024]{0:T(1024)S(1)} %convert_element_type.138, ...), kind=kOutput, calls=%fused_computation.49 | convolution fusion | flops 13319012352 | bytes 48275456 | tf_op jit(solution)/shard_map/dot_general | solution.py:147
  84.9 17.3 convolution_convert_fusion
  107.1 17.9 convolution_add_fusion
  162.9 252.1 %while.32 = (s32[]{:T(128)}, bf16[6,512,8,64]{1,3,2,0:T(8,128)(2,1)}, f32[6,8,512,1]{2,1,3,0:T(8,128)S(1)}, s32[6]{0:T(128)S(1)}, bf16[3072,8,64]{0,2,1:T(8,128)...) while((s32[]{:T(128)}, ...), condition=%wide.region_7.8_spmd.clone, body=%wide.region_4.0_spmd.clone.sunk | while | flops 1657008128 | bytes 94552856 | solution.py:144
  167.5 15.3 fusion.117
  209.5 15.1 fusion.117
  335.3 15.1 fusion.117
  459.9 909.8 %while.33 = (s32[]{:T(128)}, f32[3072,8,64]{0,2,1:T(8,128)}, f32[3072,8,64]{0,2,1:T(8,128)}, f32[6,512,8,64]{1,0,3,2:T(8,128)}, s32[6]{0:T(128)S(1)}, /*index=5*...) while((s32[]{:T(128)}, f32[3072,8,64]{0,2,1:T(8,128)}, ...), condition=%wide.region_12.13_spmd.clone, body=%wide.region_10.12_spmd.clone.sunk | while | flops 4088131584 | bytes 240256304 | solution.py:210
  478.4 18.8 multiply_reduce_fusion.9
  497.2 22.2 %multiply_convert_fusion.2 = bf16[8,512,1536]{2,1,0:T(8,128)(2,1)} fusion(f32[8,512,1536]{2,1,0:T(8,128)} %get-tuple-element.604, f32[8,512,1536]{2,1,0:T(8,128)} %fusion.127, f32[8,512]{1,0:T(8,128)S(1)} %get-tuple-element.605), kind=kLoop, calls=%fused_computation.15.clone.1 | loop fusion | flops 18874368 | bytes 62930944 | tf_op jit(solution)/shard_map/while/body/eval_jaxpr/convert_element_type | solution.py:193
  529.0 21.9 %dynamic_update_slice.48 = f32[6,512,8,64]{1,0,3,2:T(8,128)} dynamic-update-slice(f32[6,512,8,64]{1,0,3,2:T(8,128)} %get-tuple-element.668, f32[1,512,8,64]{1,0,3,2:T(1,128)S(1)} %copy.58, s32[]{:T(128)} %get-tuple-element.665, s32[]{:T(128)} %constant.168.clone.1..sunk.1, s32[]{:T(128)} %constant.168.clone.1..sunk.1, s32[]{:T(128)} %constant.168.clone.1..sunk.1) | dynamic-update-slice | bytes 2097156 | tf_op jit(solution)/shard_map/while/body/jit(dynamic_update_index_in_dim)/dynamic_update_slice | solution.py:144
  560.8 19.8 dynamic_update_slice.46
  593.8 19.7 dynamic_update_slice.47
  631.2 18.8 multiply_reduce_fusion.9
  650.0 21.7 %multiply_convert_fusion.2 = bf16[8,512,1536]{2,1,0:T(8,128)(2,1)} fusion(f32[8,512,1536]{2,1,0:T(8,128)} %get-tuple-element.604, f32[8,512,1536]{2,1,0:T(8,128)} %fusion.127, f32[8,512]{1,0:T(8,128)S(1)} %get-tuple-element.605), kind=kLoop, calls=%fused_computation.15.clone.1 | loop fusion | flops 18874368 | bytes 62930944 | tf_op jit(solution)/shard_map/while/body/eval_jaxpr/convert_element_type | solution.py:193
  681.2 21.8 %dynamic_update_slice.48 = f32[6,512,8,64]{1,0,3,2:T(8,128)} dynamic-update-slice(f32[6,512,8,64]{1,0,3,2:T(8,128)} %get-tuple-element.668, f32[1,512,8,64]{1,0,3,2:T(1,128)S(1)} %copy.58, s32[]{:T(128)} %get-tuple-element.665, s32[]{:T(128)} %constant.168.clone.1..sunk.1, s32[]{:T(128)} %constant.168.clone.1..sunk.1, s32[]{:T(128)} %constant.168.clone.1..sunk.1) | dynamic-update-slice | bytes 2097156 | tf_op jit(solution)/shard_map/while/body/jit(dynamic_update_index_in_dim)/dynamic_update_slice | solution.py:144
  712.8 19.7 dynamic_update_slice.46
  745.8 19.7 dynamic_update_slice.47
  783.2 18.8 multiply_reduce_fusion.9
  801.9 21.7 %multiply_convert_fusion.2 = bf16[8,512,1536]{2,1,0:T(8,128)(2,1)} fusion(f32[8,512,1536]{2,1,0:T(8,128)} %get-tuple-element.604, f32[8,512,1536]{2,1,0:T(8,128)} %fusion.127, f32[8,512]{1,0:T(8,128)S(1)} %get-tuple-element.605), kind=kLoop, calls=%fused_computation.15.clone.1 | loop fusion | flops 18874368 | bytes 62930944 | tf_op jit(solution)/shard_map/while/body/eval_jaxpr/convert_element_type | solution.py:193
  833.2 21.8 %dynamic_update_slice.48 = f32[6,512,8,64]{1,0,3,2:T(8,128)} dynamic-update-slice(f32[6,512,8,64]{1,0,3,2:T(8,128)} %get-tuple-element.668, f32[1,512,8,64]{1,0,3,2:T(1,128)S(1)} %copy.58, s32[]{:T(128)} %get-tuple-element.665, s32[]{:T(128)} %constant.168.clone.1..sunk.1, s32[]{:T(128)} %constant.168.clone.1..sunk.1, s32[]{:T(128)} %constant.168.clone.1..sunk.1) | dynamic-update-slice | bytes 2097156 | tf_op jit(solution)/shard_map/while/body/jit(dynamic_update_index_in_dim)/dynamic_update_slice | solution.py:144
  864.8 19.7 dynamic_update_slice.46
  897.8 19.7 dynamic_update_slice.47
  935.1 18.8 multiply_reduce_fusion.9
  954.0 21.7 %multiply_convert_fusion.2 = bf16[8,512,1536]{2,1,0:T(8,128)(2,1)} fusion(f32[8,512,1536]{2,1,0:T(8,128)} %get-tuple-element.604, f32[8,512,1536]{2,1,0:T(8,128)} %fusion.127, f32[8,512]{1,0:T(8,128)S(1)} %get-tuple-element.605), kind=kLoop, calls=%fused_computation.15.clone.1 | loop fusion | flops 18874368 | bytes 62930944 | tf_op jit(solution)/shard_map/while/body/eval_jaxpr/convert_element_type | solution.py:193
  985.2 21.8 %dynamic_update_slice.48 = f32[6,512,8,64]{1,0,3,2:T(8,128)} dynamic-update-slice(f32[6,512,8,64]{1,0,3,2:T(8,128)} %get-tuple-element.668, f32[1,512,8,64]{1,0,3,2:T(1,128)S(1)} %copy.58, s32[]{:T(128)} %get-tuple-element.665, s32[]{:T(128)} %constant.168.clone.1..sunk.1, s32[]{:T(128)} %constant.168.clone.1..sunk.1, s32[]{:T(128)} %constant.168.clone.1..sunk.1) | dynamic-update-slice | bytes 2097156 | tf_op jit(solution)/shard_map/while/body/jit(dynamic_update_index_in_dim)/dynamic_update_slice | solution.py:144
  1016.8 19.4 dynamic_update_slice.46
  1049.5 19.4 dynamic_update_slice.47
  1086.5 18.8 multiply_reduce_fusion.9
  1105.3 21.7 %multiply_convert_fusion.2 = bf16[8,512,1536]{2,1,0:T(8,128)(2,1)} fusion(f32[8,512,1536]{2,1,0:T(8,128)} %get-tuple-element.604, f32[8,512,1536]{2,1,0:T(8,128)} %fusion.127, f32[8,512]{1,0:T(8,128)S(1)} %get-tuple-element.605), kind=kLoop, calls=%fused_computation.15.clone.1 | loop fusion | flops 18874368 | bytes 62930944 | tf_op jit(solution)/shard_map/while/body/eval_jaxpr/convert_element_type | solution.py:193
  1136.6 21.8 %dynamic_update_slice.48 = f32[6,512,8,64]{1,0,3,2:T(8,128)} dynamic-update-slice(f32[6,512,8,64]{1,0,3,2:T(8,128)} %get-tuple-element.668, f32[1,512,8,64]{1,0,3,2:T(1,128)S(1)} %copy.58, s32[]{:T(128)} %get-tuple-element.665, s32[]{:T(128)} %constant.168.clone.1..sunk.1, s32[]{:T(128)} %constant.168.clone.1..sunk.1, s32[]{:T(128)} %constant.168.clone.1..sunk.1) | dynamic-update-slice | bytes 2097156 | tf_op jit(solution)/shard_map/while/body/jit(dynamic_update_index_in_dim)/dynamic_update_slice | solution.py:144
  1168.2 19.2 dynamic_update_slice.46
  1200.6 19.2 dynamic_update_slice.47
  1237.5 18.8 multiply_reduce_fusion.9
  1256.3 21.7 %multiply_convert_fusion.2 = bf16[8,512,1536]{2,1,0:T(8,128)(2,1)} fusion(f32[8,512,1536]{2,1,0:T(8,128)} %get-tuple-element.604, f32[8,512,1536]{2,1,0:T(8,128)} %fusion.127, f32[8,512]{1,0:T(8,128)S(1)} %get-tuple-element.605), kind=kLoop, calls=%fused_computation.15.clone.1 | loop fusion | flops 18874368 | bytes 62930944 | tf_op jit(solution)/shard_map/while/body/eval_jaxpr/convert_element_type | solution.py:193
  1287.5 21.8 %dynamic_update_slice.48 = f32[6,512,8,64]{1,0,3,2:T(8,128)} dynamic-update-slice(f32[6,512,8,64]{1,0,3,2:T(8,128)} %get-tuple-element.668, f32[1,512,8,64]{1,0,3,2:T(1,128)S(1)} %copy.58, s32[]{:T(128)} %get-tuple-element.665, s32[]{:T(128)} %constant.168.clone.1..sunk.1, s32[]{:T(128)} %constant.168.clone.1..sunk.1, s32[]{:T(128)} %constant.168.clone.1..sunk.1) | dynamic-update-slice | bytes 2097156 | tf_op jit(solution)/shard_map/while/body/jit(dynamic_update_index_in_dim)/dynamic_update_slice | solution.py:144
  1319.0 18.7 dynamic_update_slice.46
  1350.9 18.7 dynamic_update_slice.47
  1397.4 27.0 %convert_reduce_fusion = (f32[2048]{0:T(1024)}, bf16[3072,2048]{1,0:T(8,128)(2,1)}) fusion(f32[3072,2048]{1,0:T(8,128)} %get-tuple-element.458, f32[2048]{0:T(1024)S(1)} %copy-done.24, bf16[3072,1024]{1,0:T(8,128)(2,1)S(1)} %bitcast.135, bf16[2048,1024]{1,0:T(8,128)(2,1)S(1)} %copy-done.40), kind=kOutput, calls=%fused_computation.56 | convolution fusion | flops 12966688768 | bytes 48250880 | tf_op jit(solution)/shard_map/dot_general | solution.py:167
  1424.4 17.1 fusion.75
  1441.6 22.9 %multiply_reduce_fusion.2 = (f32[1024]{0:T(1024)S(1)}, f32[3072]{0:T(1024)S(1)}, f32[3072]{0:T(1024)S(1)}, f32[1024]{0:T(1024)S(1)}, f32[1024]{0:T(1024)S(1)}, /...) fusion(bf16[3072,1024]{1,0:T(8,128)(2,1)S(1)} %bitcast.117, ...), kind=kOutput, calls=%fused_computation.77 | convolution fusion | flops 9717137408 | bytes 44138496 | tf_op jit(solution)/shard_map/dot_general | solution.py:224
  1483.9 20.5 fusion.77
  1504.4 20.3 fusion.69
  1524.8 18.2 fusion.61
  1552.2 42.6 %all-reduce = (f32[1024]{0:T(1024)}, f32[1024]{0:T(1024)}, f32[1024]{0:T(1024)}, f32[1024]{0:T(1024)}) all-reduce(f32[1024]{0:T(1024)S(1)} %get-tuple-element.366, f32[1024]{0:T(1024)S(1)} %get-tuple-element.371, f32[1024]{0:T(1024)S(1)} %get-tuple-element.375, ...), channel_id=1, replica_groups=mesh['dp'=16,'tensor'=2] {'dp','tensor'}, use_global_device_ids=true, to_apply=%region_19.20 | all-reduce | flops 4096 | bytes 32768 | tf_op jit(solution)/shard_map/psum | solution.py:263
  1604.1 21.3 %reduce-scatter.8.cloned.1.call-done = f32[3072,512]{1,0:T(8,128)} async-done(((f32[3072,1024]{1,0:T(8,128)}), f32[3072,512]{1,0:T(8,128)}) %reduce-scatter.8.cloned.1.call-update) | async-done | bytes 6291472 | tf_op jit(solution)/shard_map/reduce_scatter | solution.py:254
  1633.2 64.6 %all-reduce.1 = (f32[3,512]{1,0:T(4,128)}, f32[512]{0:T(512)S(1)}, f32[2048]{0:T(1024)}) all-reduce(f32[3,512]{1,0:T(4,128)S(1)} %reshape.294, f32[512]{0:T(512)S(1)} %get-tuple-element.443, f32[2048]{0:T(1024)S(1)} %copy-done.25), channel_id=1, replica_groups=mesh['dp'=16,'tensor'=2] {'dp'}, use_global_device_ids=true, to_apply=%region_28.29 | all-reduce | flops 4096 | bytes 32768 | tf_op jit(solution)/shard_map/psum | solution.py:225
  1697.9 377.5 %all-reduce.5.cloned.1.call-done = (f32[1024,3,512]{2,0,1:T(8,128)}, f32[512,1024]{1,0:T(8,128)}, f32[1024,2048]{1,0:T(8,128)}, f32[2048,1024]{1,0:T(8,128)}) async-done(((f32[1024,3,512]{2,0,1:T(8,128)}, f32[512,1024]{1,0:T(8,128)}, f32[1024,2048]{1,0:T(8,128)}, f32[2048,1024]{1,0:T(8,128)}), (f32[1024,3,512]{2,0,1:T(8,128)}, f32[512,1024]{1,0:T(8,128)}, f32[1024,2048]{1,0:T(8,128)}, ...) | async-done | bytes 25165840 | tf_op jit(solution)/shard_map/psum | solution.py:225
  (346 shorter events, 662.5 us)
Async XLA Ops:
  7.2 415.1 %copy-start = (bf16[512,1024]{1,0:T(8,128)(2,1)S(1)}, bf16[512,1024]{1,0:T(8,128)(2,1)}, u32[]{:S(2)}) copy-start(bf16[512,1024]{1,0:T(8,128)(2,1)} %param.28) | copy-start | bytes 3145732
  7.2 7.6 copy-start.33
  7.2 421.6 %all-gather.2.cloned.1.call-start = ((), (), s32[]{:S(2)}) async-start(), calls=%async_computation.5 | async-start | bytes 9437184 | tf_op jit(solution)/shard_map/all_gather | solution.py:163
  8.0 1586.9 %reduce-scatter.6.cloned.1.call-start = ((), (), s32[]{:S(2)}) async-start(), calls=%async_computation.4 | async-start | bytes 9437184 | tf_op jit(solution)/shard_map/reduce_scatter | solution.py:154
  12.6 94.4 %copy-start.14 = (f32[3072]{0:T(1024)}, f32[3072]{0:T(1024)S(1)}, u32[]{:S(2)}) copy-start(f32[3072]{0:T(1024)S(1)} %broadcast_multiply_fusion.4) | copy-start | bytes 36868
  14.7 92.3 %copy-start.16 = (f32[3072]{0:T(1024)}, f32[3072]{0:T(1024)S(1)}, u32[]{:S(2)}) copy-start(f32[3072]{0:T(1024)S(1)} %add_rsqrt_fusion) | copy-start | bytes 36868
  14.8 70.1 %copy-start.19 = (f32[1024]{0:T(1024)}, f32[1024]{0:T(1024)S(1)}, u32[]{:S(2)}) copy-start(f32[1024]{0:T(1024)S(1)} %convert_element_type.138) | copy-start | bytes 12292
  14.8 70.1 %copy-start.23 = (f32[2048]{0:T(1024)}, f32[2048]{0:T(1024)S(1)}, u32[]{:S(2)}) copy-start(f32[2048]{0:T(1024)S(1)} %convert_element_type.141) | copy-start | bytes 24580
  14.8 70.0 %copy-start.28 = (f32[1024]{0:T(1024)}, f32[1024]{0:T(1024)S(1)}, u32[]{:S(2)}) copy-start(f32[1024]{0:T(1024)S(1)} %convert_element_type.139) | copy-start | bytes 12292
  14.8 70.0 %copy-start.39 = (bf16[2048,1024]{1,0:T(8,128)(2,1)S(1)}, bf16[2048,1024]{1,0:T(8,128)(2,1)}, u32[]{:S(2)}) copy-start(bf16[2048,1024]{1,0:T(8,128)(2,1)} %param.32) | copy-start | bytes 12582916
  84.9 17.4 copy-start.34
  102.2 1492.7 %reduce-scatter.4.cloned.1.call-start = ((), (), s32[]{:S(2)}) async-start(), calls=%async_computation.3 | async-start | bytes 18874368 | tf_op jit(solution)/shard_map/reduce_scatter | solution.py:152
  102.3 22.6 %copy-start.21 = (f32[1024]{0:T(1024)}, f32[1024]{0:T(1024)S(1)}, u32[]{:S(2)}) copy-start(f32[1024]{0:T(1024)S(1)} %convert_element_type.128) | copy-start | bytes 12292
  107.0 17.9 copy-start.30
  138.6 13.1 copy-start.13
  182.7 11.5 copy-start.4
  224.7 11.5 copy-start.4
  266.6 11.5 copy-start.4
  308.5 11.5 copy-start.4
  350.4 11.5 copy-start.4
  392.2 11.5 copy-start.4
  428.7 1196.6 %reduce-scatter.8.cloned.1.call-start = ((), (), s32[]{:S(2)}) async-start(), calls=%async_computation.6 | async-start | bytes 18874368 | tf_op jit(solution)/shard_map/reduce_scatter | solution.py:254
  497.2 22.2 %copy-start.2 = (bf16[3072,8,64]{0,2,1:T(8,128)(2,1)S(1)}, bf16[3072,8,64]{0,2,1:T(8,128)(2,1)}, u32[]{:S(2)}) copy-start(bf16[3072,8,64]{0,2,1:T(8,128)(2,1)} %get-tuple-element.690) | copy-start | bytes 9437188 | tf_op jit(solution)/shard_map/while
  650.0 21.7 %copy-start.2 = (bf16[3072,8,64]{0,2,1:T(8,128)(2,1)S(1)}, bf16[3072,8,64]{0,2,1:T(8,128)(2,1)}, u32[]{:S(2)}) copy-start(bf16[3072,8,64]{0,2,1:T(8,128)(2,1)} %get-tuple-element.690) | copy-start | bytes 9437188 | tf_op jit(solution)/shard_map/while
  801.9 21.7 %copy-start.2 = (bf16[3072,8,64]{0,2,1:T(8,128)(2,1)S(1)}, bf16[3072,8,64]{0,2,1:T(8,128)(2,1)}, u32[]{:S(2)}) copy-start(bf16[3072,8,64]{0,2,1:T(8,128)(2,1)} %get-tuple-element.690) | copy-start | bytes 9437188 | tf_op jit(solution)/shard_map/while
  954.0 21.7 %copy-start.2 = (bf16[3072,8,64]{0,2,1:T(8,128)(2,1)S(1)}, bf16[3072,8,64]{0,2,1:T(8,128)(2,1)}, u32[]{:S(2)}) copy-start(bf16[3072,8,64]{0,2,1:T(8,128)(2,1)} %get-tuple-element.690) | copy-start | bytes 9437188 | tf_op jit(solution)/shard_map/while
  1105.3 21.7 %copy-start.2 = (bf16[3072,8,64]{0,2,1:T(8,128)(2,1)S(1)}, bf16[3072,8,64]{0,2,1:T(8,128)(2,1)}, u32[]{:S(2)}) copy-start(bf16[3072,8,64]{0,2,1:T(8,128)(2,1)} %get-tuple-element.690) | copy-start | bytes 9437188 | tf_op jit(solution)/shard_map/while
  1256.3 21.7 %copy-start.2 = (bf16[3072,8,64]{0,2,1:T(8,128)(2,1)S(1)}, bf16[3072,8,64]{0,2,1:T(8,128)(2,1)}, u32[]{:S(2)}) copy-start(bf16[3072,8,64]{0,2,1:T(8,128)(2,1)} %get-tuple-element.690) | copy-start | bytes 9437188 | tf_op jit(solution)/shard_map/while
  1369.8 15.3 copy-start.10
  1390.9 50.6 %slice-start.2 = ((s8[6291456]{0:T(1024)(128)(4,1)}), s8[4194304]{0:T(1024)(128)(4,1)S(1)}, s32[]{:S(2)}) async-start(s8[6291456]{0:T(1024)(128)(4,1)} %bitcast.116), calls=%async_computation.10 | async-start | bytes 8388608
  1397.4 44.2 %slice-start.3 = ((s8[6291456]{0:T(1024)(128)(4,1)}), s8[2097152]{0:T(1024)(128)(4,1)S(1)}, s32[]{:S(2)}) async-start(s8[6291456]{0:T(1024)(128)(4,1)} %bitcast.116), calls=%async_computation.11 | async-start | bytes 4194304
  1424.4 17.2 copy-start.15
  1424.4 17.2 copy-start.17
  1424.4 17.2 copy-start.20
  1424.4 17.2 copy-start.22
  1475.3 600.1 %all-reduce.5.cloned.1.call-start = ((), (), s32[]{:S(2)}) async-start(), calls=%async_computation.7 | async-start | bytes 50331648 | tf_op jit(solution)/shard_map/psum | solution.py:225
  1475.3 29.1 %slice-start.4 = ((s8[6291456]{0:T(1024)(128)(4,1)}), s8[4194304]{0:T(1024)(128)(4,1)S(1)}, s32[]{:S(2)}) async-start(s8[6291456]{0:T(1024)(128)(4,1)} %bitcast.118), calls=%async_computation.12 | async-start | bytes 8388608
  1483.9 20.5 slice-start.5
  1483.9 20.5 copy-start.29
  1504.4 20.4 copy-start.31
  1543.0 9.1 copy-start.37
  1543.0 9.1 copy-start.38
  1543.0 9.1 copy-start.18
  1604.1 29.2 %copy-start.25 = (f32[2048]{0:T(1024)S(1)}, f32[2048]{0:T(1024)}, u32[]{:S(2)}) copy-start(f32[2048]{0:T(1024)} %get-tuple-element.460) | copy-start | bytes 24580
  1697.9 390.2 %copy-start.36 = (f32[512]{0:T(512)}, f32[512]{0:T(512)S(1)}, u32[]{:S(2)}) copy-start(f32[512]{0:T(512)S(1)} %get-tuple-element.736) | copy-start | bytes 6148
  2075.4 8.4 slice-start.8
  2075.9 7.9 slice-start.9
  2083.8 9.5 copy-start.1
  (21 other events, 109.4 us)
Sparse Core Ops, SparseCore 0:
  9.6 83.0 all-gather.1
  102.3 79.7 reduce-scatter.5
  428.9 147.4 reduce-scatter.3
  1475.4 149.8 reduce-scatter.7
  1631.9 443.3 all-reduce.4
where the time goes:
time: 2120 us; the launch traced here: 2100 us
  matrix products  794 us (37%)
  local copies, waits for them, and re-layouts  477 us (22%)
  waiting for transfers between devices  399 us (19%)
  other arithmetic  274 us (13%)
  blocking collectives  107 us (5%)
  loops' own time  32.6 us (2%)
    psum x1, waiting for transfers between devices, on_device(): lax.psum((qkv_weight_grad, qkv_bias_grad, dense_weight_grad, out_bias_gra...  377 us
    dot_general x12, matrix products, scores_for(): jnp.einsum('qhd,khd->hqk', rows_query, key_rows, preferred_element_type=j...  204 us
    dynamic_update_slice x12, local copies, waits for them, and re-layouts, on_device(): mixed, totals = lax.map(attend, starts)  138 us
    convert_element_type x6, other arithmetic, back_step(): score_grad = (probs * (prob_grad - inner)).astype(jnp.bfloat16)  131 us
    dynamic_update_slice x6, local copies, waits for them, and re-layouts, back_step(): key_grad = lax.dynamic_update_slice_in_dim(key_grad, key_part, first, 0)  117 us
    dynamic_update_slice x6, local copies, waits for them, and re-layouts, back_step(): lax.dynamic_update_slice_in_dim(value_grad, value_part, first, 0)  117 us
    dot_general x6, matrix products, back_step(): jnp.einsum('qhd,khd->hqk', grad_rows, value_rows, preferred_element_type=...  81 us
    dot_general x6, matrix products, back_step(): jnp.einsum('hqk,qhd->khd', probs.astype(jnp.bfloat16), grad_rows, preferr...  79.3 us
  transfers between devices with their start and end apart: 5, of which 2 were waited for; matrix products, arithmetic and copies ran while one was open for 73% of the time, Pallas kernels for 0%

commit v1 on v0

v1 whole, which is shorter than its diff:
```python
import functools

import jax
import jax.numpy as jnp
from jax import lax
from jax.experimental import pallas as pl
from jax.experimental.pallas import tpu as pltpu
from jax.sharding import PartitionSpec as P

BQ = 256
BK = 256
PAIR = 128
NEG = -1e30
ROT = 16
NORM_EPS = 1e-05
VMEM = 60 * 1024 * 1024
GF = 4
GB = 4
AHEAD = 2
BEHIND = 2
AHEADB = 2
BEHINDB = 1
F32 = jnp.float32
BF = jnp.bfloat16
NT = (((1,), (1,)), ((), ()))
NN = (((1,), (0,)), ((), ()))
TN = (((0,), (0,)), ((), ()))

def mm(a, b, dims=NN):
    return lax.dot_general(a, b, dims, preferred_element_type=F32)

def lane_half(shape):
    return lax.broadcasted_iota(jnp.int32, shape, 1) < 64

def fwd_kernel(lo_ref, start_ref, q_ref, k_ref, v_ref, o_ref, lse_ref, vt_ref):
    length = q_ref.shape[0]
    nq = length // BQ
    nk = length // BK
    groups = q_ref.shape[1] // PAIR
    for i in range(nk):
        vt_ref[i] = jnp.transpose(v_ref[i * BK:(i + 1) * BK, :])
    first = lane_half((BQ, PAIR))

    def q_block(b, _):
        rows = pl.ds(pl.multiple_of(b * BQ, BQ), BQ)
        qs = []
        for g in range(groups):
            q = q_ref[rows, PAIR * g:PAIR * g + PAIR]
            zero = jnp.zeros_like(q)
            qs += [jnp.where(first, q, zero), jnp.where(first, zero, q)]
        starts = start_ref[pl.ds(b, 1), :]
        def step(kb, carry, diagonal):
            keys = pl.ds(pl.multiple_of(kb * BK, BK), BK)
            place = lax.broadcasted_iota(jnp.int32, (BK, BQ), 0)
            allowed = place >= starts - kb * BK
            if diagonal:
                allowed = allowed & (place <= lax.broadcasted_iota(jnp.int32, (BK, BQ), 1))
            heads = range(2 * groups)
            scores, weights, out = {}, {}, []
            def score(h):
                if h in heads:
                    k = k_ref[keys, PAIR * (h // 2):PAIR * (h // 2) + PAIR]
                    scores[h] = mm(k, qs[h], NT)
            def soften(h):
                m, l, acc = carry[h]
                s = jnp.where(allowed, scores[h], NEG)
                m_new = jnp.maximum(m, jnp.max(s, axis=0, keepdims=True))
                p = jnp.exp(s - m_new)
                alpha = jnp.exp(m - m_new)
                weights[h] = (m_new, l * alpha + jnp.sum(p, axis=0, keepdims=True), alpha, p.astype(BF))
            def mix(h):
                m_new, l, alpha, p = weights[h]
                out.append((m_new, l, carry[h][2] * alpha + mm(vt_ref[kb, 64 * h:64 * h + 64, :], p)))
            for h in range(AHEAD):
                score(h)
            for h in heads:
                score(h + AHEAD)
                soften(h)
                if h >= BEHIND:
                    mix(h - BEHIND)
            for h in heads[len(heads) - BEHIND:] if BEHIND else ():
                mix(h)
            return tuple(out)
        init = tuple((jnp.full((1, BQ), NEG, F32), jnp.zeros((1, BQ), F32), jnp.zeros((64, BQ), F32)) for _ in range(2 * groups))
        carry = step(b, init, True)
        carry = lax.fori_loop(lo_ref[b], b, lambda kb, c: step(kb, c, False), carry)
        for h in range(2 * groups):
            lse_ref[h, pl.ds(b, 1), :] = carry[h][0] + jnp.log(carry[h][1])
        ot = jnp.concatenate([c[2] / c[1] for c in carry], axis=0)
        o_ref[rows, :] = jnp.transpose(ot).astype(BF)
        return 0
    lax.fori_loop(0, nq, q_block, 0)

def attn_fwd(lo, starts, q, k, v):
    length, width = q.shape
    nq = length // BQ
    group = min(GF * PAIR, width)
    pairs = width // group
    col = pl.BlockSpec((length, group), lambda p, *_: (0, p))
    return pl.pallas_call(
        fwd_kernel,
        grid_spec=pltpu.PrefetchScalarGridSpec(
            num_scalar_prefetch=1, grid=(pairs,),
            in_specs=[pl.BlockSpec((nq, BQ), lambda p, *_: (0, 0)), col, col, col],
            out_specs=[col, pl.BlockSpec((group // 64, nq, BQ), lambda p, *_: (p, 0, 0))],
            scratch_shapes=[pltpu.VMEM((length // BK, group, BK), BF)],
        ),
        out_shape=[jax.ShapeDtypeStruct((length, width), BF), jax.ShapeDtypeStruct((width // 64, nq, BQ), F32)],
        compiler_params=pltpu.CompilerParams(vmem_limit_bytes=VMEM),
        name="attention_forward",
    )(lo, starts, q, k, v)

def bwd_kernel(lo_ref, start_ref, q_ref, k_ref, v_ref, o_ref, do_ref, lse_ref, cos_ref, sa_ref, sb_ref, dq_ref, dk_ref, dv_ref, kt_ref, dk_acc, dv_acc):
    length = q_ref.shape[0]
    nq = length // BQ
    nk = length // BK
    groups = q_ref.shape[1] // PAIR
    for i in range(nk):
        kt_ref[i] = jnp.transpose(k_ref[i * BK:(i + 1) * BK, :])
    first = lane_half((BQ, PAIR))
    dk_acc[...] = jnp.zeros_like(dk_acc)
    dv_acc[...] = jnp.zeros_like(dv_acc)

    def unrotate(w, rows):
        return w * cos_ref[rows, :] - pltpu.roll(w, PAIR - 8, 1) * sa_ref[rows, :] - pltpu.roll(w, 8, 1) * sb_ref[rows, :]

    cols = [slice(PAIR * g, PAIR * g + PAIR) for g in range(groups)]

    def q_block(step_index, _):
        b = nq - 1 - step_index
        rows = pl.ds(pl.multiple_of(b * BQ, BQ), BQ)
        starts = start_ref[pl.ds(b, 1), :]
        qs, dos, deltas, lses = [], [], [], []
        for g in range(groups):
            q = q_ref[rows, cols[g]]
            do = do_ref[rows, cols[g]]
            zero = jnp.zeros_like(q)
            qs += [jnp.where(first, q, zero), jnp.where(first, zero, q)]
            dos += [jnp.where(first, do, zero), jnp.where(first, zero, do)]
            prod = jnp.transpose(do.astype(F32) * o_ref[rows, cols[g]].astype(F32))
            deltas += [jnp.sum(prod[:64], axis=0, keepdims=True), jnp.sum(prod[64:], axis=0, keepdims=True)]
            lses += [lse_ref[2 * g, pl.ds(b, 1), :], lse_ref[2 * g + 1, pl.ds(b, 1), :]]
        def step(kb, carry, diagonal):
            keys = pl.ds(pl.multiple_of(kb * BK, BK), BK)
            place = lax.broadcasted_iota(jnp.int32, (BK, BQ), 0)
            allowed = place >= starts - kb * BK
            if diagonal:
                allowed = allowed & (place <= lax.broadcasted_iota(jnp.int32, (BK, BQ), 1))
            out = []
            heads = range(2 * groups)
            raw, soft = {}, {}
            def score(h):
                if h in heads:
                    raw[h] = (mm(k_ref[keys, cols[h // 2]], qs[h], NT), mm(v_ref[keys, cols[h // 2]], dos[h], NT))
            def soften(h):
                s, dp = raw[h]
                p = jnp.exp(jnp.where(allowed, s - lses[h], NEG))
                soft[h] = (p.astype(BF), (p * (dp - deltas[h])).astype(BF))
            def mix(h):
                out.append(carry[h] + mm(kt_ref[kb, 64 * h:64 * h + 64, :], soft[h][1]))
                if h % 2 == 1:
                    g = h // 2
                    dv_acc[keys, cols[g]] += mm(jnp.concatenate([soft[h - 1][0], soft[h][0]], axis=1), jnp.concatenate(dos[2 * g:2 * g + 2], axis=0))
                    dk_acc[keys, cols[g]] += mm(jnp.concatenate([soft[h - 1][1], soft[h][1]], axis=1), jnp.concatenate(qs[2 * g:2 * g + 2], axis=0))
            for h in range(AHEADB):
                score(h)
            for h in heads:
                score(h + AHEADB)
                soften(h)
                if h >= BEHINDB:
                    mix(h - BEHINDB)
            for h in heads[len(heads) - BEHINDB:] if BEHINDB else ():
                mix(h)
            return tuple(out)
        carry = tuple(jnp.zeros((64, BQ), F32) for _ in range(2 * groups))
        carry = lax.fori_loop(lo_ref[b], b, lambda kb, c: step(kb, c, False), carry)
        carry = step(b, carry, True)
        for g in range(groups):
            dq = jnp.transpose(jnp.concatenate(carry[2 * g:2 * g + 2], axis=0)) * 0.125
            dq_ref[rows, cols[g]] = unrotate(dq, rows).astype(BF)
            dk_ref[rows, cols[g]] = unrotate(dk_acc[rows, cols[g]], rows).astype(BF)
            dv_ref[rows, cols[g]] = dv_acc[rows, cols[g]].astype(BF)
        return 0
    lax.fori_loop(0, nq, q_block, 0)

def attn_bwd(lo, starts, q, k, v, o, do, lse, cos, sa, sb):
    length, width = q.shape
    nq = length // BQ
    group = min(GB * PAIR, width)
    pairs = width // group
    col = pl.BlockSpec((length, group), lambda p, *_: (0, p))
    whole = pl.BlockSpec((length, PAIR), lambda p, *_: (0, 0))
    return pl.pallas_call(
        bwd_kernel,
        grid_spec=pltpu.PrefetchScalarGridSpec(
            num_scalar_prefetch=1, grid=(pairs,),
            in_specs=[pl.BlockSpec((nq, BQ), lambda p, *_: (0, 0)), col, col, col, col, col,
                      pl.BlockSpec((group // 64, nq, BQ), lambda p, *_: (p, 0, 0)), whole, whole, whole],
            out_specs=[col, col, col],
            scratch_shapes=[pltpu.VMEM((length // BK, group, BK), BF), pltpu.VMEM((length, group), F32), pltpu.VMEM((length, group), F32)],
        ),
        out_shape=[jax.ShapeDtypeStruct((length, width), BF)] * 3,
        compiler_params=pltpu.CompilerParams(vmem_limit_bytes=VMEM),
        name="attention_backward",
    )(lo, starts, q, k, v, o, do, lse, cos, sa, sb)

T = 512
TT = 512


def norm_rows(x, eps=NORM_EPS):
    centred = x - jnp.mean(x, axis=-1, keepdims=True)
    root_inv = lax.rsqrt(jnp.mean(centred * centred, axis=-1, keepdims=True) + eps)
    return centred * root_inv, root_inv


def fold_rows(v):
    return jnp.sum(v.reshape(v.shape[0] // 8, 8, v.shape[1]), axis=0)


def project_kernel(x_ref, gain_ref, shift_ref, w_ref, b_ref, cos_ref, sa_ref, sb_ref, q_ref, k_ref, v_ref):
    local = q_ref.shape[1]
    xhat, _ = norm_rows(x_ref[...].astype(F32))
    normed = (xhat * gain_ref[...] + shift_ref[...]).astype(BF)
    for which, out in enumerate((q_ref, k_ref, v_ref)):
        span = slice(which * local, which * local + local)
        y = mm(normed, w_ref[:, span]) + b_ref[:, span]
        if which == 2:
            out[...] = y.astype(BF)
            continue
        for c in range(local // PAIR):
            cols = slice(c * PAIR, c * PAIR + PAIR)
            u = y[:, cols]
            u = u * cos_ref[...] + pltpu.roll(u, PAIR - 8, 1) * sa_ref[...] + pltpu.roll(u, 8, 1) * sb_ref[...]
            out[:, cols] = (u * 0.125 if which == 0 else u).astype(BF)


def fixed(shape):
    return pl.BlockSpec(shape, lambda i, *_: (0,) * len(shape), pipeline_mode=pl.Buffered(1))


def tokens(rows, cols):
    return pl.BlockSpec((rows, cols), lambda i, *_: (i, 0))


def project(x, gain, shift, w, b, cos, sa, sb):
    length, width = x.shape
    local = w.shape[1] // 3
    return pl.pallas_call(
        project_kernel,
        grid=(length // T,),
        in_specs=[tokens(T, width), fixed((1, width)), fixed((1, width)), fixed(w.shape), fixed(b.shape)] + [tokens(T, PAIR)] * 3,
        out_specs=[tokens(T, local)] * 3,
        out_shape=[jax.ShapeDtypeStruct((length, local), BF)] * 3,
        compiler_params=pltpu.CompilerParams(vmem_limit_bytes=VMEM),
        cost_estimate=pl.CostEstimate(flops=2 * length * width * 3 * local, bytes_accessed=length * width * 4, transcendentals=0),
        name="project_qkv",
    )(x, gain, shift, w, b, cos, sa, sb)


def scatter_pieces(total, me, outs):
    ranks, local = len(outs), outs[0].shape[1]
    for d in range(ranks):
        target = lax.rem(me + d, ranks)
        cols = pl.ds(pl.multiple_of(target * local, 128), local)
        outs[d][...] = total[:, cols].astype(outs[d].dtype)


def feedforward_kernel(ranks, me_ref, x_ref, gain_ref, shift_ref, w1_ref, b1_ref, w2_ref, wd_ref, mixed_ref, *refs):
    pieces, refs = refs[:ranks], refs[ranks:]
    outs, refs = refs[:ranks], refs[ranks:]
    mixed_grad_ref, n2g_ref, w1g_ref, w2g_ref, wdg_ref, b1g_ref, lng_ref, lnb_ref, g_ref, n2t_ref, total_ref, back_ref = refs
    step = pl.program_id(0)
    me = me_ref[0]
    local = pieces[0].shape[1]
    hidden_units = w1_ref.shape[1]
    chunk = min(512, hidden_units)
    chunks = hidden_units // chunk

    @pl.when(step == 0)
    def _():
        for ref in (w1g_ref, w2g_ref, wdg_ref, b1g_ref, lng_ref, lnb_ref):
            ref[...] = jnp.zeros_like(ref)

    for d in range(ranks):
        source = lax.rem(me + d, ranks)
        g_ref[:, pl.ds(pl.multiple_of(source * local, 128), local)] = pieces[d][...]
    xhat, _ = norm_rows(x_ref[...].astype(F32))
    normed = (xhat * gain_ref[...] + shift_ref[...]).astype(BF)
    n2t_ref[...] = jnp.transpose(normed)
    g = g_ref[...]
    raw, soft = {}, {}

    def expand(c):
        if c < chunks:
            cols = slice(c * chunk, c * chunk + chunk)
            raw[c] = (mm(normed, w1_ref[:, cols]) + b1_ref[:, cols], mm(g, w2_ref[cols, :], NT))

    def bend(c):
        cols = slice(c * chunk, c * chunk + chunk)
        hidden, active_grad = raw[c]
        cumulative = 0.5 * (1.0 + lax.erf(hidden * 0.7071067811865476))
        density = jnp.exp(-0.5 * hidden * hidden) * 0.3989422804014327
        active = (hidden * cumulative).astype(BF)
        hidden_grad = (active_grad * (cumulative + hidden * density)).astype(BF)
        b1g_ref[:, cols] += fold_rows(hidden_grad.astype(F32))
        soft[c] = (active, hidden_grad)

    def contract(c):
        cols = slice(c * chunk, c * chunk + chunk)
        active, hidden_grad = soft[c]
        feed = mm(active, w2_ref[cols, :])
        back = mm(hidden_grad, w1_ref[:, cols], NT)
        if c == 0:
            total_ref[...] = feed
            back_ref[...] = back
        else:
            total_ref[...] += feed
            back_ref[...] += back
        w2g_ref[cols, :] += mm(active, g, TN)
        w1g_ref[:, cols] += mm(n2t_ref[...], hidden_grad)

    expand(0)
    for c in range(chunks):
        expand(c + 1)
        bend(c)
        if c >= 1:
            contract(c - 1)
    mixed = mixed_ref[...]
    mixed_grad_ref[...] = mm(g, wd_ref[...], NT).astype(BF)
    contract(chunks - 1)
    total_ref[...] += mm(mixed, wd_ref[...])
    wdg_ref[...] += mm(mixed, g, TN)
    back = back_ref[...]
    n2g_ref[...] = back.astype(BF)
    lnb_ref[...] += fold_rows(back)
    lng_ref[...] += fold_rows(back * xhat)
    scatter_pieces(total_ref, me, outs)


def feedforward(me, x, gain, shift, w1, b1, w2, wd, mixed, pieces):
    length, width = x.shape
    local, hidden_units, ranks = mixed.shape[1], w1.shape[1], len(pieces)
    shapes = [((length, local), F32)] + [((length, local), BF)] * (ranks - 1) + [((length, local), BF), ((length, width), BF)]
    sums = [(width, hidden_units), (hidden_units, width), (local, width), (8, hidden_units), (8, width), (8, width)]
    return pl.pallas_call(
        functools.partial(feedforward_kernel, ranks),
        grid_spec=pltpu.PrefetchScalarGridSpec(
            num_scalar_prefetch=1,
            grid=(length // TT,),
            in_specs=[tokens(TT, width), fixed((1, width)), fixed((1, width)), fixed(w1.shape), fixed(b1.shape), fixed(w2.shape), fixed(wd.shape), tokens(TT, local)]
            + [tokens(TT, local)] * ranks,
            out_specs=[tokens(TT, s[1]) for s, _ in shapes] + [fixed(s) for s in sums],
            scratch_shapes=[pltpu.VMEM((TT, width), BF), pltpu.VMEM((width, TT), BF), pltpu.VMEM((TT, width), F32), pltpu.VMEM((TT, width), F32)],
        ),
        out_shape=[jax.ShapeDtypeStruct(s, d) for s, d in shapes] + [jax.ShapeDtypeStruct(s, F32) for s in sums],
        compiler_params=pltpu.CompilerParams(vmem_limit_bytes=VMEM),
        cost_estimate=pl.CostEstimate(flops=2 * length * width * (6 * hidden_units + 3 * local), bytes_accessed=length * width * 12, transcendentals=length * hidden_units),
        name="feedforward_both_ways",
    )(me, x, gain, shift, w1, b1, w2, wd, mixed, *pieces)


def input_kernel(ranks, me_ref, x_ref, gain1_ref, shift1_ref, gain2_ref, w_ref, dq_ref, dk_ref, dv_ref, n2g_ref, *refs):
    outs, refs = refs[:ranks], refs[ranks:]
    wg_ref, bg_ref, lng_ref, lnb_ref, n1t_ref, total_ref = refs
    local = dq_ref.shape[1]

    @pl.when(pl.program_id(0) == 0)
    def _():
        for ref in (wg_ref, bg_ref, lng_ref, lnb_ref):
            ref[...] = jnp.zeros_like(ref)

    xhat, root_inv = norm_rows(x_ref[...].astype(F32))
    n1t_ref[...] = jnp.transpose((xhat * gain1_ref[...] + shift1_ref[...]).astype(BF))
    grads = (dq_ref[...], dk_ref[...], dv_ref[...])
    spans = [slice(w * local, w * local + local) for w in range(3)]
    back = mm(grads[0], w_ref[:, spans[0]], NT) + mm(grads[1], w_ref[:, spans[1]], NT) + mm(grads[2], w_ref[:, spans[2]], NT)
    for grad, span in zip(grads, spans):
        wg_ref[:, span] += mm(n1t_ref[...], grad)
        bg_ref[:, span] += fold_rows(grad.astype(F32))
    lnb_ref[...] += fold_rows(back)
    lng_ref[...] += fold_rows(back * xhat)
    e = back * gain1_ref[...] + n2g_ref[...].astype(F32) * gain2_ref[...]
    total_ref[...] = root_inv * (e - jnp.mean(e, axis=-1, keepdims=True) - xhat * jnp.mean(e * xhat, axis=-1, keepdims=True))
    scatter_pieces(total_ref, me_ref[0], outs)


def input_backward(me, ranks, x, gain1, shift1, gain2, w, dq, dk, dv, n2g):
    length, width = x.shape
    local = dq.shape[1]
    shapes = [((length, local), F32)] + [((length, local), BF)] * (ranks - 1)
    sums = [w.shape, (8, w.shape[1]), (8, width), (8, width)]
    return pl.pallas_call(
        functools.partial(input_kernel, ranks),
        grid_spec=pltpu.PrefetchScalarGridSpec(
            num_scalar_prefetch=1,
            grid=(length // T,),
            in_specs=[tokens(T, width), fixed((1, width)), fixed((1, width)), fixed((1, width)), fixed(w.shape)] + [tokens(T, local)] * 3 + [tokens(T, width)],
            out_specs=[tokens(T, s[1]) for s, _ in shapes] + [fixed(s) for s in sums],
            scratch_shapes=[pltpu.VMEM((width, T), BF), pltpu.VMEM((T, width), F32)],
        ),
        out_shape=[jax.ShapeDtypeStruct(s, d) for s, d in shapes] + [jax.ShapeDtypeStruct(s, F32) for s in sums],
        compiler_params=pltpu.CompilerParams(vmem_limit_bytes=VMEM),
        cost_estimate=pl.CostEstimate(flops=2 * length * width * 6 * local, bytes_accessed=length * width * 12, transcendentals=0),
        name="input_backward",
    )(me, x, gain1, shift1, gain2, w, dq, dk, dv, n2g)


def sum_weights(grads, packs):
    return [v.astype(F32) for v in lax.psum(tuple(v.astype(BF) for v in grads), "dp")]


def rotary_tables(segments):
    length = segments.shape[0]
    places = jnp.arange(length, dtype=jnp.int32)
    first = jnp.concatenate([jnp.ones((1,), dtype=bool), segments[1:] != segments[:-1]])
    starts = lax.cummax(jnp.where(first, places, jnp.zeros_like(places)), axis=0)
    offsets = (places - starts).astype(F32)
    lane = jnp.arange(PAIR, dtype=jnp.int32) % 64
    inverse = 10000.0 ** (-(2 * (lane % (ROT // 2))).astype(F32) / ROT)
    angles = offsets[:, None] * inverse[None, :]
    cosine, sine = jnp.cos(angles), jnp.sin(angles)
    turned = lane < ROT
    low = lane < ROT // 2
    return (
        starts,
        jnp.where(turned, cosine, 1.0),
        jnp.where(low, -sine, 0.0),
        jnp.where(turned & ~low, sine, 0.0),
    )


def shifted(ranks, distance):
    return [(i, (i + distance) % ranks) for i in range(ranks)]


def send_pieces(pieces):
    ranks = len(pieces)
    total = pieces[0]
    for d in range(1, ranks):
        total = total + lax.ppermute(pieces[d], "tensor", shifted(ranks, d)).astype(F32)
    return total


def swap_sum(value, axis, ranks):
    step = 1
    while step < ranks:
        value = value + lax.ppermute(value, axis, [(i, i ^ step) for i in range(ranks)])
        step *= 2
    return value


def on_device(sizes, inputs, segment_ids, cotangent, ln1_gain, attention_norm_bias, ln2_gain, feedforward_norm_bias, w_qkv, b_qkv, w_dense, b_dense, w_fc1, b_fc1, w_fc2, b_fc2):
    packs, ranks = sizes
    segments = segment_ids[0]
    width = inputs.shape[1]
    local = w_qkv.shape[2]
    hidden_units = w_fc1.shape[1]
    me = lax.axis_index("tensor").astype(jnp.int32).reshape(1)
    pieces = [cotangent] + [lax.ppermute(cotangent, "tensor", shifted(ranks, ranks - d)) for d in range(1, ranks)]
    starts, cosine, sine_a, sine_b = rotary_tables(segments)
    starts = starts.reshape(-1, BQ)
    lowest = starts[:, 0] // BK
    row = lambda v: v.astype(F32).reshape(1, -1)
    qkv_matrix = w_qkv.reshape(width, 3 * local)
    gain1, gain2 = row(ln1_gain), row(ln2_gain)
    shift1, shift2 = row(attention_norm_bias), row(feedforward_norm_bias)
    query, key, value = project(inputs, gain1, shift1, qkv_matrix, row(b_qkv), cosine, sine_a, sine_b)
    mixed, totals = attn_fwd(lowest, starts, query, key, value)
    made = feedforward(me, inputs, gain2, shift2, w_fc1, row(b_fc1), w_fc2, w_dense, mixed, pieces)
    outs, (mixed_grad, normed2_grad, w1g, w2g, wdg, b1g, ln2g, ln2b) = made[:ranks], made[ranks:]
    own = lax.dynamic_slice_in_dim(inputs, me[0] * local, local, 1).astype(F32)
    outputs = (send_pieces(outs) + own + b_dense.astype(F32) + b_fc2.astype(F32)).astype(BF)
    big = sum_weights((w1g, w2g, wdg), packs)
    dq, dk, dv = attn_bwd(lowest, starts, query, key, value, mixed, mixed_grad, totals, cosine, sine_a, sine_b)
    made = input_backward(me, ranks, inputs, gain1, shift1, gain2, qkv_matrix, dq, dk, dv, normed2_grad)
    partials, (wg, bg, ln1g, ln1b) = made[:ranks], made[ranks:]
    input_grad = send_pieces(partials) + cotangent.astype(F32)
    (wg,) = sum_weights((wg,), packs)
    out_bias = jnp.sum(cotangent.astype(F32), axis=0)
    norms = jnp.stack([jnp.sum(v, axis=0) for v in (ln1g, ln1b, ln2g, ln2b)]).reshape(-1)
    norms = swap_sum(norms, "tensor", ranks)
    biases = (jnp.sum(bg, axis=0), out_bias, jnp.sum(b1g, axis=0))
    small = jnp.concatenate((norms,) + biases).reshape(-1, 128)
    small = swap_sum(small, "dp", packs).reshape(-1)
    norms = small[: 4 * width].reshape(4, width)
    small = small[4 * width :]
    qkv_bias_grad = small[: 3 * local].reshape(3, local)
    dense_bias_grad = small[3 * local : 4 * local]
    fc1_bias_grad = small[4 * local :]
    return (
        outputs,
        input_grad,
        norms[0],
        norms[1],
        norms[2],
        norms[3],
        wg.reshape(width, 3, local),
        qkv_bias_grad,
        big[2],
        dense_bias_grad,
        big[0],
        fc1_bias_grad,
        big[1],
        dense_bias_grad,
    )


def solution(mesh):
    placed = (
        P("dp", None),
        P("dp", None),
        P("dp", "tensor"),
        P(),
        P(),
        P(),
        P(),
        P(None, None, "tensor"),
        P(None, "tensor"),
        P("tensor", None),
        P("tensor"),
        P(None, "tensor"),
        P("tensor"),
        P("tensor", None),
        P("tensor"),
    )
    sizes = (mesh.shape["dp"], mesh.shape["tensor"])
    return jax.shard_map(
        functools.partial(on_device, sizes),
        mesh=mesh,
        in_specs=placed,
        out_specs=(
            P("dp", "tensor"),
            P("dp", "tensor"),
            P(),
            P(),
            P(),
            P(),
            P(None, None, "tensor"),
            P(None, "tensor"),
            P("tensor", None),
            P("tensor"),
            P(None, "tensor"),
            P("tensor"),
            P("tensor", None),
            P("tensor"),
        ),
        check_vma=False,
    )
```

time: 2120 us -> 594 us (0.28)
  matrix products: 794 us -> 0 us
  local copies, waits for them, and re-layouts: 477 us -> 18.3 us
  Pallas kernels: 0 us -> 269 us
  other arithmetic: 274 us -> 60.7 us
  waiting for transfers between devices: 399 us -> 216 us
  blocking collectives: 107 us -> 0 us
  loops' own time: 32.6 us -> 0 us
    dot_general x54 -> x0, matrix products: 794 us -> none  [the longest x12 204 us: scores_for(): jnp.einsum('qhd,khd->hqk', rows_query, key_rows, preferred_element_type=j...]
    dynamic_update_slice x24 -> x0, local copies, waits for them, and re-layouts: 371 us -> none  [the longest x12 138 us: on_device(): mixed, totals = lax.map(attend, starts)]
    psum x1, waiting for transfers between devices: 377 us -> 72.3 us  [sum_weights(): lax.psum(tuple((v.astype(BF) for v in grads)), 'dp')]
    pallas_call x0 -> x5, Pallas kernels: none -> 269 us  [the longest x1 111 us: feedforward(): pl.pallas_call(functools.partial(feedforward_kernel, ranks), grid_spec=pl...]
    ppermute x0 -> x8, waiting for transfers between devices: none -> 144 us  [the longest x5 144 us: swap_sum(): lax.ppermute(value, axis, [(i, i ^ step) for i in range(ranks)])]
    convert_element_type x16 -> x11, other arithmetic: 149 us -> 35.8 us  [the longest x4 14.9 us: sum_weights(): v.astype(BF)]
    psum x2 -> x0, blocking collectives: 107 us -> none  [the longest x1 64.6 us: on_device(): lax.psum((qkv_weight_grad, qkv_bias_grad, dense_weight_grad, out_bias_gra...]
    reduce_sum x10 -> x7, other arithmetic: 88.4 us -> 8.12 us  [the longest x1 8.02 us: on_device(): out_bias = jnp.sum(cotangent.astype(F32), axis=0)]
  transfers between devices with their start and end apart: 5 -> 9, of which waited for: 2 -> 5; matrix products, arithmetic and copies ran while one was open for 73% -> 7% of each run, Pallas kernels for 0% -> 10%
where the time goes in v1:
time: 594 us; the launch traced here: 590 us
  Pallas kernels  269 us (45%)
  waiting for transfers between devices  216 us (36%)
  other arithmetic  60.7 us (10%)
  local copies, waits for them, and re-layouts  18.3 us (3%)
  between operations  14.8 us (2%)
  starting transfers between devices  12 us (2%)
    ppermute x5, waiting for transfers between devices, swap_sum(): lax.ppermute(value, axis, [(i, i ^ step) for i in range(ranks)])  144 us
    pallas_call x1, Pallas kernels, feedforward(): pl.pallas_call(functools.partial(feedforward_kernel, ranks), grid_spec=pl...  111 us
    psum x1, waiting for transfers between devices, sum_weights(): lax.psum(tuple((v.astype(BF) for v in grads)), 'dp')  72.3 us
    pallas_call x1, Pallas kernels, attn_bwd(): pl.pallas_call(bwd_kernel, grid_spec=pltpu.PrefetchScalarGridSpec(num_sca...  64 us
    pallas_call x1, Pallas kernels, attn_fwd(): pl.pallas_call(fwd_kernel, grid_spec=pltpu.PrefetchScalarGridSpec(num_sca...  43 us
    pallas_call x1, Pallas kernels, input_backward(): pl.pallas_call(functools.partial(input_kernel, ranks), grid_spec=pltpu.Pr...  33.8 us
    pallas_call x1, Pallas kernels, project(): pl.pallas_call(project_kernel, grid=(length // T,), in_specs=[tokens(T, w...  17.3 us
    convert_element_type x4, other arithmetic, sum_weights(): v.astype(BF)  14.9 us
  transfers between devices with their start and end apart: 9, of which 5 were waited for; matrix products, arithmetic and copies ran while one was open for 7% of the time, Pallas kernels for 10%

profile of v1, /device:TPU:0, one launch (start us, length us, event | category | flops | bytes accessed | tf_op | source)
XLA Modules:
  0.0 590.3 jit_solution(3664318580240512262)
XLA Ops:
  7.2 3.0 collective-permute-start
  10.2 0.9 compare_reduce_fusion
  11.2 0.3 reduce-window.9
  11.6 1.3 reshape.190
  12.9 1.3 reshape.192
  14.1 1.3 reshape.194
  15.5 0.1 slice_reduce_fusion
  15.6 0.1 reshape.175
  15.7 0.1 broadcast.82
  15.8 1.3 reshape.196
  17.0 1.3 reshape.198
  18.3 3.2 copy.31
  21.5 2.9 copy.32.w_ref
  24.5 0.6 copy.37
  25.1 0.1 slice_reduce_fusion.1
  25.2 0.5 and_select_fusion.2.lo_ref
  25.8 8.4 %fusion = (f32[3072,128]{1,0:T(8,128)}, f32[3072,128]{1,0:T(8,128)}, f32[3072,128]{1,0:T(8,128)}) fusion(f32[128]{0:T(128)S(1)} %fusion.9, f32[3072]{0:T(1024)S(1)} %fusion.4, pred[128]{0:T(512)(128)(4,1)S(1)} %get-tuple-element.89, pred[128]{0:T(512)(128)(4,1)S(1)} %get-tuple-element.90, pred[128]{0:T(512)(128)(4,1)S(1)} %broadcast_compare_fusion.1), kind=kLoop, calls=%fused_computation.5 | loop fusion | flops 1966080 | bytes 4731776 | tf_op jit(solution)/shard_map/jit(_where)/select_n | solution.py:429
  34.2 17.3 %project_qkv.1 = (bf16[3072,512]{1,0:T(8,128)(2,1)}, bf16[3072,512]{1,0:T(8,128)(2,1)}, bf16[3072,512]{1,0:T(8,128)(2,1)}) custom-call(bf16[3072,1024]{1,0:T(8,128)(2,1)} %x_ref.5, f32[1,1024]{1,0:T(1,128)} %bitcast.67, f32[1,1024]{1,0:T(1,128)} %bitcast.69, bf16[1024,1536]{1,0:T(8,128)(2,1)} %copy.32.w_ref, f32[1,1536]{1,0:T(1,128)} %bitcast.64, ...), custom_call_target="tpu_custom_call" | custom-call | flops 9663676416 | bytes 12582912 | tf_op jit(solution)/shard_map/project_qkv/pallas_call | solution.py:249
  51.6 43.0 %attention_forward.1 = (bf16[3072,512]{1,0:T(8,128)(2,1)}, f32[8,12,256]{2,1,0:T(8,128)}) custom-call(s32[12]{0:T(128)} %and_select_fusion.2.lo_ref, s32[12,256]{1,0:T(8,128)} %copy-done.3, bf16[3072,512]{1,0:T(8,128)(2,1)} %get-tuple-element.38.q_ref, bf16[3072,512]{1,0:T(8,128)(2,1)} %get-tuple-element.39.k_ref, bf16[3072,512]{1,0:T(8,128)(2,1)} %get-tuple-element.40.v_ref), custom_call_target="tpu_custom_call" | custom-call | tf_op jit(solution)/shard_map/attention_forward/pallas_call | solution.py:100
  94.5 110.7 %feedforward_both_ways.1 = (f32[3072,512]{1,0:T(8,128)}, bf16[3072,512]{1,0:T(8,128)(2,1)}, bf16[3072,512]{1,0:T(8,128)(2,1)}, bf16[3072,1024]{1,0:T(8,128)(2,1)...) custom-call(s32[1]{0:T(128)} %bitcast.me_ref, ...), custom_call_target="tpu_custom_call" | custom-call | flops 86973087744 | bytes 37748736 | tf_op jit(solution)/shard_map/feedforward_both_ways/pallas_call | solution.py:346
  205.2 64.0 %attention_backward.1 = (bf16[3072,512]{1,0:T(8,128)(2,1)}, bf16[3072,512]{1,0:T(8,128)(2,1)}, bf16[3072,512]{1,0:T(8,128)(2,1)}) custom-call(s32[12]{0:T(128)} %and_select_fusion.2.lo_ref, s32[12,256]{1,0:T(8,128)} %copy-done.3, bf16[3072,512]{1,0:T(8,128)(2,1)} %get-tuple-element.38.q_ref, bf16[3072,512]{1,0:T(8,128)(2,1)} %get-tuple-element.39.k_ref, ...), custom_call_target="tpu_custom_call" | custom-call | tf_op jit(solution)/shard_map/attention_backward/pallas_call | solution.py:193
  269.3 33.8 %input_backward.1 = (f32[3072,512]{1,0:T(8,128)}, bf16[3072,512]{1,0:T(8,128)(2,1)}, f32[1024,1536]{1,0:T(8,128)}, f32[8,1536]{1,0:T(8,128)}, f32[8,1024]{1,0:T(8,128)}, /*index=5*/f32[8,1024]{1,0:T(8,128)}) custom-call(s32[1]{0:T(128)} %bitcast.me_ref, bf16[3072,1024]{1,0:T(8,128)(2,1)} %x_ref.5, f32[1,1024]{1,0:T(1,128)} %bitcast.68, f32[1,1024]{1,0:T(1,128)} %bitcast.70, ...), custom_call_target="tpu_custom_call" | custom-call | flops 19327352832 | bytes 37748736 | tf_op jit(solution)/shard_map/input_backward/pallas_call | solution.py:393
  303.0 3.2 convert_element_type.73
  306.2 3.1 copy.34
  309.3 2.9 convert_element_type.74
  312.2 6.2 %convert_element_type.76 = bf16[1024,2048]{1,0:T(8,128)(2,1)} convert(f32[1024,2048]{1,0:T(8,128)} %get-tuple-element.60) | non-fusion elementwise | flops 2097152 | bytes 12582912 | tf_op jit(solution)/shard_map/convert_element_type | solution.py:410
  318.4 2.7 convert_element_type.78
  321.1 0.4 collective-permute-start.2
  321.5 1.7 collective-permute-start.1
  323.4 0.4 collective-permute-start.3
  323.8 135.3 %collective-permute-done.3 = f32[4096]{0:T(1024)S(1)} collective-permute-done((f32[4096]{0:T(1024)S(1)}, f32[4096]{0:T(1024)S(1)}, u32[]{:S(2)}, u32[]{:S(2)}) %collective-permute-start.3) | collective-permute-done | bytes 16416 | tf_op jit(solution)/shard_map/ppermute | solution.py:448
  459.1 8.0 %convert_reduce_fusion = (f32[512]{0:T(512)S(1)}, f32[3072,512]{1,0:T(8,128)}) fusion(bf16[3072,512]{1,0:T(8,128)(2,1)S(1)} %copy-done.1, f32[3072,512]{1,0:T(8,128)} %get-tuple-element.50, bf16[3072,512]{1,0:T(8,128)(2,1)} %collective-permute-done.2), kind=kLoop, calls=%fused_computation | loop fusion | flops 7863808 | bytes 18876416 | tf_op jit(solution)/shard_map/reduce_sum | solution.py:480
  467.2 1.4 collective-permute-start.4
  468.5 0.9 collective-permute-done.4
  469.4 3.9 collective-permute-done.5
  473.3 0.4 collective-permute-start.6
  473.7 3.6 collective-permute-done.6
  477.3 4.7 collective-permute-start.7
  482.0 8.0 %add_convert_fusion = bf16[3072,512]{1,0:T(8,128)(2,1)} fusion(f32[3072,512]{1,0:T(8,128)} %get-tuple-element.42, bf16[3072,512]{1,0:T(8,128)(2,1)} %collective-permute-done.1, f32[512]{0:T(512)S(1)} %convert_element_type.69, f32[512]{0:T(512)S(1)} %convert_element_type.68, bf16[3072,1024]{1,0:T(8,128)(2,1)} %x_ref.5, s32[]{:T(128)S(6)} %select_n.55), kind=kLoop, calls=%fused_computation.2 | loop fusion | flops 11010048 | bytes 15732740 | tf_op jit(solution)/shard_map/convert_element_type | solution.py:473
  490.1 0.6 reshape.189
  490.7 0.6 slice_bitcast_fusion
  491.3 0.6 slice_bitcast_fusion.1
  491.9 72.3 %all-reduce.3.cloned.1.call-done = (bf16[1024,3,512]{0,2,1:T(8,128)(2,1)}, bf16[512,1024]{1,0:T(8,128)(2,1)}, bf16[1024,2048]{1,0:T(8,128)(2,1)}, bf16[2048,1024]{1,0:T(8,128)(2,1)}) async-done(((bf16[1024,3,512]{0,2,1:T(8,128)(2,1)}, bf16[512,1024]{1,0:T(8,128)(2,1)}, bf16[1024,2048]{1,0:T(8,128)(2,1)}, bf16[2048,1024]{1,0:T(8,128)(2,1)}), (bf16[1024,3,512]{0,2,1:T(8,128)(2,1)}, ...) | async-done | bytes 12582928 | tf_op jit(solution)/shard_map/psum | solution.py:410
  564.1 5.5 copy.35
  569.6 1.6 convert_element_type.75
  571.2 6.8 %convert_element_type.77 = f32[1024,2048]{1,0:T(8,128)} convert(bf16[1024,2048]{1,0:T(8,128)(2,1)} %get-tuple-element.78) | non-fusion elementwise | flops 2097152 | bytes 12582912 | tf_op jit(solution)/shard_map/convert_element_type | solution.py:410
  578.0 4.4 convert_element_type.79
  582.4 0.6 copy.48
  (70 shorter events, 0.6 us)
Async XLA Ops:
  7.2 557.0 %all-reduce.3.cloned.1.call-start = ((), (), s32[]{:S(2)}) async-start(), calls=%async_computation | async-start | bytes 25165824 | tf_op jit(solution)/shard_map/psum | solution.py:410
  7.2 87.3 %collective-permute-start = (bf16[3072,512]{1,0:T(8,128)(2,1)}, bf16[3072,512]{1,0:T(8,128)(2,1)}, u32[]{:S(2)}, u32[]{:S(2)}) collective-permute-start(bf16[3072,512]{1,0:T(8,128)(2,1)} %refs_0_.1), channel_id=1, source_target_pairs={{0,1},{1,0},{2,3},{3,2},{4,5},{5,4},{6,7},{7,6},{8,9},{9,8},{10,11... | collective-permute-start | bytes 9437192 | tf_op jit(solution)/shard_map/ppermute | solution.py:460
  21.5 2.9 copy-start.11
  25.1 26.5 %copy-start.3 = (s32[12,256]{1,0:T(8,128)}, s32[12,256]{1,0:T(8,128)S(1)}, u32[]{:S(2)}) copy-start(s32[12,256]{1,0:T(8,128)S(1)} %reduce_window_max.21.start_ref) | copy-start | bytes 36868
  309.3 9.1 %slice-start = ((s8[8388608]{0:T(1024)(128)(4,1)}), s8[4194304]{0:T(1024)(128)(4,1)S(1)}, s32[]{:S(2)}) async-start(s8[8388608]{0:T(1024)(128)(4,1)} %bitcast.54), calls=%async_computation.1 | async-start | bytes 8388608
  312.2 6.2 %slice-start.1 = ((s8[8388608]{0:T(1024)(128)(4,1)}), s8[4194304]{0:T(1024)(128)(4,1)S(1)}, s32[]{:S(2)}) async-start(s8[8388608]{0:T(1024)(128)(4,1)} %bitcast.54), calls=%async_computation.2 | async-start | bytes 8388608
  321.1 2.2 copy-start.7
  321.1 2.2 copy-start.6
  321.1 2.2 copy-start.9
  321.1 2.2 copy-start.8
  321.1 2.7 copy-start.4
  321.1 2.7 copy-start.5
  321.1 138.0 %copy-start.1 = (bf16[3072,512]{1,0:T(8,128)(2,1)S(1)}, bf16[3072,512]{1,0:T(8,128)(2,1)}, u32[]{:S(2)}) copy-start(bf16[3072,512]{1,0:T(8,128)(2,1)} %refs_0_.1) | copy-start | bytes 9437188
  321.1 138.0 %collective-permute-start.2 = (bf16[3072,512]{1,0:T(8,128)(2,1)}, bf16[3072,512]{1,0:T(8,128)(2,1)}, u32[]{:S(2)}, u32[]{:S(2)}) collective-permute-start(bf16[3072,512]{1,0:T(8,128)(2,1)} %get-tuple-element.51), channel_id=1, source_target_pairs={{0,1},{1,0},{2,3},{3,2},{4,5},{5,4},{6,7},{7,6},{8,9},{9,8},{10,11... | collective-permute-start | bytes 9437192 | tf_op jit(solution)/shard_map/ppermute | solution.py:441
  321.5 160.5 %collective-permute-start.1 = (bf16[3072,512]{1,0:T(8,128)(2,1)}, bf16[3072,512]{1,0:T(8,128)(2,1)}, u32[]{:S(2)}, u32[]{:S(2)}) collective-permute-start(bf16[3072,512]{1,0:T(8,128)(2,1)} %get-tuple-element.43), channel_id=1, source_target_pairs={{0,1},{1,0},{2,3},{3,2},{4,5},{5,4},{6,7},{7,6},{8,9},{9,8},{10,11... | collective-permute-start | bytes 9437192 | tf_op jit(solution)/shard_map/ppermute | solution.py:441
  323.4 135.7 %collective-permute-start.3 = (f32[4096]{0:T(1024)S(1)}, f32[4096]{0:T(1024)S(1)}, u32[]{:S(2)}, u32[]{:S(2)}) collective-permute-start(f32[4096]{0:T(1024)S(1)} %bitcast.58), channel_id=1, source_target_pairs={{0,1},{1,0},{2,3},{3,2},{4,5},{5,4},{6,7},{7,6},{8,9},{9,8},{10,11... | collective-permute-start | bytes 49160 | tf_op jit(solution)/shard_map/ppermute | solution.py:448
  459.1 14.6 %copy-start.12 = (bf16[512]{0:T(512)(128)(2,1)S(1)}, bf16[512]{0:T(512)(128)(2,1)}, u32[]{:S(2)}) copy-start(bf16[512]{0:T(512)(128)(2,1)} %param.29) | copy-start | bytes 3076
  459.1 14.6 %copy-start.13 = (bf16[512]{0:T(512)(128)(2,1)S(1)}, bf16[512]{0:T(512)(128)(2,1)}, u32[]{:S(2)}) copy-start(bf16[512]{0:T(512)(128)(2,1)} %param.25) | copy-start | bytes 3076
  467.2 2.2 collective-permute-start.4
  469.4 3.9 collective-permute-start.5
  473.3 4.0 collective-permute-start.6
  477.3 12.7 %collective-permute-start.7 = (f32[64,128]{1,0:T(8,128)S(1)}, f32[64,128]{1,0:T(8,128)S(1)}, u32[]{:S(2)}, u32[]{:S(2)}) collective-permute-start(f32[64,128]{1,0:T(8,128)S(1)} %add.94), channel_id=1, source_target_pairs={{0,16},{2,18},{4,20},{6,22},{8,24},{10,26},{12,28},{14,30},{16,0},... | collective-permute-start | bytes 98312 | tf_op jit(solution)/shard_map/ppermute | solution.py:448
  490.7 91.8 %copy-start.10 = (f32[512]{0:T(512)}, f32[512]{0:T(512)S(1)}, u32[]{:S(2)}) copy-start(f32[512]{0:T(512)S(1)} %slice_bitcast_fusion.5) | copy-start | bytes 6148
  564.1 5.5 copy-start.2
  571.2 6.8 %copy-start = (bf16[2048,1024]{1,0:T(8,128)(2,1)S(1)}, bf16[2048,1024]{1,0:T(8,128)(2,1)}, u32[]{:S(2)}) copy-start(bf16[2048,1024]{1,0:T(8,128)(2,1)} %get-tuple-element.79) | copy-start | bytes 12582916
Sparse Core Ops, SparseCore 0:
  321.3 242.8 all-reduce.2

commit v2 on v1

--- a/solution.py
+++ b/solution.py
@@ -14,6 +14,7 @@
 ROT = 16
 NORM_EPS = 1e-05
 VMEM = 60 * 1024 * 1024
+COST = pl.CostEstimate(flops=1, bytes_accessed=1, transcendentals=0)
 GF = 4
 GB = 4
 AHEAD = 2
@@ -28,6 +29,16 @@
 
 def mm(a, b, dims=NN):
     return lax.dot_general(a, b, dims, preferred_element_type=F32)
+
+def rotary_lanes(cos, sin):
+    rest = jnp.ones((64 - ROT, cos.shape[1]), F32)
+    none = jnp.zeros((64 - ROT, cos.shape[1]), F32)
+    blank = jnp.zeros_like(cos)
+    wide = jnp.concatenate([cos, cos, rest] * 2, axis=0)
+    low = jnp.concatenate([-sin, blank, none] * 2, axis=0)
+    high = jnp.concatenate([blank, sin, none] * 2, axis=0)
+    return jnp.transpose(wide), jnp.transpose(low), jnp.transpose(high)
+
 
 def lane_half(shape):
     return lax.broadcasted_iota(jnp.int32, shape, 1) < 64
@@ -107,10 +118,11 @@
         ),
         out_shape=[jax.ShapeDtypeStruct((length, width), BF), jax.ShapeDtypeStruct((width // 64, nq, BQ), F32)],
         compiler_params=pltpu.CompilerParams(vmem_limit_bytes=VMEM),
+        cost_estimate=COST,
         name="attention_forward",
     )(lo, starts, q, k, v)
 
-def bwd_kernel(lo_ref, start_ref, q_ref, k_ref, v_ref, o_ref, do_ref, lse_ref, cos_ref, sa_ref, sb_ref, dq_ref, dk_ref, dv_ref, kt_ref, dk_acc, dv_acc):
+def bwd_kernel(lo_ref, start_ref, q_ref, k_ref, v_ref, o_ref, do_ref, lse_ref, cos_ref, sin_ref, dq_ref, dk_ref, dv_ref, kt_ref, dk_acc, dv_acc):
     length = q_ref.shape[0]
     nq = length // BQ
     nk = length // BK
@@ -120,9 +132,6 @@
     first = lane_half((BQ, PAIR))
     dk_acc[...] = jnp.zeros_like(dk_acc)
     dv_acc[...] = jnp.zeros_like(dv_acc)
-
-    def unrotate(w, rows):
-        return w * cos_ref[rows, :] - pltpu.roll(w, PAIR - 8, 1) * sa_ref[rows, :] - pltpu.roll(w, 8, 1) * sb_ref[rows, :]
 
     cols = [slice(PAIR * g, PAIR * g + PAIR) for g in range(groups)]
 
@@ -175,34 +184,40 @@
         carry = tuple(jnp.zeros((64, BQ), F32) for _ in range(2 * groups))
         carry = lax.fori_loop(lo_ref[b], b, lambda kb, c: step(kb, c, False), carry)
         carry = step(b, carry, True)
+        cos, sin = cos_ref[:, rows], sin_ref[:, rows]
+        wide, low, high = rotary_lanes(cos, sin)
         for g in range(groups):
-            dq = jnp.transpose(jnp.concatenate(carry[2 * g:2 * g + 2], axis=0)) * 0.125
-            dq_ref[rows, cols[g]] = unrotate(dq, rows).astype(BF)
-            dk_ref[rows, cols[g]] = unrotate(dk_acc[rows, cols[g]], rows).astype(BF)
+            turned = []
+            for w in carry[2 * g:2 * g + 2]:
+                turned += [w[:8] * cos + w[8:16] * sin, w[8:16] * cos - w[:8] * sin, w[16:]]
+            dq_ref[rows, cols[g]] = (jnp.transpose(jnp.concatenate(turned, axis=0)) * 0.125).astype(BF)
+            dk = dk_acc[rows, cols[g]]
+            dk = dk * wide - pltpu.roll(dk, PAIR - 8, 1) * low - pltpu.roll(dk, 8, 1) * high
+            dk_ref[rows, cols[g]] = dk.astype(BF)
             dv_ref[rows, cols[g]] = dv_acc[rows, cols[g]].astype(BF)
         return 0
     lax.fori_loop(0, nq, q_block, 0)
 
-def attn_bwd(lo, starts, q, k, v, o, do, lse, cos, sa, sb):
-    length, width = q.shape
+def attn_bwd(group, index, lo, starts, q, k, v, o, do, lse, cos, sin):
+    length = q.shape[0]
     nq = length // BQ
-    group = min(GB * PAIR, width)
-    pairs = width // group
-    col = pl.BlockSpec((length, group), lambda p, *_: (0, p))
-    whole = pl.BlockSpec((length, PAIR), lambda p, *_: (0, 0))
+    col = pl.BlockSpec((length, group), lambda p, *_: (0, index))
+    own = pl.BlockSpec((length, group), lambda p, *_: (0, 0))
+    whole = pl.BlockSpec((ROT // 2, length), lambda p, *_: (0, 0))
     return pl.pallas_call(
         bwd_kernel,
         grid_spec=pltpu.PrefetchScalarGridSpec(
-            num_scalar_prefetch=1, grid=(pairs,),
+            num_scalar_prefetch=1, grid=(1,),
             in_specs=[pl.BlockSpec((nq, BQ), lambda p, *_: (0, 0)), col, col, col, col, col,
-                      pl.BlockSpec((group // 64, nq, BQ), lambda p, *_: (p, 0, 0)), whole, whole, whole],
-            out_specs=[col, col, col],
+                      pl.BlockSpec((group // 64, nq, BQ), lambda p, *_: (index, 0, 0)), whole, whole],
+            out_specs=[own, own, own],
             scratch_shapes=[pltpu.VMEM((length // BK, group, BK), BF), pltpu.VMEM((length, group), F32), pltpu.VMEM((length, group), F32)],
         ),
-        out_shape=[jax.ShapeDtypeStruct((length, width), BF)] * 3,
+        out_shape=[jax.ShapeDtypeStruct((length, group), BF)] * 3,
         compiler_params=pltpu.CompilerParams(vmem_limit_bytes=VMEM),
+        cost_estimate=COST,
         name="attention_backward",
-    )(lo, starts, q, k, v, o, do, lse, cos, sa, sb)
+    )(lo, starts, q, k, v, o, do, lse, cos, sin)
 
 T = 512
 TT = 512
@@ -218,10 +233,15 @@
     return jnp.sum(v.reshape(v.shape[0] // 8, 8, v.shape[1]), axis=0)
 
 
-def project_kernel(x_ref, gain_ref, shift_ref, w_ref, b_ref, cos_ref, sa_ref, sb_ref, q_ref, k_ref, v_ref):
+def project_kernel(x_ref, gain_ref, shift_ref, gain2_ref, shift2_ref, w_ref, b_ref, cos_ref, sin_ref, q_ref, k_ref, v_ref, n1t_ref, n2_ref, n2t_ref):
     local = q_ref.shape[1]
     xhat, _ = norm_rows(x_ref[...].astype(F32))
     normed = (xhat * gain_ref[...] + shift_ref[...]).astype(BF)
+    n1t_ref[...] = jnp.transpose(normed)
+    normed2 = (xhat * gain2_ref[...] + shift2_ref[...]).astype(BF)
+    n2_ref[...] = normed2
+    n2t_ref[...] = jnp.transpose(normed2)
+    wide, low, high = rotary_lanes(cos_ref[...], sin_ref[...])
     for which, out in enumerate((q_ref, k_ref, v_ref)):
         span = slice(which * local, which * local + local)
         y = mm(normed, w_ref[:, span]) + b_ref[:, span]
@@ -231,7 +251,7 @@
         for c in range(local // PAIR):
             cols = slice(c * PAIR, c * PAIR + PAIR)
             u = y[:, cols]
-            u = u * cos_ref[...] + pltpu.roll(u, PAIR - 8, 1) * sa_ref[...] + pltpu.roll(u, 8, 1) * sb_ref[...]
+            u = u * wide + pltpu.roll(u, PAIR - 8, 1) * low + pltpu.roll(u, 8, 1) * high
             out[:, cols] = (u * 0.125 if which == 0 else u).astype(BF)
 
 
@@ -243,19 +263,23 @@
     return pl.BlockSpec((rows, cols), lambda i, *_: (i, 0))
 
 
-def project(x, gain, shift, w, b, cos, sa, sb):
+def across(rows, cols):
+    return pl.BlockSpec((rows, cols), lambda i, *_: (0, i))
+
+
+def project(x, gain, shift, gain2, shift2, w, b, cos, sin):
     length, width = x.shape
     local = w.shape[1] // 3
     return pl.pallas_call(
         project_kernel,
         grid=(length // T,),
-        in_specs=[tokens(T, width), fixed((1, width)), fixed((1, width)), fixed(w.shape), fixed(b.shape)] + [tokens(T, PAIR)] * 3,
-        out_specs=[tokens(T, local)] * 3,
-        out_shape=[jax.ShapeDtypeStruct((length, local), BF)] * 3,
+        in_specs=[tokens(T, width)] + [fixed((1, width))] * 4 + [fixed(w.shape), fixed(b.shape)] + [across(ROT // 2, T)] * 2,
+        out_specs=[tokens(T, local)] * 3 + [across(width, T), tokens(T, width), across(width, T)],
+        out_shape=[jax.ShapeDtypeStruct(s, BF) for s in ((length, local),) * 3 + ((width, length), (length, width), (width, length))],
         compiler_params=pltpu.CompilerParams(vmem_limit_bytes=VMEM),
-        cost_estimate=pl.CostEstimate(flops=2 * length * width * 3 * local, bytes_accessed=length * width * 4, transcendentals=0),
+        cost_estimate=COST,
         name="project_qkv",
-    )(x, gain, shift, w, b, cos, sa, sb)
+    )(x, gain, shift, gain2, shift2, w, b, cos, sin)
 
 
 def scatter_pieces(total, me, outs):
@@ -266,10 +290,31 @@
         outs[d][...] = total[:, cols].astype(outs[d].dtype)
 
 
-def feedforward_kernel(ranks, me_ref, x_ref, gain_ref, shift_ref, w1_ref, b1_ref, w2_ref, wd_ref, mixed_ref, *refs):
+def feedforward_kernel(ranks, part, parts, me_ref, n2_ref, n2t_ref, w1_ref, b1_ref, w2_ref, *refs):
+    first, last = part == 0, part == parts - 1
     pieces, refs = refs[:ranks], refs[ranks:]
-    outs, refs = refs[:ranks], refs[ranks:]
-    mixed_grad_ref, n2g_ref, w1g_ref, w2g_ref, wdg_ref, b1g_ref, lng_ref, lnb_ref, g_ref, n2t_ref, total_ref, back_ref = refs
+    if first:
+        (wd_ref, mixed_ref), refs = refs[:2], refs[2:]
+    else:
+        (total_in, back_in), refs = refs[:2], refs[2:]
+    if last:
+        (x_ref,), refs = refs[:1], refs[1:]
+        outs, refs = refs[:ranks], refs[ranks:]
+        (n2g_ref, lng_ref, lnb_ref), refs = refs[:3], refs[3:]
+        sums = [lng_ref, lnb_ref]
+    else:
+        (total_out, back_out), refs = refs[:2], refs[2:]
+        sums = []
+    if first:
+        (w1_out, w2_out), refs = refs[:2], refs[2:]
+    else:
+        w1_out, w2_out, refs = refs[0].at[0], refs[0].at[1], refs[1:]
+    (b1g_ref,), refs = refs[:1], refs[1:]
+    if first:
+        (mixed_grad_ref, wd_out), refs = refs[:2], refs[2:]
+        (wdg_ref,), refs = refs[:1], refs[1:]
+        sums.append(wdg_ref)
+    w1g_ref, w2g_ref, g_ref, total_ref, back_ref = refs
     step = pl.program_id(0)
     me = me_ref[0]
     local = pieces[0].shape[1]
@@ -279,15 +324,13 @@
 
     @pl.when(step == 0)
     def _():
-        for ref in (w1g_ref, w2g_ref, wdg_ref, b1g_ref, lng_ref, lnb_ref):
+        for ref in [w1g_ref, w2g_ref, b1g_ref] + sums:
             ref[...] = jnp.zeros_like(ref)
 
     for d in range(ranks):
         source = lax.rem(me + d, ranks)
         g_ref[:, pl.ds(pl.multiple_of(source * local, 128), local)] = pieces[d][...]
-    xhat, _ = norm_rows(x_ref[...].astype(F32))
-    normed = (xhat * gain_ref[...] + shift_ref[...]).astype(BF)
-    n2t_ref[...] = jnp.transpose(normed)
+    normed = n2_ref[...]
     g = g_ref[...]
     raw, soft = {}, {}
 
@@ -311,9 +354,12 @@
         active, hidden_grad = soft[c]
         feed = mm(active, w2_ref[cols, :])
         back = mm(hidden_grad, w1_ref[:, cols], NT)
-        if c == 0:
+        if c == 0 and first:
             total_ref[...] = feed
             back_ref[...] = back
+        elif c == 0:
+            total_ref[...] = total_in[...] + feed
+            back_ref[...] = back_in[...] + back
         else:
             total_ref[...] += feed
             back_ref[...] += back
@@ -326,58 +372,151 @@
         bend(c)
         if c >= 1:
             contract(c - 1)
-    mixed = mixed_ref[...]
-    mixed_grad_ref[...] = mm(g, wd_ref[...], NT).astype(BF)
+    if first:
+        mixed = mixed_ref[...]
+        mixed_grad_ref[...] = mm(g, wd_ref[...], NT).astype(BF)
+        wdg_ref[...] += mm(mixed, g, TN)
     contract(chunks - 1)
-    total_ref[...] += mm(mixed, wd_ref[...])
-    wdg_ref[...] += mm(mixed, g, TN)
-    back = back_ref[...]
-    n2g_ref[...] = back.astype(BF)
-    lnb_ref[...] += fold_rows(back)
-    lng_ref[...] += fold_rows(back * xhat)
-    scatter_pieces(total_ref, me, outs)
-
-
-def feedforward(me, x, gain, shift, w1, b1, w2, wd, mixed, pieces):
+    if first:
+        total_ref[...] += mm(mixed, wd_ref[...])
+    if last:
+        xhat, _ = norm_rows(x_ref[...].astype(F32))
+        back = back_ref[...]
+        n2g_ref[...] = back.astype(BF)
+        lnb_ref[...] += fold_rows(back)
+        lng_ref[...] += fold_rows(back * xhat)
+        scatter_pieces(total_ref, me, outs)
+    else:
+        total_out[...] = total_ref[...]
+        back_out[...] = back_ref[...]
+
+    @pl.when(step == pl.num_programs(0) - 1)
+    def _():
+        w1_out[...] = w1g_ref[...].astype(BF)
+        w2_out[...] = w2g_ref[...].astype(BF)
+        if first:
+            wd_out[...] = wdg_ref[...].astype(BF)
+
+
+def feedforward(part, parts, me, x, n2, n2t, w1, b1, w2, wd, mixed, pieces, carried):
     length, width = x.shape
-    local, hidden_units, ranks = mixed.shape[1], w1.shape[1], len(pieces)
-    shapes = [((length, local), F32)] + [((length, local), BF)] * (ranks - 1) + [((length, local), BF), ((length, width), BF)]
-    sums = [(width, hidden_units), (hidden_units, width), (local, width), (8, hidden_units), (8, width), (8, width)]
-    return pl.pallas_call(
-        functools.partial(feedforward_kernel, ranks),
+    local, ranks = pieces[0].shape[1], len(pieces)
+    units = w1.shape[1] // parts
+    first, last = part == 0, part == parts - 1
+    lone = dict(pipeline_mode=pl.Buffered(1))
+    ins = [n2, n2t, w1, b1, w2, *pieces]
+    specs = [
+        tokens(TT, width),
+        across(width, TT),
+        pl.BlockSpec((width, units), lambda i, *_: (0, part), **lone),
+        pl.BlockSpec((1, units), lambda i, *_: (0, part), **lone),
+        pl.BlockSpec((units, width), lambda i, *_: (part, 0), **lone),
+    ] + [tokens(TT, local)] * ranks
+    if first:
+        ins += [wd, mixed]
+        specs += [fixed(wd.shape), tokens(TT, local)]
+    else:
+        ins += list(carried)
+        specs += [tokens(TT, width)] * 2
+    outs = []
+    if last:
+        ins.append(x)
+        specs.append(tokens(TT, width))
+        outs += [(tokens(TT, local), (length, local), F32)] + [(tokens(TT, local), (length, local), BF)] * (ranks - 1)
+        outs += [(tokens(TT, width), (length, width), BF)] + [(fixed((8, width)), (8, width), F32)] * 2
+    else:
+        outs += [(tokens(TT, width), (length, width), F32)] * 2
+    if first:
+        outs += [(fixed((width, units)), (width, units), BF), (fixed((units, width)), (units, width), BF)]
+    else:
+        outs.append((fixed((2, width, units)), (2, width, units), BF))
+    outs.append((fixed((8, units)), (8, units), F32))
+    scratch = []
+    if first:
+        outs += [(tokens(TT, local), (length, local), BF), (fixed((local, width)), (local, width), BF)]
+        scratch.append(pltpu.VMEM((local, width), F32))
+    scratch += [pltpu.VMEM((width, units), F32), pltpu.VMEM((units, width), F32), pltpu.VMEM((TT, width), BF), pltpu.VMEM((TT, width), F32), pltpu.VMEM((TT, width), F32)]
+    made = pl.pallas_call(
+        functools.partial(feedforward_kernel, ranks, part, parts),
         grid_spec=pltpu.PrefetchScalarGridSpec(
             num_scalar_prefetch=1,
             grid=(length // TT,),
-            in_specs=[tokens(TT, width), fixed((1, width)), fixed((1, width)), fixed(w1.shape), fixed(b1.shape), fixed(w2.shape), fixed(wd.shape), tokens(TT, local)]
-            + [tokens(TT, local)] * ranks,
-            out_specs=[tokens(TT, s[1]) for s, _ in shapes] + [fixed(s) for s in sums],
-            scratch_shapes=[pltpu.VMEM((TT, width), BF), pltpu.VMEM((width, TT), BF), pltpu.VMEM((TT, width), F32), pltpu.VMEM((TT, width), F32)],
+            in_specs=specs,
+            out_specs=[o[0] for o in outs],
+            scratch_shapes=scratch,
         ),
-        out_shape=[jax.ShapeDtypeStruct(s, d) for s, d in shapes] + [jax.ShapeDtypeStruct(s, F32) for s in sums],
+        out_shape=[jax.ShapeDtypeStruct(o[1], o[2]) for o in outs],
         compiler_params=pltpu.CompilerParams(vmem_limit_bytes=VMEM),
-        cost_estimate=pl.CostEstimate(flops=2 * length * width * (6 * hidden_units + 3 * local), bytes_accessed=length * width * 12, transcendentals=length * hidden_units),
+        cost_estimate=COST,
         name="feedforward_both_ways",
-    )(me, x, gain, shift, w1, b1, w2, wd, mixed, *pieces)
-
-
-def input_kernel(ranks, me_ref, x_ref, gain1_ref, shift1_ref, gain2_ref, w_ref, dq_ref, dk_ref, dv_ref, n2g_ref, *refs):
+    )(me, *ins)
+    made = list(made)
+    result = {}
+    if last:
+        result["outs"], made = made[:ranks], made[ranks:]
+        result["n2g"], result["ln2g"], result["ln2b"] = made[:3]
+        made = made[3:]
+    else:
+        result["carried"], made = made[:2], made[2:]
+    if first:
+        result["w1g"], result["w2g"], result["b1g"], result["mixed_grad"], result["wdg"] = made
+    else:
+        result["both"], result["b1g"] = made
+    return result
+
+
+def weights_kernel(n1t_ref, dq_ref, dk_ref, dv_ref, out_ref, bg_ref, acc_ref):
+    step = pl.program_id(0)
+
+    @pl.when(step == 0)
+    def _():
+        acc_ref[...] = jnp.zeros_like(acc_ref)
+        bg_ref[...] = jnp.zeros_like(bg_ref)
+
+    n1t = n1t_ref[...]
+    for which, ref in enumerate((dq_ref, dk_ref, dv_ref)):
+        acc_ref[which] += mm(n1t, ref[...])
+        bg_ref[which] += fold_rows(ref[...].astype(F32))
+
+    @pl.when(step == pl.num_programs(0) - 1)
+    def _():
+        out_ref[...] = acc_ref[...].astype(BF)
+
+
+def weights_backward(index, group, n1t, dq, dk, dv):
+    width, length = n1t.shape
+    rows = 1024
+    return pl.pallas_call(
+        weights_kernel,
+        grid=(length // rows,),
+        in_specs=[across(width, rows)] + [pl.BlockSpec((rows, group), lambda i: (i, index))] * 3,
+        out_specs=[fixed((3, width, group)), fixed((3, 8, group))],
+        out_shape=[jax.ShapeDtypeStruct((3, width, group), BF), jax.ShapeDtypeStruct((3, 8, group), F32)],
+        scratch_shapes=[pltpu.VMEM((3, width, group), F32)],
+        compiler_params=pltpu.CompilerParams(vmem_limit_bytes=VMEM),
+        cost_estimate=COST,
+        name="qkv_weights_backward",
+    )(n1t, dq, dk, dv)
+
+
+def input_kernel(ranks, groups, me_ref, x_ref, gain1_ref, gain2_ref, w_ref, n2g_ref, *refs):
+    grads, refs = refs[:3 * groups], refs[3 * groups:]
     outs, refs = refs[:ranks], refs[ranks:]
-    wg_ref, bg_ref, lng_ref, lnb_ref, n1t_ref, total_ref = refs
-    local = dq_ref.shape[1]
+    lng_ref, lnb_ref, total_ref = refs
+    group = grads[0].shape[1]
 
     @pl.when(pl.program_id(0) == 0)
     def _():
-        for ref in (wg_ref, bg_ref, lng_ref, lnb_ref):
-            ref[...] = jnp.zeros_like(ref)
-
+        lng_ref[...] = jnp.zeros_like(lng_ref)
+        lnb_ref[...] = jnp.zeros_like(lnb_ref)
+
+    back = None
+    for which in range(3):
+        for c in range(groups):
+            first = (which * groups + c) * group
+            term = mm(grads[3 * c + which][...], w_ref[:, first:first + group], NT)
+            back = term if back is None else back + term
     xhat, root_inv = norm_rows(x_ref[...].astype(F32))
-    n1t_ref[...] = jnp.transpose((xhat * gain1_ref[...] + shift1_ref[...]).astype(BF))
-    grads = (dq_ref[...], dk_ref[...], dv_ref[...])
-    spans = [slice(w * local, w * local + local) for w in range(3)]
-    back = mm(grads[0], w_ref[:, spans[0]], NT) + mm(grads[1], w_ref[:, spans[1]], NT) + mm(grads[2], w_ref[:, spans[2]], NT)
-    for grad, span in zip(grads, spans):
-        wg_ref[:, span] += mm(n1t_ref[...], grad)
-        bg_ref[:, span] += fold_rows(grad.astype(F32))
     lnb_ref[...] += fold_rows(back)
     lng_ref[...] += fold_rows(back * xhat)
     e = back * gain1_ref[...] + n2g_ref[...].astype(F32) * gain2_ref[...]
@@ -385,29 +524,27 @@
     scatter_pieces(total_ref, me_ref[0], outs)
 
 
-def input_backward(me, ranks, x, gain1, shift1, gain2, w, dq, dk, dv, n2g):
-    length, width = x.shape
-    local = dq.shape[1]
-    shapes = [((length, local), F32)] + [((length, local), BF)] * (ranks - 1)
-    sums = [w.shape, (8, w.shape[1]), (8, width), (8, width)]
+def input_backward(start, rows, me, ranks, x, gain1, gain2, w, n2g, grads):
+    width = x.shape[1]
+    group = grads[0].shape[1]
+    local = w.shape[1] // 3
+    shift = start // T
+    piece = lambda cols: pl.BlockSpec((T, cols), lambda i, *_: (i + shift, 0))
+    shapes = [((rows, local), F32)] + [((rows, local), BF)] * (ranks - 1)
     return pl.pallas_call(
-        functools.partial(input_kernel, ranks),
+        functools.partial(input_kernel, ranks, len(grads) // 3),
         grid_spec=pltpu.PrefetchScalarGridSpec(
             num_scalar_prefetch=1,
-            grid=(length // T,),
-            in_specs=[tokens(T, width), fixed((1, width)), fixed((1, width)), fixed((1, width)), fixed(w.shape)] + [tokens(T, local)] * 3 + [tokens(T, width)],
-            out_specs=[tokens(T, s[1]) for s, _ in shapes] + [fixed(s) for s in sums],
-            scratch_shapes=[pltpu.VMEM((width, T), BF), pltpu.VMEM((T, width), F32)],
+            grid=(rows // T,),
+            in_specs=[piece(width), fixed((1, width)), fixed((1, width)), fixed(w.shape), piece(width)] + [piece(group)] * len(grads),
+            out_specs=[tokens(T, s[1]) for s, _ in shapes] + [fixed((8, width))] * 2,
+            scratch_shapes=[pltpu.VMEM((T, width), F32)],
         ),
-        out_shape=[jax.ShapeDtypeStruct(s, d) for s, d in shapes] + [jax.ShapeDtypeStruct(s, F32) for s in sums],
+        out_shape=[jax.ShapeDtypeStruct(s, d) for s, d in shapes] + [jax.ShapeDtypeStruct((8, width), F32)] * 2,
         compiler_params=pltpu.CompilerParams(vmem_limit_bytes=VMEM),
-        cost_estimate=pl.CostEstimate(flops=2 * length * width * 6 * local, bytes_accessed=length * width * 12, transcendentals=0),
+        cost_estimate=COST,
         name="input_backward",
-    )(me, x, gain1, shift1, gain2, w, dq, dk, dv, n2g)
-
-
-def sum_weights(grads, packs):
-    return [v.astype(F32) for v in lax.psum(tuple(v.astype(BF) for v in grads), "dp")]
+    )(me, x, gain1, gain2, w, n2g, *grads)
 
 
 def rotary_tables(segments):
@@ -416,18 +553,13 @@
     first = jnp.concatenate([jnp.ones((1,), dtype=bool), segments[1:] != segments[:-1]])
     starts = lax.cummax(jnp.where(first, places, jnp.zeros_like(places)), axis=0)
     offsets = (places - starts).astype(F32)
-    lane = jnp.arange(PAIR, dtype=jnp.int32) % 64
-    inverse = 10000.0 ** (-(2 * (lane % (ROT // 2))).astype(F32) / ROT)
-    angles = offsets[:, None] * inverse[None, :]
-    cosine, sine = jnp.cos(angles), jnp.sin(angles)
-    turned = lane < ROT
-    low = lane < ROT // 2
-    return (
-        starts,
-        jnp.where(turned, cosine, 1.0),
-        jnp.where(low, -sine, 0.0),
-        jnp.where(turned & ~low, sine, 0.0),
-    )
+    inverse = 10000.0 ** (-jnp.arange(0, ROT, 2).astype(F32) / ROT)
+    angles = inverse[:, None] * offsets[None, :]
+    return starts, jnp.cos(angles), jnp.sin(angles)
+
+
+def tie(value, *others):
+    return lax.optimization_barrier((value, *others))[0]
 
 
 def shifted(ranks, distance):
@@ -436,10 +568,8 @@
 
 def send_pieces(pieces):
     ranks = len(pieces)
-    total = pieces[0]
-    for d in range(1, ranks):
-        total = total + lax.ppermute(pieces[d], "tensor", shifted(ranks, d)).astype(F32)
-    return total
+    came = [lax.ppermute(pieces[d], "tensor", shifted(ranks, d)) for d in range(1, ranks)]
+    return sum([c.astype(F32) for c in came], pieces[0]), came
 
 
 def swap_sum(value, axis, ranks):
@@ -450,44 +580,118 @@
     return value
 
 
+def halve_sum(value, packs, step):
+    bit = (lax.axis_index("dp") // step) % 2
+    half = value.shape[0] // 2
+    sent = lax.dynamic_slice_in_dim(value, (1 - bit) * half, half, 0).astype(BF)
+    kept = lax.dynamic_slice_in_dim(value, bit * half, half, 0).astype(F32)
+    return kept + lax.ppermute(sent, "dp", [(i, i ^ step) for i in range(packs)]).astype(F32)
+
+
+def double(value, packs, step):
+    bit = (lax.axis_index("dp") // step) % 2
+    other = lax.ppermute(value, "dp", [(i, i ^ step) for i in range(packs)])
+    return jnp.where(bit == 0, jnp.concatenate([value, other], axis=0), jnp.concatenate([other, value], axis=0))
+
+
+def far_shift(packs, far, distance):
+    return [(i, ((i // far + distance) * far) % packs + i % far) for i in range(packs)]
+
+
+def far_sum(value, packs, far):
+    count = packs // far
+    place = lax.axis_index("dp") // far
+    part = value.shape[0] // count
+    total = lax.dynamic_slice_in_dim(value, place * part, part, 0)
+    for d in range(1, count):
+        sent = lax.dynamic_slice_in_dim(value, ((place + d) % count) * part, part, 0).astype(BF)
+        total = total + lax.ppermute(sent, "dp", far_shift(packs, far, d)).astype(F32)
+    return total
+
+
+def far_gather(value, packs, far):
+    count = packs // far
+    place = lax.axis_index("dp") // far
+    part = value.shape[0]
+    whole = jnp.zeros((count * part,) + value.shape[1:], value.dtype)
+    whole = lax.dynamic_update_slice_in_dim(whole, value, place * part, 0)
+    for d in range(1, count):
+        came = lax.ppermute(value, "dp", far_shift(packs, far, d))
+        whole = lax.dynamic_update_slice_in_dim(whole, came, ((place + count - d) % count) * part, 0)
+    return whole
+
+
 def on_device(sizes, inputs, segment_ids, cotangent, ln1_gain, attention_norm_bias, ln2_gain, feedforward_norm_bias, w_qkv, b_qkv, w_dense, b_dense, w_fc1, b_fc1, w_fc2, b_fc2):
     packs, ranks = sizes
     segments = segment_ids[0]
-    width = inputs.shape[1]
+    length, width = inputs.shape
     local = w_qkv.shape[2]
-    hidden_units = w_fc1.shape[1]
     me = lax.axis_index("tensor").astype(jnp.int32).reshape(1)
     pieces = [cotangent] + [lax.ppermute(cotangent, "tensor", shifted(ranks, ranks - d)) for d in range(1, ranks)]
-    starts, cosine, sine_a, sine_b = rotary_tables(segments)
+    starts, cosine, sine = rotary_tables(segments)
     starts = starts.reshape(-1, BQ)
     lowest = starts[:, 0] // BK
     row = lambda v: v.astype(F32).reshape(1, -1)
     qkv_matrix = w_qkv.reshape(width, 3 * local)
     gain1, gain2 = row(ln1_gain), row(ln2_gain)
     shift1, shift2 = row(attention_norm_bias), row(feedforward_norm_bias)
-    query, key, value = project(inputs, gain1, shift1, qkv_matrix, row(b_qkv), cosine, sine_a, sine_b)
+    query, key, value, n1t, n2, n2t = project(inputs, gain1, shift1, gain2, shift2, qkv_matrix, row(b_qkv), cosine, sine)
     mixed, totals = attn_fwd(lowest, starts, query, key, value)
-    made = feedforward(me, inputs, gain2, shift2, w_fc1, row(b_fc1), w_fc2, w_dense, mixed, pieces)
-    outs, (mixed_grad, normed2_grad, w1g, w2g, wdg, b1g, ln2g, ln2b) = made[:ranks], made[ranks:]
+    parts = 2 if w_fc1.shape[1] == 2 * width else 1
+    made, carried = [], None
+    for part in range(parts):
+        made.append(feedforward(part, parts, me, inputs, n2, n2t, w_fc1, row(b_fc1), w_fc2, w_dense, mixed, pieces, carried))
+        carried = made[-1].get("carried")
+    early = lax.psum((made[0]["w1g"], made[0]["w2g"], made[0]["wdg"]), "dp")
+    late = [lax.psum_scatter(m["both"].reshape(2 * width, width), "dp", scatter_dimension=0, tiled=True) for m in made[1:]]
     own = lax.dynamic_slice_in_dim(inputs, me[0] * local, local, 1).astype(F32)
-    outputs = (send_pieces(outs) + own + b_dense.astype(F32) + b_fc2.astype(F32)).astype(BF)
-    big = sum_weights((w1g, w2g, wdg), packs)
-    dq, dk, dv = attn_bwd(lowest, starts, query, key, value, mixed, mixed_grad, totals, cosine, sine_a, sine_b)
-    made = input_backward(me, ranks, inputs, gain1, shift1, gain2, qkv_matrix, dq, dk, dv, normed2_grad)
-    partials, (wg, bg, ln1g, ln1b) = made[:ranks], made[ranks:]
-    input_grad = send_pieces(partials) + cotangent.astype(F32)
-    (wg,) = sum_weights((wg,), packs)
+    outputs = (send_pieces(made[-1]["outs"])[0] + own + b_dense.astype(F32) + b_fc2.astype(F32)).astype(BF)
+    grads = attn_bwd(min(GB * PAIR, local), 0, lowest, starts, query, key, value, mixed, made[0]["mixed_grad"], totals, cosine, sine)
+    group = min(2 * PAIR, local)
+    groups = local // group
+    count = 3 if length % (3 * T) == 0 else 1
+    rows = length // count
+    weights, biases, input_grad, norms, arrived = [], [], [], [], []
+    n1t = tie(n1t, grads[0], *early)
+    for c in range(groups):
+        wg, bg = weights_backward(c, group, n1t, *grads)
+        wg = halve_sum(wg.reshape(3 * width, group), packs, 1)
+        n1t = tie(n1t, wg)
+        biases.append(jnp.sum(bg, axis=1))
+        weights.append(halve_sum(wg, packs, 2))
+    normed2_grad = tie(made[-1]["n2g"], n1t, outputs, *weights[:-1])
+    for c in range(count):
+        got = input_backward(c * rows, rows, me, ranks, inputs, gain1, gain2, qkv_matrix, normed2_grad, grads)
+        total, came = send_pieces(got[:ranks])
+        arrived += came[:1]
+        input_grad.append(total + cotangent[c * rows : c * rows + rows].astype(F32))
+        norms.append(jnp.stack([jnp.sum(v, axis=0) for v in got[ranks:]]))
+        if c == 0:
+            normed2_grad = tie(normed2_grad, got[0], *weights)
+            wg = far_sum(jnp.concatenate(weights, axis=1), packs, 4).astype(BF)
+        if c == 1:
+            normed2_grad = tie(normed2_grad, got[0], wg)
+            wg = far_gather(wg, packs, 4)
+    if count == 1:
+        wg = far_gather(wg, packs, 4)
+    norms[-1] = tie(norms[-1], *arrived[:2], *late)
+    late = lax.optimization_barrier((*late, got[0]))[:-1]
+    late = [lax.all_gather(v, "dp", axis=0, tiled=True) for v in late]
+    input_grad = jnp.concatenate(input_grad, axis=0)
+    wg = double(double(wg, packs, 2), packs, 1).astype(F32)
+    qkv_weight_grad = wg.reshape(3, width, local).transpose(1, 0, 2)
+    norms = jnp.concatenate([sum(norms)] + [jnp.sum(made[-1][n], axis=0, keepdims=True) for n in ("ln2g", "ln2b")], axis=0)
     out_bias = jnp.sum(cotangent.astype(F32), axis=0)
-    norms = jnp.stack([jnp.sum(v, axis=0) for v in (ln1g, ln1b, ln2g, ln2b)]).reshape(-1)
+    b1g = [jnp.sum(m["b1g"], axis=0) for m in made]
+    bias = jnp.concatenate(biases, axis=1).reshape(-1)
+    small = jnp.concatenate([norms.reshape(-1), out_bias, bias] + b1g).reshape(-1, 128)
+    small = swap_sum(small, "dp", packs).reshape(-1)
+    norms, small = small[: 4 * width].reshape(4, width), small[4 * width :]
     norms = swap_sum(norms, "tensor", ranks)
-    biases = (jnp.sum(bg, axis=0), out_bias, jnp.sum(b1g, axis=0))
-    small = jnp.concatenate((norms,) + biases).reshape(-1, 128)
-    small = swap_sum(small, "dp", packs).reshape(-1)
-    norms = small[: 4 * width].reshape(4, width)
-    small = small[4 * width :]
-    qkv_bias_grad = small[: 3 * local].reshape(3, local)
-    dense_bias_grad = small[3 * local : 4 * local]
-    fc1_bias_grad = small[4 * local :]
+    dense_bias_grad, small = small[:local], small[local:]
+    qkv_bias_grad, fc1_bias_grad = small[: 3 * local].reshape(3, local), small[3 * local :]
+    w1g = [v.astype(F32) for v in [early[0]] + [v[:width] for v in late]]
+    w2g = [v.astype(F32) for v in [early[1]] + [v[width:] for v in late]]
     return (
         outputs,
         input_grad,
@@ -495,13 +699,13 @@
         norms[1],
         norms[2],
         norms[3],
-        wg.reshape(width, 3, local),
+        qkv_weight_grad,
         qkv_bias_grad,
-        big[2],
+        early[2].astype(F32),
         dense_bias_grad,
-        big[0],
+        jnp.concatenate(w1g, axis=1),
         fc1_bias_grad,
-        big[1],
+        jnp.concatenate(w2g, axis=0),
         dense_bias_grad,
     )
 

time: 594 us -> 521 us (0.88)
  waiting for transfers between devices: 216 us -> 81.7 us
  Pallas kernels: 269 us -> 299 us
  starting transfers between devices: 12 us -> 35.6 us
  local copies, waits for them, and re-layouts: 18.3 us -> 26.1 us
    ppermute x5, waiting for transfers between devices: 144 us -> 0.9 us  [swap_sum(): lax.ppermute(value, axis, [(i, i ^ step) for i in range(ranks)])]
    ppermute x2 -> x16, waiting for transfers between devices: 0.01 us -> 75.3 us  [the longest x4 33.7 us: send_pieces(): lax.ppermute(pieces[d], 'tensor', shifted(ranks, d))]
    psum x1, waiting for transfers between devices: 72.3 us -> 5.39 us  [on_device(): early = lax.psum((made[0]['w1g'], made[0]['w2g'], made[0]['wdg']), 'dp')]
    pallas_call x2 -> x7, Pallas kernels: 144 us -> 171 us  [the longest x2 120 us: feedforward(): pl.pallas_call(functools.partial(feedforward_kernel, ranks, part, parts),...]
    convert_element_type x8 -> x3, other arithmetic: 35.7 us -> 11 us  [the longest x1 7.97 us: on_device(): (send_pieces(made[-1]['outs'])[0] + own + b_dense.astype(F32) + b_fc2.ast...]
    ppermute x2 -> x16, starting transfers between devices: 2.09 us -> 22.1 us  [the longest x3 7.26 us: far_sum(): lax.ppermute(sent, 'dp', far_shift(packs, far, d)).astype(F32)]
    concatenate x0 -> x4, other arithmetic: none -> 12.4 us  [the longest x1 4.54 us: on_device(): jnp.concatenate(w2g, axis=0)]
    add x0 -> x6, other arithmetic: none -> 9.61 us  [the longest x4 4.98 us: halve_sum(): kept + lax.ppermute(sent, 'dp', [(i, i ^ step) for i in range(packs)]).as...]
  transfers between devices with their start and end apart: 9 -> 25, of which waited for: 5 -> 11; matrix products, arithmetic and copies ran while one was open for 7% -> 14% of each run, Pallas kernels for 10% -> 46%
where the time goes in v2:
time: 521 us; the launch traced here: 516 us
  Pallas kernels  299 us (57%)
  waiting for transfers between devices  81.7 us (16%)
  other arithmetic  58.8 us (11%)
  starting transfers between devices  35.6 us (7%)
  local copies, waits for them, and re-layouts  26.1 us (5%)
  between operations  14.5 us (3%)
    pallas_call x2, Pallas kernels, feedforward(): pl.pallas_call(functools.partial(feedforward_kernel, ranks, part, parts),...  120 us
    pallas_call x1, Pallas kernels, attn_bwd(): pl.pallas_call(bwd_kernel, grid_spec=pltpu.PrefetchScalarGridSpec(num_sca...  63.6 us
    pallas_call x1, Pallas kernels, attn_fwd(): pl.pallas_call(fwd_kernel, grid_spec=pltpu.PrefetchScalarGridSpec(num_sca...  44.1 us
    ppermute x4, waiting for transfers between devices, send_pieces(): lax.ppermute(pieces[d], 'tensor', shifted(ranks, d))  33.7 us
    pallas_call x3, Pallas kernels, input_backward(): pl.pallas_call(functools.partial(input_kernel, ranks, len(grads) // 3), g...  32.4 us
    ppermute x4, waiting for transfers between devices, halve_sum(): lax.ppermute(sent, 'dp', [(i, i ^ step) for i in range(packs)]).astype(F32)  24.6 us
    pallas_call x1, Pallas kernels, project(): pl.pallas_call(project_kernel, grid=(length // T,), in_specs=[tokens(T, w...  20.3 us
    pallas_call x2, Pallas kernels, weights_backward(): pl.pallas_call(weights_kernel, grid=(length // rows,), in_specs=[across(w...  18.7 us
  transfers between devices with their start and end apart: 25, of which 11 were waited for; matrix products, arithmetic and copies ran while one was open for 14% of the time, Pallas kernels for 46%

profile of v2, /device:TPU:0, one launch (start us, length us, event | category | flops | bytes accessed | tf_op | source)
XLA Modules:
  0.0 515.7 jit_solution(7610049760315793707)
XLA Ops:
  7.2 3.0 collective-permute-start
  11.6 4.6 copy.30
  16.3 4.7 copy.31.w_ref
  25.3 20.3 %project_qkv.1 = (bf16[3072,512]{1,0:T(8,128)(2,1)}, bf16[3072,512]{1,0:T(8,128)(2,1)}, bf16[3072,512]{1,0:T(8,128)(2,1)}, bf16[1024,3072]{1,0:T(8,128)(2,1)}, b...) custom-call(bf16[3072,1024]{1,0:T(8,128)(2,1)} %x_ref.7, f32[1,1024]{1,0:T(1,128)} %bitcast.61, f32[1,1024]{1,0:T(1,128)} %bitcast.74, ...), custom_call_target="tpu_custom_call" | custom-call | flops 1 | bytes 1 | tf_op jit(solution)/shard_map/project_qkv/pallas_call | solution.py:273
  46.4 44.1 %attention_forward.1 = (bf16[3072,512]{1,0:T(8,128)(2,1)}, f32[8,12,256]{2,1,0:T(8,128)}) custom-call(s32[12]{0:T(128)} %and_select_fusion.lo_ref, s32[12,256]{1,0:T(8,128)} %copy-done.8, bf16[3072,512]{1,0:T(8,128)(2,1)} %get-tuple-element.64.q_ref, bf16[3072,512]{1,0:T(8,128)(2,1)} %get-tuple-element.65.k_ref, bf16[3072,512]{1,0:T(8,128)(2,1)} %get-tuple-element.66.v_ref), custom_call_target="tpu_custom_call" | custom-call | flops 1 | bytes 1 | tf_op jit(solution)/shard_map/attention_forward/pallas_call | solution.py:111
  91.2 1.6 copy-done.1
  92.8 61.8 %feedforward_both_ways.2 = (f32[3072,1024]{1,0:T(8,128)}, f32[3072,1024]{1,0:T(8,128)}, bf16[1024,1024]{1,0:T(8,128)(2,1)}, bf16[1024,1024]{1,0:T(8,128)(2,1)}, ...) custom-call(s32[1]{0:T(128)} %bitcast.me_ref, ...), custom_call_target="tpu_custom_call" | custom-call | flops 1 | bytes 1 | tf_op jit(solution)/shard_map/feedforward_both_ways/pallas_call | solution.py:439
  154.7 58.2 %feedforward_both_ways.3 = (f32[3072,512]{1,0:T(8,128)}, bf16[3072,512]{1,0:T(8,128)(2,1)}, bf16[3072,1024]{1,0:T(8,128)(2,1)}, f32[8,1024]{1,0:T(8,128)}, f32[8...) custom-call(s32[1]{0:T(128)} %bitcast.me_ref, bf16[3072,1024]{1,0:T(8,128)(2,1)} %get-tuple-element.62.n2_ref, ...), custom_call_target="tpu_custom_call" | custom-call | flops 1 | bytes 1 | tf_op jit(solution)/shard_map/feedforward_both_ways/pallas_call | solution.py:439
  213.0 63.6 %attention_backward.1 = (bf16[3072,512]{1,0:T(8,128)(2,1)}, bf16[3072,512]{1,0:T(8,128)(2,1)}, bf16[3072,512]{1,0:T(8,128)(2,1)}) custom-call(s32[12]{0:T(128)} %and_select_fusion.lo_ref, s32[12,256]{1,0:T(8,128)} %copy-done.8, bf16[3072,512]{1,0:T(8,128)(2,1)} %get-tuple-element.64.q_ref, bf16[3072,512]{1,0:T(8,128)(2,1)} %get-tuple-element.65.k_ref, ...), custom_call_target="tpu_custom_call" | custom-call | flops 1 | bytes 1 | tf_op jit(solution)/shard_map/attention_backward/pallas_call | solution.py:207
  276.6 5.4 %all-reduce.3.cloned.1.call-done = (bf16[1024,1024]{1,0:T(8,128)(2,1)}, bf16[1024,1024]{1,0:T(8,128)(2,1)}, bf16[512,1024]{1,0:T(8,128)(2,1)}) async-done(((bf16[1024,1024]{1,0:T(8,128)(2,1)}, bf16[1024,1024]{1,0:T(8,128)(2,1)}, bf16[512,1024]{1,0:T(8,128)(2,1)}), (bf16[1024,1024]{1,0:T(8,128)(2,1)}, bf16[1024,1024]{1,0:T(8,128)(2,1)}, bf16[512,1024]{1,0:T(8,128)(2,1)})) %all-reduce.3.cloned.1.call-update) | async-done | bytes 5242896 | tf_op jit(solution)/shard_map/psum | solution.py:645
  282.0 9.1 %qkv_weights_backward.2 = (bf16[3,1024,256]{2,1,0:T(8,128)(2,1)}, f32[3,8,256]{2,1,0:T(8,128)}) custom-call(bf16[1024,3072]{1,0:T(8,128)(2,1)} %get-tuple-element.87.n1t_ref, bf16[3072,512]{1,0:T(8,128)(2,1)} %get-tuple-element.76.dq_ref.refs_0_, bf16[3072,512]{1,0:T(8,128)(2,1)} %get-tuple-element.81.dk_ref.refs_1_, ...), custom_call_target="tpu_custom_call" | custom-call | flops 1 | bytes 1 | tf_op jit(solution)/shard_map/qkv_weights_backward/pallas_call | solution.py:489
  292.4 1.6 collective-permute-start.1
  296.0 9.5 %qkv_weights_backward.3 = (bf16[3,1024,256]{2,1,0:T(8,128)(2,1)}, f32[3,8,256]{2,1,0:T(8,128)}) custom-call(bf16[1024,3072]{1,0:T(8,128)(2,1)} %get-tuple-element.87.n1t_ref, bf16[3072,512]{1,0:T(8,128)(2,1)} %get-tuple-element.76.dq_ref.refs_0_, bf16[3072,512]{1,0:T(8,128)(2,1)} %get-tuple-element.81.dk_ref.refs_1_, ...), custom_call_target="tpu_custom_call" | custom-call | flops 1 | bytes 1 | tf_op jit(solution)/shard_map/qkv_weights_backward/pallas_call | solution.py:489
  307.8 1.9 collective-permute-start.3
  309.7 1.5 convert_add_fusion.3
  312.0 1.5 collective-permute-start.6
  313.5 9.6 %collective-permute-done.3 = bf16[768,256]{1,0:T(8,128)(2,1)} collective-permute-done((bf16[768,256]{1,0:T(8,128)(2,1)}, bf16[768,256]{1,0:T(8,128)(2,1)}, u32[]{:S(2)}, u32[]{:S(2)}) %collective-permute-start.3) | collective-permute-done | bytes 393248 | tf_op jit(solution)/shard_map/ppermute | solution.py:588
  324.2 14.4 %collective-permute-done.6 = bf16[768,256]{1,0:T(8,128)(2,1)} collective-permute-done((bf16[768,256]{1,0:T(8,128)(2,1)}, bf16[768,256]{1,0:T(8,128)(2,1)}, u32[]{:S(2)}, u32[]{:S(2)}) %collective-permute-start.6) | collective-permute-done | bytes 393248 | tf_op jit(solution)/shard_map/ppermute | solution.py:588
  339.7 1.8 collective-permute-start.10
  341.5 2.4 collective-permute-start.8
  343.9 3.1 collective-permute-start.9
  347.0 16.3 %collective-permute-done.1 = bf16[3072,512]{1,0:T(8,128)(2,1)} collective-permute-done((bf16[3072,512]{1,0:T(8,128)(2,1)}, bf16[3072,512]{1,0:T(8,128)(2,1)}, u32[]{:S(2)}, u32[]{:S(2)}) %collective-permute-start.1) | collective-permute-done | bytes 3145760 | tf_op jit(solution)/shard_map/ppermute | solution.py:571
  363.3 8.0 %add_convert_fusion = bf16[3072,512]{1,0:T(8,128)(2,1)} fusion(f32[3072,512]{1,0:T(8,128)} %get-tuple-element.70, bf16[3072,512]{1,0:T(8,128)(2,1)} %collective-permute-done.1, f32[512]{0:T(512)S(1)} %convert_element_type.119, f32[512]{0:T(512)S(1)} %convert_element_type.118, bf16[3072,1024]{1,0:T(8,128)(2,1)} %x_ref.7, s32[]{:T(128)S(6)} %select_n.115), kind=kLoop, calls=%fused_computation.3 | loop fusion | flops 11010048 | bytes 15732740 | tf_op jit(solution)/shard_map/convert_element_type | solution.py:648
  371.2 10.9 %input_backward.3 = (f32[1024,512]{1,0:T(8,128)}, bf16[1024,512]{1,0:T(8,128)(2,1)}, f32[8,1024]{1,0:T(8,128)}, f32[8,1024]{1,0:T(8,128)}) custom-call(s32[1]{0:T(128)} %bitcast.me_ref, bf16[3072,1024]{1,0:T(8,128)(2,1)} %x_ref.7, f32[1,1024]{1,0:T(1,128)} %bitcast.62, f32[1,1024]{1,0:T(1,128)} %bitcast.66, bf16[1024,1536]{1,0:T(8,128)(2,1)} %copy.31.w_ref, ...), custom_call_target="tpu_custom_call" | custom-call | flops 1 | bytes 1 | tf_op jit(solution)/shard_map/input_backward/pallas_call | solution.py:534
  382.1 10.7 %input_backward.4 = (f32[1024,512]{1,0:T(8,128)}, bf16[1024,512]{1,0:T(8,128)(2,1)}, f32[8,1024]{1,0:T(8,128)}, f32[8,1024]{1,0:T(8,128)}) custom-call(s32[1]{0:T(128)} %bitcast.me_ref, bf16[3072,1024]{1,0:T(8,128)(2,1)} %x_ref.7, f32[1,1024]{1,0:T(1,128)} %bitcast.63, f32[1,1024]{1,0:T(1,128)} %bitcast.67, bf16[1024,1536]{1,0:T(8,128)(2,1)} %copy.31.w_ref, ...), custom_call_target="tpu_custom_call" | custom-call | flops 1 | bytes 1 | tf_op jit(solution)/shard_map/input_backward/pallas_call | solution.py:534
  394.6 10.8 %input_backward.5 = (f32[1024,512]{1,0:T(8,128)}, bf16[1024,512]{1,0:T(8,128)(2,1)}, f32[8,1024]{1,0:T(8,128)}, f32[8,1024]{1,0:T(8,128)}) custom-call(s32[1]{0:T(128)} %bitcast.me_ref, bf16[3072,1024]{1,0:T(8,128)(2,1)} %x_ref.7, f32[1,1024]{1,0:T(1,128)} %bitcast.64, f32[1,1024]{1,0:T(1,128)} %bitcast.68, bf16[1024,1536]{1,0:T(8,128)(2,1)} %copy.31.w_ref, ...), custom_call_target="tpu_custom_call" | custom-call | flops 1 | bytes 1 | tf_op jit(solution)/shard_map/input_backward/pallas_call | solution.py:534
  405.5 1.7 collective-permute-start.4
  410.0 3.4 collective-permute-start.17
  415.9 2.6 collective-permute-start.19
  418.5 1.4 reduce_sum.121
  419.8 1.4 reduce_sum.122
  423.5 11.2 %collective-permute-done.18 = bf16[192,512]{1,0:T(8,128)(2,1)} collective-permute-done((bf16[192,512]{1,0:T(8,128)(2,1)}, bf16[192,512]{1,0:T(8,128)(2,1)}, u32[]{:S(2)}, u32[]{:S(2)}) %collective-permute-start.18) | collective-permute-done | bytes 196640 | tf_op jit(solution)/shard_map/ppermute | solution.py:619
  434.7 1.6 constant_dynamic-update-slice_fusion.1
  437.7 16.8 %collective-permute-done.7 = bf16[1024,512]{1,0:T(8,128)(2,1)} collective-permute-done((bf16[1024,512]{1,0:T(8,128)(2,1)}, bf16[1024,512]{1,0:T(8,128)(2,1)}, u32[]{:S(2)}, u32[]{:S(2)}) %collective-permute-start.7) | collective-permute-done | bytes 1048608 | tf_op jit(solution)/shard_map/ppermute | solution.py:571
  456.8 2.9 convert_element_type.144
  459.7 1.6 collective-permute-start.13
  461.4 5.7 %collective-permute-done.20 = bf16[768,512]{1,0:T(8,128)(2,1)} collective-permute-done((bf16[768,512]{1,0:T(8,128)(2,1)}, bf16[768,512]{1,0:T(8,128)(2,1)}, u32[]{:S(2)}, u32[]{:S(2)}) %collective-permute-start.20) | collective-permute-done | bytes 786464 | tf_op jit(solution)/shard_map/ppermute | solution.py:593
  467.1 3.1 maximum_select_fusion.1
  470.2 4.8 collective-permute-start.14
  475.6 3.9 convert_add_fusion.2
  479.5 2.2 collective-permute-start.15
  481.7 3.4 pad_maximum_fusion
  485.1 1.7 collective-permute-start.16
  489.5 3.4 maximum_select_fusion
  493.0 3.6 convert_bitcast_fusion
  496.6 2.8 fusion.14
  499.4 4.5 maximum_convert_fusion.1
  504.0 4.4 maximum_convert_fusion
  (159 shorter events, 32.8 us)
Async XLA Ops:
  7.2 274.8 %all-reduce.3.cloned.1.call-start = ((), (), s32[]{:S(2)}) async-start(), calls=%async_computation.3 | async-start | bytes 10485760 | tf_op jit(solution)/shard_map/psum | solution.py:645
  7.2 83.9 %collective-permute-start = (bf16[3072,512]{1,0:T(8,128)(2,1)}, bf16[3072,512]{1,0:T(8,128)(2,1)S(1)}, u32[]{:S(2)}, u32[]{:S(2)}) collective-permute-start(bf16[3072,512]{1,0:T(8,128)(2,1)} %refs_0_.3), channel_id=1, source_target_pairs={{0,1},{1,0},{2,3},{3,2},{4,5},{5,4},{6,7},{7,6},{8,9},{9,8},{10,11... | collective-permute-start | bytes 9437192 | tf_op jit(solution)/shard_map/ppermute | solution.py:630
  16.3 4.7 copy-start.22
  16.3 5.3 %copy-start.23 = (bf16[1024]{0:T(1024)(128)(2,1)S(1)}, bf16[1024]{0:T(1024)(128)(2,1)}, u32[]{:S(2)}) copy-start(bf16[1024]{0:T(1024)(128)(2,1)} %param.20) | copy-start | bytes 6148
  16.3 5.9 %copy-start.20 = (bf16[3,512]{1,0:T(4,128)(2,1)S(1)}, bf16[3,512]{1,0:T(4,128)(2,1)}, u32[]{:S(2)}) copy-start(bf16[3,512]{1,0:T(4,128)(2,1)} %param.23) | copy-start | bytes 9220
  16.3 6.5 %copy-start.24 = (bf16[1024]{0:T(1024)(128)(2,1)S(1)}, bf16[1024]{0:T(1024)(128)(2,1)}, u32[]{:S(2)}) copy-start(bf16[1024]{0:T(1024)(128)(2,1)} %param.19) | copy-start | bytes 6148
  16.3 7.1 %copy-start.25 = (bf16[1024]{0:T(1024)(128)(2,1)S(1)}, bf16[1024]{0:T(1024)(128)(2,1)}, u32[]{:S(2)}) copy-start(bf16[1024]{0:T(1024)(128)(2,1)} %param.21) | copy-start | bytes 6148
  46.4 44.1 %copy-start.21 = (bf16[2048]{0:T(1024)(128)(2,1)S(1)}, bf16[2048]{0:T(1024)(128)(2,1)}, u32[]{:S(2)}) copy-start(bf16[2048]{0:T(1024)(128)(2,1)} %param.27) | copy-start | bytes 12292
  154.6 250.9 %reduce-scatter.2.cloned.1.call-start = ((), (), s32[]{:S(2)}) async-start(), calls=%async_computation.1 | async-start | bytes 4456448 | tf_op jit(solution)/shard_map/reduce_scatter | solution.py:646
  212.9 283.6 %all-gather.2.cloned.1.call-start = ((), (), s32[]{:S(2)}) async-start(), calls=%async_computation.2 | async-start | bytes 4456448 | tf_op jit(solution)/shard_map/all_gather | solution.py:679
  292.3 2.4 collective-permute-start.2
  292.4 70.8 %collective-permute-start.1 = (bf16[3072,512]{1,0:T(8,128)(2,1)}, bf16[3072,512]{1,0:T(8,128)(2,1)}, u32[]{:S(2)}, u32[]{:S(2)}) collective-permute-start(bf16[3072,512]{1,0:T(8,128)(2,1)} %get-tuple-element.71), channel_id=1, source_target_pairs={{0,1},{1,0},{2,3},{3,2},{4,5},{5,4},{6,7},{7,6},{8,9},{9,8},{10,11... | collective-permute-start | bytes 9437192 | tf_op jit(solution)/shard_map/ppermute | solution.py:571
  305.5 8.0 %copy-start.26 = (bf16[512]{0:T(512)(128)(2,1)S(1)}, bf16[512]{0:T(512)(128)(2,1)}, u32[]{:S(2)}) copy-start(bf16[512]{0:T(512)(128)(2,1)} %param.25) | copy-start | bytes 3076
  305.5 8.0 %copy-start.27 = (bf16[512]{0:T(512)(128)(2,1)S(1)}, bf16[512]{0:T(512)(128)(2,1)}, u32[]{:S(2)}) copy-start(bf16[512]{0:T(512)(128)(2,1)} %param.29) | copy-start | bytes 3076
  306.8 2.9 collective-permute-start.5
  307.8 15.3 %collective-permute-start.3 = (bf16[768,256]{1,0:T(8,128)(2,1)}, bf16[768,256]{1,0:T(8,128)(2,1)}, u32[]{:S(2)}, u32[]{:S(2)}) collective-permute-start(bf16[768,256]{1,0:T(8,128)(2,1)} %dynamic-slice_convert_fusion.1), channel_id=1, source_target_pairs={{0,4},{2,6},{4,0},{6,2},{8,12},{10,14},{12,8},{14,10},{16,20},{18,... | collective-permute-start | bytes 1179656 | tf_op jit(solution)/shard_map/ppermute | solution.py:588
  312.0 26.5 %collective-permute-start.6 = (bf16[768,256]{1,0:T(8,128)(2,1)}, bf16[768,256]{1,0:T(8,128)(2,1)}, u32[]{:S(2)}, u32[]{:S(2)}) collective-permute-start(bf16[768,256]{1,0:T(8,128)(2,1)} %dynamic-slice_convert_fusion), channel_id=1, source_target_pairs={{0,4},{2,6},{4,0},{6,2},{8,12},{10,14},{12,8},{14,10},{16,20},{18,... | collective-permute-start | bytes 1179656 | tf_op jit(solution)/shard_map/ppermute | solution.py:588
  339.7 53.1 %collective-permute-start.10 = (bf16[192,512]{1,0:T(8,128)(2,1)S(1)}, bf16[192,512]{1,0:T(8,128)(2,1)S(1)}, u32[]{:S(2)}, u32[]{:S(2)}) collective-permute-start(bf16[192,512]{1,0:T(8,128)(2,1)S(1)} %get-tuple-element.122), channel_id=1, source_target_pairs={{0,24},{2,26},{4,28},{6,30},{8,0},{10,2},{12,4},{14,6},{16,8},{18,... | collective-permute-start | bytes 589832 | tf_op jit(solution)/shard_map/ppermute | solution.py:608
  341.5 51.3 %collective-permute-start.8 = (bf16[192,512]{1,0:T(8,128)(2,1)S(1)}, bf16[192,512]{1,0:T(8,128)(2,1)S(1)}, u32[]{:S(2)}, u32[]{:S(2)}) collective-permute-start(bf16[192,512]{1,0:T(8,128)(2,1)S(1)} %get-tuple-element.120), channel_id=1, source_target_pairs={{0,8},{2,10},{4,12},{6,14},{8,16},{10,18},{12,20},{14,22},{16,24},... | collective-permute-start | bytes 589832 | tf_op jit(solution)/shard_map/ppermute | solution.py:608
  343.9 48.9 %collective-permute-start.9 = (bf16[192,512]{1,0:T(8,128)(2,1)S(1)}, bf16[192,512]{1,0:T(8,128)(2,1)S(1)}, u32[]{:S(2)}, u32[]{:S(2)}) collective-permute-start(bf16[192,512]{1,0:T(8,128)(2,1)S(1)} %get-tuple-element.121), channel_id=1, source_target_pairs={{0,16},{2,18},{4,20},{6,22},{8,24},{10,26},{12,28},{14,30},{16,0},... | collective-permute-start | bytes 589832 | tf_op jit(solution)/shard_map/ppermute | solution.py:608
  394.6 13.1 %copy-start = (bf16[3072,512]{1,0:T(8,128)(2,1)S(1)}, bf16[3072,512]{1,0:T(8,128)(2,1)}, u32[]{:S(2)}) copy-start(bf16[3072,512]{1,0:T(8,128)(2,1)} %refs_0_.3) | copy-start | bytes 9437188
  405.4 3.9 copy-start.11
  405.4 4.5 copy-start.9
  405.4 4.5 copy-start.10
  405.4 4.5 copy-start.17
  405.4 4.5 copy-start.18
  405.4 8.0 %copy-start.15 = (f32[8,1024]{1,0:T(8,128)S(1)}, f32[8,1024]{1,0:T(8,128)}, u32[]{:S(2)}) copy-start(f32[8,1024]{1,0:T(8,128)} %get-tuple-element.95) | copy-start | bytes 98308
  405.5 8.6 %copy-start.13 = (f32[8,1024]{1,0:T(8,128)S(1)}, f32[8,1024]{1,0:T(8,128)}, u32[]{:S(2)}) copy-start(f32[8,1024]{1,0:T(8,128)} %get-tuple-element.96) | copy-start | bytes 98308
  405.5 9.2 %copy-start.16 = (f32[8,1024]{1,0:T(8,128)S(1)}, f32[8,1024]{1,0:T(8,128)}, u32[]{:S(2)}) copy-start(f32[8,1024]{1,0:T(8,128)} %get-tuple-element.97) | copy-start | bytes 98308
  405.5 9.8 %copy-start.14 = (f32[8,1024]{1,0:T(8,128)S(1)}, f32[8,1024]{1,0:T(8,128)}, u32[]{:S(2)}) copy-start(f32[8,1024]{1,0:T(8,128)} %get-tuple-element.98) | copy-start | bytes 98308
  405.5 32.2 %collective-permute-start.4 = (bf16[1024,512]{1,0:T(8,128)(2,1)}, bf16[1024,512]{1,0:T(8,128)(2,1)}, u32[]{:S(2)}, u32[]{:S(2)}) collective-permute-start(bf16[1024,512]{1,0:T(8,128)(2,1)} %get-tuple-element.86), channel_id=1, source_target_pairs={{0,1},{1,0},{2,3},{3,2},{4,5},{5,4},{6,7},{7,6},{8,9},{9,8},{10,11... | collective-permute-start | bytes 3145736 | tf_op jit(solution)/shard_map/ppermute | solution.py:571
  407.2 47.2 %collective-permute-start.7 = (bf16[1024,512]{1,0:T(8,128)(2,1)}, bf16[1024,512]{1,0:T(8,128)(2,1)}, u32[]{:S(2)}, u32[]{:S(2)}) collective-permute-start(bf16[1024,512]{1,0:T(8,128)(2,1)} %get-tuple-element.91), channel_id=1, source_target_pairs={{0,1},{1,0},{2,3},{3,2},{4,5},{5,4},{6,7},{7,6},{8,9},{9,8},{10,11... | collective-permute-start | bytes 3145736 | tf_op jit(solution)/shard_map/ppermute | solution.py:571
  410.0 12.0 %collective-permute-start.17 = (bf16[192,512]{1,0:T(8,128)(2,1)}, bf16[192,512]{1,0:T(8,128)(2,1)S(1)}, u32[]{:S(2)}, u32[]{:S(2)}) collective-permute-start(bf16[192,512]{1,0:T(8,128)(2,1)} %get-tuple-element.114), channel_id=1, source_target_pairs={{0,8},{2,10},{4,12},{6,14},{8,16},{10,18},{12,20},{14,22},{16,24},... | collective-permute-start | bytes 589832 | tf_op jit(solution)/shard_map/ppermute | solution.py:619
  415.9 18.8 %collective-permute-start.18 = (bf16[192,512]{1,0:T(8,128)(2,1)}, bf16[192,512]{1,0:T(8,128)(2,1)}, u32[]{:S(2)}, u32[]{:S(2)}) collective-permute-start(bf16[192,512]{1,0:T(8,128)(2,1)} %get-tuple-element.114), channel_id=1, source_target_pairs={{0,16},{2,18},{4,20},{6,22},{8,24},{10,26},{12,28},{14,30},{16,0},... | collective-permute-start | bytes 589832 | tf_op jit(solution)/shard_map/ppermute | solution.py:619
  415.9 20.4 %collective-permute-start.19 = (bf16[192,512]{1,0:T(8,128)(2,1)}, bf16[192,512]{1,0:T(8,128)(2,1)S(1)}, u32[]{:S(2)}, u32[]{:S(2)}) collective-permute-start(bf16[192,512]{1,0:T(8,128)(2,1)} %get-tuple-element.114), channel_id=1, source_target_pairs={{0,24},{2,26},{4,28},{6,30},{8,0},{10,2},{12,4},{14,6},{16,8},{18,... | collective-permute-start | bytes 589832 | tf_op jit(solution)/shard_map/ppermute | solution.py:619
  422.1 53.5 %collective-permute-start.11 = (bf16[1024,512]{1,0:T(8,128)(2,1)}, bf16[1024,512]{1,0:T(8,128)(2,1)}, u32[]{:S(2)}, u32[]{:S(2)}) collective-permute-start(bf16[1024,512]{1,0:T(8,128)(2,1)} %get-tuple-element.94), channel_id=1, source_target_pairs={{0,1},{1,0},{2,3},{3,2},{4,5},{5,4},{6,7},{7,6},{8,9},{9,8},{10,11... | collective-permute-start | bytes 3145736 | tf_op jit(solution)/shard_map/ppermute | solution.py:571
  436.9 30.1 %collective-permute-start.20 = (bf16[768,512]{1,0:T(8,128)(2,1)}, bf16[768,512]{1,0:T(8,128)(2,1)}, u32[]{:S(2)}, u32[]{:S(2)}) collective-permute-start(bf16[768,512]{1,0:T(8,128)(2,1)} %constant_dynamic-update-slice_fusion), channel_id=1, source_target_pairs={{0,4},{2,6},{4,0},{6,2},{8,12},{10,14},{12,8},{14,10},{16,20},{18,... | collective-permute-start | bytes 2359304 | tf_op jit(solution)/shard_map/ppermute | solution.py:593
  456.7 3.1 collective-permute-start.12
  456.8 10.3 %copy-start.3 = (bf16[768,512]{1,0:T(8,128)(2,1)S(1)}, bf16[768,512]{1,0:T(8,128)(2,1)}, u32[]{:S(2)}) copy-start(bf16[768,512]{1,0:T(8,128)(2,1)} %constant_dynamic-update-slice_fusion) | copy-start | bytes 2359300
  456.8 18.8 %copy-start.4 = (f32[1024,512]{1,0:T(8,128)S(1)}, f32[1024,512]{1,0:T(8,128)}, u32[]{:S(2)}) copy-start(f32[1024,512]{1,0:T(8,128)} %get-tuple-element.85) | copy-start | bytes 6291460
  456.8 18.8 %copy-start.5 = (f32[1024,512]{1,0:T(8,128)S(1)}, f32[1024,512]{1,0:T(8,128)}, u32[]{:S(2)}) copy-start(f32[1024,512]{1,0:T(8,128)} %get-tuple-element.90) | copy-start | bytes 6291460
  459.7 10.5 %collective-permute-start.13 = (f32[64,128]{1,0:T(8,128)S(1)}, f32[64,128]{1,0:T(8,128)S(1)}, u32[]{:S(2)}, u32[]{:S(2)}) collective-permute-start(f32[64,128]{1,0:T(8,128)S(1)} %bitcast_add_fusion), channel_id=1, source_target_pairs={{0,4},{2,6},{4,0},{6,2},{8,12},{10,14},{12,8},{14,10},{16,20},{18,... | collective-permute-start | bytes 98312 | tf_op jit(solution)/shard_map/ppermute | solution.py:578
  470.2 19.3 %collective-permute-start.21 = (bf16[1536,512]{1,0:T(8,128)(2,1)}, bf16[1536,512]{1,0:T(8,128)(2,1)}, u32[]{:S(2)}, u32[]{:S(2)}) collective-permute-start(bf16[1536,512]{1,0:T(8,128)(2,1)} %maximum_select_fusion.1), channel_id=1, source_target_pairs={{0,2},{2,0},{4,6},{6,4},{8,10},{10,8},{12,14},{14,12},{16,18},{18,... | collective-permute-start | bytes 4718600 | tf_op jit(solution)/shard_map/ppermute | solution.py:593
  470.2 9.3 %collective-permute-start.14 = (f32[64,128]{1,0:T(8,128)S(1)}, f32[64,128]{1,0:T(8,128)S(1)}, u32[]{:S(2)}, u32[]{:S(2)}) collective-permute-start(f32[64,128]{1,0:T(8,128)S(1)} %fusion.16), channel_id=1, source_target_pairs={{0,8},{2,10},{4,12},{6,14},{8,0},{10,2},{12,4},{14,6},{16,24},{18,... | collective-permute-start | bytes 98312 | tf_op jit(solution)/shard_map/ppermute | solution.py:578
  479.5 5.6 %collective-permute-start.15 = (f32[64,128]{1,0:T(8,128)S(1)}, f32[64,128]{1,0:T(8,128)S(1)}, u32[]{:S(2)}, u32[]{:S(2)}) collective-permute-start(f32[64,128]{1,0:T(8,128)S(1)} %add.214), channel_id=1, source_target_pairs={{0,16},{2,18},{4,20},{6,22},{8,24},{10,26},{12,28},{14,30},{16,0},... | collective-permute-start | bytes 98312 | tf_op jit(solution)/shard_map/ppermute | solution.py:578
  485.1 3.8 collective-permute-start.16
  487.4 21.0 %copy-start.19 = (f32[512]{0:T(512)}, f32[512]{0:T(512)S(1)}, u32[]{:S(2)}) copy-start(f32[512]{0:T(512)S(1)} %slice_bitcast_fusion.1) | copy-start | bytes 6148
  499.4 4.5 copy-start.6
  (5 other events, 9.3 us)
Sparse Core Ops, SparseCore 0:
  154.8 127.1 all-reduce.2
  286.4 91.3 reduce-scatter.1
  405.7 74.1 all-gather.1

commit v3 on v2

--- a/solution.py
+++ b/solution.py
@@ -580,12 +580,61 @@
     return value
 
 
-def halve_sum(value, packs, step):
-    bit = (lax.axis_index("dp") // step) % 2
-    half = value.shape[0] // 2
-    sent = lax.dynamic_slice_in_dim(value, (1 - bit) * half, half, 0).astype(BF)
-    kept = lax.dynamic_slice_in_dim(value, bit * half, half, 0).astype(F32)
-    return kept + lax.ppermute(sent, "dp", [(i, i ^ step) for i in range(packs)]).astype(F32)
+def pick_kernel(bits_ref, x_ref, out_ref):
+    out_ref[...] = x_ref[...]
+
+
+def merge_kernel(bits_ref, x_ref, came_ref, sent_ref, kept_ref, sum_ref):
+    rows = sent_ref.shape[0]
+    sum_ref[...] = x_ref[...].astype(F32) + came_ref[...].astype(F32)
+    bit = bits_ref[1]
+    sent_ref[...] = sum_ref[pl.ds(pl.multiple_of((1 - bit) * rows, rows), rows), :].astype(BF)
+    kept_ref[...] = sum_ref[pl.ds(pl.multiple_of(bit * rows, rows), rows), :]
+
+
+def pick_half(bits, x):
+    half, cols = x.shape[0] // 2, x.shape[1]
+    quarter = half // 2
+    return pl.pallas_call(
+        pick_kernel,
+        grid_spec=pltpu.PrefetchScalarGridSpec(
+            num_scalar_prefetch=1,
+            grid=(2,),
+            in_specs=[pl.BlockSpec((quarter, cols), lambda i, b: (2 * (1 - b[0]) + i, 0))],
+            out_specs=pl.BlockSpec((quarter, cols), lambda i, b: (i, 0)),
+        ),
+        out_shape=jax.ShapeDtypeStruct((half, cols), BF),
+        compiler_params=pltpu.CompilerParams(vmem_limit_bytes=VMEM),
+        cost_estimate=COST,
+        name="pick_half",
+    )(bits, x)
+
+
+def swap_pair(sent, packs):
+    return lax.ppermute(sent, "dp", [(i, i ^ 1) for i in range(packs)])
+
+
+def merge_halves(bits, x, came):
+    half, cols = came.shape
+    quarter = half // 2
+    return pl.pallas_call(
+        merge_kernel,
+        grid_spec=pltpu.PrefetchScalarGridSpec(
+            num_scalar_prefetch=1,
+            grid=(1,),
+            in_specs=[pl.BlockSpec((half, cols), lambda i, b: (b[0], 0)), pl.BlockSpec((half, cols), lambda i, b: (0, 0))],
+            out_specs=[pl.BlockSpec((quarter, cols), lambda i, b: (0, 0))] * 2,
+            scratch_shapes=[pltpu.VMEM((half, cols), F32)],
+        ),
+        out_shape=[jax.ShapeDtypeStruct((quarter, cols), BF), jax.ShapeDtypeStruct((quarter, cols), F32)],
+        compiler_params=pltpu.CompilerParams(vmem_limit_bytes=VMEM),
+        cost_estimate=COST,
+        name="merge_halves",
+    )(bits, x, came)
+
+
+def cross_sum(sent, kept, packs):
+    return kept + lax.ppermute(sent, "dp", [(i, i ^ 2) for i in range(packs)]).astype(F32)
 
 
 def double(value, packs, step):
@@ -643,40 +692,56 @@
         made.append(feedforward(part, parts, me, inputs, n2, n2t, w_fc1, row(b_fc1), w_fc2, w_dense, mixed, pieces, carried))
         carried = made[-1].get("carried")
     early = lax.psum((made[0]["w1g"], made[0]["w2g"], made[0]["wdg"]), "dp")
-    late = [lax.psum_scatter(m["both"].reshape(2 * width, width), "dp", scatter_dimension=0, tiled=True) for m in made[1:]]
+    place = lax.axis_index("dp").astype(jnp.int32)
+    bits = jnp.stack([place % 2, (place // 2) % 2])
+    late = [m["both"].reshape(2 * width, width) for m in made[1:]]
+    picked = [pick_half(bits, v) for v in late]
+    swapped = [swap_pair(v, packs) for v in picked]
     own = lax.dynamic_slice_in_dim(inputs, me[0] * local, local, 1).astype(F32)
-    outputs = (send_pieces(made[-1]["outs"])[0] + own + b_dense.astype(F32) + b_fc2.astype(F32)).astype(BF)
-    grads = attn_bwd(min(GB * PAIR, local), 0, lowest, starts, query, key, value, mixed, made[0]["mixed_grad"], totals, cosine, sine)
+    total, out_came = send_pieces(made[-1]["outs"])
+    outputs = (total + own + b_dense.astype(F32) + b_fc2.astype(F32)).astype(BF)
+    mixed_grad = tie(made[0]["mixed_grad"], made[-1]["n2g"], *picked)
+    grads = attn_bwd(min(GB * PAIR, local), 0, lowest, starts, query, key, value, mixed, mixed_grad, totals, cosine, sine)
     group = min(2 * PAIR, local)
     groups = local // group
     count = 3 if length % (3 * T) == 0 else 1
     rows = length // count
     weights, biases, input_grad, norms, arrived = [], [], [], [], []
-    n1t = tie(n1t, grads[0], *early)
+
+    def chunk(c, normed2_grad):
+        got = input_backward(c * rows, rows, me, ranks, inputs, gain1, gain2, qkv_matrix, normed2_grad, grads)
+        total, came = send_pieces(got[:ranks])
+        arrived.append(came)
+        input_grad.append(total + cotangent[c * rows : c * rows + rows].astype(F32))
+        norms.append(jnp.stack([jnp.sum(v, axis=0) for v in got[ranks:]]))
+        return got[0]
+
+    late = [merge_halves(bits, tie(v, grads[0], *early), s) for v, s in zip(late, swapped)]
+    normed2_grad = tie(made[-1]["n2g"], grads[0], *early, *[v[1] for v in late])
+    late = [cross_sum(*v, packs) for v in late]
+    done = chunk(0, normed2_grad)
+    n1t = tie(n1t, done)
     for c in range(groups):
         wg, bg = weights_backward(c, group, n1t, *grads)
-        wg = halve_sum(wg.reshape(3 * width, group), packs, 1)
-        n1t = tie(n1t, wg)
+        wg = tie(wg, *out_came, *late) if c == 0 else tie(wg, *arrived[0])
+        wg = wg.reshape(3 * width, group)
+        halves = merge_halves(bits, wg, swap_pair(pick_half(bits, wg), packs))
+        n1t = tie(n1t, halves[1])
+        if c == 0:
+            late = [far_sum(v, packs, 4).astype(BF) for v in late]
         biases.append(jnp.sum(bg, axis=1))
-        weights.append(halve_sum(wg, packs, 2))
-    normed2_grad = tie(made[-1]["n2g"], n1t, outputs, *weights[:-1])
-    for c in range(count):
-        got = input_backward(c * rows, rows, me, ranks, inputs, gain1, gain2, qkv_matrix, normed2_grad, grads)
-        total, came = send_pieces(got[:ranks])
-        arrived += came[:1]
-        input_grad.append(total + cotangent[c * rows : c * rows + rows].astype(F32))
-        norms.append(jnp.stack([jnp.sum(v, axis=0) for v in got[ranks:]]))
-        if c == 0:
-            normed2_grad = tie(normed2_grad, got[0], *weights)
-            wg = far_sum(jnp.concatenate(weights, axis=1), packs, 4).astype(BF)
+        weights.append(cross_sum(*halves, packs))
+    normed2_grad = tie(normed2_grad, halves[1], *arrived[0])
+    for c in range(1, count):
+        done = chunk(c, normed2_grad)
         if c == 1:
-            normed2_grad = tie(normed2_grad, got[0], wg)
-            wg = far_gather(wg, packs, 4)
-    if count == 1:
-        wg = far_gather(wg, packs, 4)
-    norms[-1] = tie(norms[-1], *arrived[:2], *late)
-    late = lax.optimization_barrier((*late, got[0]))[:-1]
-    late = [lax.all_gather(v, "dp", axis=0, tiled=True) for v in late]
+            normed2_grad = tie(normed2_grad, done, *weights, *late)
+    late = [far_gather(v, packs, 4) for v in late]
+    wg = far_sum(jnp.concatenate(weights, axis=1), packs, 4).astype(BF)
+    ready = lax.optimization_barrier((done, wg, norms[-1], *[p for came in arrived[:2] for p in came]))
+    wg, norms[-1] = ready[1], ready[2]
+    wg = far_gather(wg, packs, 4)
+    late = [double(double(v, packs, 2), packs, 1) for v in late]
     input_grad = jnp.concatenate(input_grad, axis=0)
     wg = double(double(wg, packs, 2), packs, 1).astype(F32)
     qkv_weight_grad = wg.reshape(3, width, local).transpose(1, 0, 2)

time: 521 us -> 545 us (1.046)
  waiting for transfers between devices: 81.7 us -> 44.3 us
  other arithmetic: 58.8 us -> 81.1 us
  Pallas kernels: 299 us -> 320 us
  local copies, waits for them, and re-layouts: 26.1 us -> 36.7 us
  starting transfers between devices: 35.6 us -> 41.6 us
    ppermute x4, waiting for transfers between devices: 33.7 us -> 0.01 us  [send_pieces(): lax.ppermute(pieces[d], 'tensor', shifted(ranks, d))]
    ppermute x5, waiting for transfers between devices: 0.9 us -> 28.7 us  [swap_sum(): lax.ppermute(value, axis, [(i, i ^ step) for i in range(ranks)])]
    ppermute x4 -> x6, waiting for transfers between devices: 24.6 us -> 0.02 us  [the longest x3 0.01 us: swap_pair(): return lax.ppermute(sent, 'dp', [(i, i ^ 1) for i in range(packs)])]
    pallas_call x0 -> x6, Pallas kernels: none -> 20.9 us  [the longest x3 12.2 us: merge_halves(): pl.pallas_call(merge_kernel, grid_spec=pltpu.PrefetchScalarGridSpec(num_s...]
    ppermute x3 -> x6, waiting for transfers between devices: 11.3 us -> 1.42 us  [far_gather(): came = lax.ppermute(value, 'dp', far_shift(packs, far, d))]
    ppermute x5, starting transfers between devices: 10.3 us -> 3.82 us  [swap_sum(): lax.ppermute(value, axis, [(i, i ^ step) for i in range(ranks)])]
    select_n x2 -> x4, other arithmetic: 6.5 us -> 11.4 us  [double(): jnp.where(bit == 0, jnp.concatenate([value, other], axis=0), jnp.concaten...]
    unnamed x65 -> x51, local copies, waits for them, and re-layouts: 9.2 us -> 12.3 us
  transfers between devices with their start and end apart: 25 -> 33, of which waited for: 11 -> 6; matrix products, arithmetic and copies ran while one was open for 14% -> 20% of each run, Pallas kernels for 46% -> 48%
where the time goes in v3:
time: 545 us; the launch traced here: 538 us
  Pallas kernels  320 us (59%)
  other arithmetic  81.1 us (15%)
  waiting for transfers between devices  44.3 us (8%)
  starting transfers between devices  41.6 us (8%)
  local copies, waits for them, and re-layouts  36.7 us (7%)
  between operations  14.7 us (3%)
    pallas_call x2, Pallas kernels, feedforward(): pl.pallas_call(functools.partial(feedforward_kernel, ranks, part, parts),...  120 us
    pallas_call x1, Pallas kernels, attn_bwd(): pl.pallas_call(bwd_kernel, grid_spec=pltpu.PrefetchScalarGridSpec(num_sca...  63.3 us
    pallas_call x1, Pallas kernels, attn_fwd(): pl.pallas_call(fwd_kernel, grid_spec=pltpu.PrefetchScalarGridSpec(num_sca...  44.1 us
    pallas_call x3, Pallas kernels, input_backward(): pl.pallas_call(functools.partial(input_kernel, ranks, len(grads) // 3), g...  32.2 us
    ppermute x5, waiting for transfers between devices, swap_sum(): lax.ppermute(value, axis, [(i, i ^ step) for i in range(ranks)])  28.7 us
    pallas_call x1, Pallas kernels, project(): pl.pallas_call(project_kernel, grid=(length // T,), in_specs=[tokens(T, w...  20.3 us
    pallas_call x2, Pallas kernels, weights_backward(): pl.pallas_call(weights_kernel, grid=(length // rows,), in_specs=[across(w...  18.7 us
    unnamed x51, local copies, waits for them, and re-layouts  12.3 us
  transfers between devices with their start and end apart: 33, of which 6 were waited for; matrix products, arithmetic and copies ran while one was open for 20% of the time, Pallas kernels for 48%

profile of v3, /device:TPU:0, one launch (start us, length us, event | category | flops | bytes accessed | tf_op | source)
XLA Modules:
  0.0 538.2 jit_solution(13871555622323868650)
XLA Ops:
  7.2 3.0 collective-permute-start
  15.3 4.6 copy.30
  20.0 4.7 copy.31.w_ref
  27.2 20.3 %project_qkv.1 = (bf16[3072,512]{1,0:T(8,128)(2,1)}, bf16[3072,512]{1,0:T(8,128)(2,1)}, bf16[3072,512]{1,0:T(8,128)(2,1)}, bf16[1024,3072]{1,0:T(8,128)(2,1)}, b...) custom-call(bf16[3072,1024]{1,0:T(8,128)(2,1)} %x_ref.7, f32[1,1024]{1,0:T(1,128)} %bitcast.64, f32[1,1024]{1,0:T(1,128)} %bitcast.77, ...), custom_call_target="tpu_custom_call" | custom-call | flops 1 | bytes 1 | tf_op jit(solution)/shard_map/project_qkv/pallas_call | solution.py:273
  48.4 44.1 %attention_forward.1 = (bf16[3072,512]{1,0:T(8,128)(2,1)}, f32[8,12,256]{2,1,0:T(8,128)}) custom-call(s32[12]{0:T(128)} %and_select_fusion.lo_ref, s32[12,256]{1,0:T(8,128)} %copy-done.9, bf16[3072,512]{1,0:T(8,128)(2,1)} %get-tuple-element.74.q_ref, bf16[3072,512]{1,0:T(8,128)(2,1)} %get-tuple-element.75.k_ref, bf16[3072,512]{1,0:T(8,128)(2,1)} %get-tuple-element.76.v_ref), custom_call_target="tpu_custom_call" | custom-call | flops 1 | bytes 1 | tf_op jit(solution)/shard_map/attention_forward/pallas_call | solution.py:111
  94.7 62.1 %feedforward_both_ways.2 = (f32[3072,1024]{1,0:T(8,128)}, f32[3072,1024]{1,0:T(8,128)}, bf16[1024,1024]{1,0:T(8,128)(2,1)}, bf16[1024,1024]{1,0:T(8,128)(2,1)}, ...) custom-call(s32[1]{0:T(128)} %bitcast.me_ref, ...), custom_call_target="tpu_custom_call" | custom-call | flops 1 | bytes 1 | tf_op jit(solution)/shard_map/feedforward_both_ways/pallas_call | solution.py:439
  157.5 58.1 %feedforward_both_ways.3 = (f32[3072,512]{1,0:T(8,128)}, bf16[3072,512]{1,0:T(8,128)(2,1)}, bf16[3072,1024]{1,0:T(8,128)(2,1)}, f32[8,1024]{1,0:T(8,128)}, f32[8...) custom-call(s32[1]{0:T(128)} %bitcast.me_ref, bf16[3072,1024]{1,0:T(8,128)(2,1)} %get-tuple-element.72.n2_ref, ...), custom_call_target="tpu_custom_call" | custom-call | flops 1 | bytes 1 | tf_op jit(solution)/shard_map/feedforward_both_ways/pallas_call | solution.py:439
  215.6 3.3 pick_half.3
  218.9 63.3 %attention_backward.1 = (bf16[3072,512]{1,0:T(8,128)(2,1)}, bf16[3072,512]{1,0:T(8,128)(2,1)}, bf16[3072,512]{1,0:T(8,128)(2,1)}) custom-call(s32[12]{0:T(128)} %and_select_fusion.lo_ref, s32[12,256]{1,0:T(8,128)} %copy-done.9, bf16[3072,512]{1,0:T(8,128)(2,1)} %get-tuple-element.74.q_ref, bf16[3072,512]{1,0:T(8,128)(2,1)} %get-tuple-element.75.k_ref, ...), custom_call_target="tpu_custom_call" | custom-call | flops 1 | bytes 1 | tf_op jit(solution)/shard_map/attention_backward/pallas_call | solution.py:207
  282.3 1.9 all-reduce.3.cloned.1.call-done
  285.5 5.5 %merge_halves.3 = (bf16[512,1024]{1,0:T(8,128)(2,1)}, f32[512,1024]{1,0:T(8,128)}) custom-call(s32[2]{0:T(128)} %pad_add_fusion.bits_ref, bf16[2048,1024]{1,0:T(8,128)(2,1)} %bitcast.56, bf16[1024,1024]{1,0:T(8,128)(2,1)} %copy-done.5), custom_call_target="tpu_custom_call" | custom-call | flops 1 | bytes 1 | tf_op jit(solution)/shard_map/merge_halves/pallas_call | solution.py:620
  291.0 5.4 collective-permute-start.4
  296.4 10.7 %input_backward.3 = (f32[1024,512]{1,0:T(8,128)}, bf16[1024,512]{1,0:T(8,128)(2,1)}, f32[8,1024]{1,0:T(8,128)}, f32[8,1024]{1,0:T(8,128)}) custom-call(s32[1]{0:T(128)} %bitcast.me_ref, bf16[3072,1024]{1,0:T(8,128)(2,1)} %x_ref.7, f32[1,1024]{1,0:T(1,128)} %bitcast.65, f32[1,1024]{1,0:T(1,128)} %bitcast.69, bf16[1024,1536]{1,0:T(8,128)(2,1)} %copy.31.w_ref, ...), custom_call_target="tpu_custom_call" | custom-call | flops 1 | bytes 1 | tf_op jit(solution)/shard_map/input_backward/pallas_call | solution.py:534
  307.1 2.2 collective-permute-start.3
  309.2 9.1 %qkv_weights_backward.2 = (bf16[3,1024,256]{2,1,0:T(8,128)(2,1)}, f32[3,8,256]{2,1,0:T(8,128)}) custom-call(bf16[1024,3072]{1,0:T(8,128)(2,1)} %get-tuple-element.104.n1t_ref, bf16[3072,512]{1,0:T(8,128)(2,1)} %get-tuple-element.87.refs_0_.dq_ref, bf16[3072,512]{1,0:T(8,128)(2,1)} %get-tuple-element.94.refs_1_.dk_ref, ...), custom_call_target="tpu_custom_call" | custom-call | flops 1 | bytes 1 | tf_op jit(solution)/shard_map/qkv_weights_backward/pallas_call | solution.py:489
  318.4 1.9 convert_add_fusion.2
  320.3 2.6 pick_half.4
  323.8 4.8 collective-permute-start.11
  328.6 2.0 collective-permute-start.10
  331.5 3.4 merge_halves.4
  334.9 9.5 %qkv_weights_backward.3 = (bf16[3,1024,256]{2,1,0:T(8,128)(2,1)}, f32[3,8,256]{2,1,0:T(8,128)}) custom-call(bf16[1024,3072]{1,0:T(8,128)(2,1)} %get-tuple-element.104.n1t_ref, bf16[3072,512]{1,0:T(8,128)(2,1)} %get-tuple-element.87.refs_0_.dq_ref, bf16[3072,512]{1,0:T(8,128)(2,1)} %get-tuple-element.94.refs_1_.dk_ref, ...), custom_call_target="tpu_custom_call" | custom-call | flops 1 | bytes 1 | tf_op jit(solution)/shard_map/qkv_weights_backward/pallas_call | solution.py:489
  344.5 2.8 pick_half.5
  348.5 3.8 collective-permute-done.11
  353.4 2.3 constant_dynamic-update-slice_fusion.3
  355.7 2.1 collective-permute-start.8
  364.3 2.8 convert_element_type.152
  370.6 3.8 collective-permute-start.29
  374.4 3.4 merge_halves.5
  377.8 1.7 constant_dynamic-update-slice_fusion.2
  381.9 10.7 %input_backward.4 = (f32[1024,512]{1,0:T(8,128)}, bf16[1024,512]{1,0:T(8,128)(2,1)}, f32[8,1024]{1,0:T(8,128)}, f32[8,1024]{1,0:T(8,128)}) custom-call(s32[1]{0:T(128)} %bitcast.me_ref, bf16[3072,1024]{1,0:T(8,128)(2,1)} %x_ref.7, f32[1,1024]{1,0:T(1,128)} %bitcast.66, f32[1,1024]{1,0:T(1,128)} %bitcast.70, bf16[1024,1536]{1,0:T(8,128)(2,1)} %copy.31.w_ref, ...), custom_call_target="tpu_custom_call" | custom-call | flops 1 | bytes 1 | tf_op jit(solution)/shard_map/input_backward/pallas_call | solution.py:534
  400.1 2.0 collective-permute-start.14
  404.8 10.8 %input_backward.5 = (f32[1024,512]{1,0:T(8,128)}, bf16[1024,512]{1,0:T(8,128)(2,1)}, f32[8,1024]{1,0:T(8,128)}, f32[8,1024]{1,0:T(8,128)}) custom-call(s32[1]{0:T(128)} %bitcast.me_ref, bf16[3072,1024]{1,0:T(8,128)(2,1)} %x_ref.7, f32[1,1024]{1,0:T(1,128)} %bitcast.67, f32[1,1024]{1,0:T(1,128)} %bitcast.71, bf16[1024,1536]{1,0:T(8,128)(2,1)} %copy.31.w_ref, ...), custom_call_target="tpu_custom_call" | custom-call | flops 1 | bytes 1 | tf_op jit(solution)/shard_map/input_backward/pallas_call | solution.py:534
  424.5 2.0 collective-permute-start.30
  426.6 7.9 %add_convert_fusion = bf16[3072,512]{1,0:T(8,128)(2,1)} fusion(f32[3072,512]{1,0:T(8,128)} %get-tuple-element.80, bf16[3072,512]{1,0:T(8,128)(2,1)} %collective-permute-done.1, f32[512]{0:T(512)S(1)} %copy-done.15, f32[512]{0:T(512)S(1)} %copy-done.16, bf16[3072,1024]{1,0:T(8,128)(2,1)} %x_ref.7, s32[]{:T(128)S(6)} %select_n.144), kind=kLoop, calls=%fused_computation.3 | loop fusion | flops 11010048 | bytes 15732740 | tf_op jit(solution)/shard_map/convert_element_type | solution.py:702
  434.5 16.7 %collective-permute-done.18 = f32[64,128]{1,0:T(8,128)S(1)} collective-permute-done((f32[64,128]{1,0:T(8,128)S(1)}, f32[64,128]{1,0:T(8,128)S(1)}, u32[]{:S(2)}, u32[]{:S(2)}) %collective-permute-start.18) | collective-permute-done | bytes 32800 | tf_op jit(solution)/shard_map/ppermute | solution.py:578
  451.3 4.0 maximum_select_fusion.2
  455.8 2.0 collective-permute-start.22
  458.7 2.0 collective-permute-start.20
  462.4 12.0 %collective-permute-done.20 = f32[64,128]{1,0:T(8,128)S(1)} collective-permute-done((f32[64,128]{1,0:T(8,128)S(1)}, f32[64,128]{1,0:T(8,128)S(1)}, u32[]{:S(2)}, u32[]{:S(2)}) %collective-permute-start.20) | collective-permute-done | bytes 32800 | tf_op jit(solution)/shard_map/ppermute | solution.py:578
  490.3 1.8 collective-permute-start.25
  492.1 5.0 convert_add_fusion.3
  497.1 3.4 pad_maximum_fusion
  500.5 8.4 %collective-permute-done.25 = bf16[768,512]{1,0:T(8,128)(2,1)S(1)} collective-permute-done((bf16[768,512]{1,0:T(8,128)(2,1)}, bf16[768,512]{1,0:T(8,128)(2,1)S(1)}, u32[]{:S(2)}, u32[]{:S(2)}) %collective-permute-start.25) | collective-permute-done | bytes 786464 | tf_op jit(solution)/shard_map/ppermute | solution.py:642
  508.9 1.9 maximum_select_fusion.3
  510.8 4.6 maximum_select_fusion
  517.0 4.4 maximum_convert_fusion
  521.4 4.5 maximum_convert_fusion.1
  526.9 3.6 convert_bitcast_fusion
  (170 shorter events, 70.7 us)
Async XLA Ops:
  7.2 277.0 %all-reduce.3.cloned.1.call-start = ((), (), s32[]{:S(2)}) async-start(), calls=%async_computation | async-start | bytes 10485760 | tf_op jit(solution)/shard_map/psum | solution.py:694
  7.2 85.8 %collective-permute-start = (bf16[3072,512]{1,0:T(8,128)(2,1)}, bf16[3072,512]{1,0:T(8,128)(2,1)S(1)}, u32[]{:S(2)}, u32[]{:S(2)}) collective-permute-start(bf16[3072,512]{1,0:T(8,128)(2,1)} %refs_0_.3), channel_id=1, source_target_pairs={{0,1},{1,0},{2,3},{3,2},{4,5},{5,4},{6,7},{7,6},{8,9},{9,8},{10,11... | collective-permute-start | bytes 9437192 | tf_op jit(solution)/shard_map/ppermute | solution.py:679
  20.0 4.7 copy-start.17
  20.0 5.3 copy-start.11
  48.4 44.1 %copy-start.18 = (bf16[2048]{0:T(1024)(128)(2,1)S(1)}, bf16[2048]{0:T(1024)(128)(2,1)}, u32[]{:S(2)}) copy-start(bf16[2048]{0:T(1024)(128)(2,1)} %param.27) | copy-start | bytes 12292
  93.1 1.6 copy-start.1
  218.9 65.3 %collective-permute-start.2 = (bf16[1024,1024]{1,0:T(8,128)(2,1)}, bf16[1024,1024]{1,0:T(8,128)(2,1)S(1)}, u32[]{:S(2)}, u32[]{:S(2)}) collective-permute-start(bf16[1024,1024]{1,0:T(8,128)(2,1)} %pick_half.3), channel_id=1, source_target_pairs={{0,2},{2,0},{4,6},{6,4},{8,10},{10,8},{12,14},{14,12},{16,18},{18,... | collective-permute-start | bytes 6291464 | tf_op jit(solution)/shard_map/ppermute | solution.py:614
  218.9 101.4 %collective-permute-start.1 = (bf16[3072,512]{1,0:T(8,128)(2,1)}, bf16[3072,512]{1,0:T(8,128)(2,1)}, u32[]{:S(2)}, u32[]{:S(2)}) collective-permute-start(bf16[3072,512]{1,0:T(8,128)(2,1)} %get-tuple-element.81), channel_id=1, source_target_pairs={{0,1},{1,0},{2,3},{3,2},{4,5},{5,4},{6,7},{7,6},{8,9},{9,8},{10,11... | collective-permute-start | bytes 9437192 | tf_op jit(solution)/shard_map/ppermute | solution.py:571
  291.0 27.4 %collective-permute-start.4 = (bf16[512,1024]{1,0:T(8,128)(2,1)}, bf16[512,1024]{1,0:T(8,128)(2,1)S(1)}, u32[]{:S(2)}, u32[]{:S(2)}) collective-permute-start(bf16[512,1024]{1,0:T(8,128)(2,1)} %get-tuple-element.101), channel_id=1, source_target_pairs={{0,4},{2,6},{4,0},{6,2},{8,12},{10,14},{12,8},{14,10},{16,20},{18,... | collective-permute-start | bytes 3145736 | tf_op jit(solution)/shard_map/ppermute | solution.py:637
  307.1 37.4 %collective-permute-start.3 = (bf16[1024,512]{1,0:T(8,128)(2,1)}, bf16[1024,512]{1,0:T(8,128)(2,1)}, u32[]{:S(2)}, u32[]{:S(2)}) collective-permute-start(bf16[1024,512]{1,0:T(8,128)(2,1)} %get-tuple-element.97), channel_id=1, source_target_pairs={{0,1},{1,0},{2,3},{3,2},{4,5},{5,4},{6,7},{7,6},{8,9},{9,8},{10,11... | collective-permute-start | bytes 3145736 | tf_op jit(solution)/shard_map/ppermute | solution.py:571
  320.3 14.7 %copy-start.4 = (f32[512,1024]{1,0:T(8,128)}, f32[512,1024]{1,0:T(8,128)S(1)}, u32[]{:S(2)}) copy-start(f32[512,1024]{1,0:T(8,128)S(1)} %convert_add_fusion.2) | copy-start | bytes 6291460
  322.9 7.8 %collective-permute-start.5 = (bf16[1536,256]{1,0:T(8,128)(2,1)}, bf16[1536,256]{1,0:T(8,128)(2,1)S(1)}, u32[]{:S(2)}, u32[]{:S(2)}) collective-permute-start(bf16[1536,256]{1,0:T(8,128)(2,1)} %pick_half.4), channel_id=1, source_target_pairs={{0,2},{2,0},{4,6},{6,4},{8,10},{10,8},{12,14},{14,12},{16,18},{18,... | collective-permute-start | bytes 2359304 | tf_op jit(solution)/shard_map/ppermute | solution.py:614
  323.8 24.7 %collective-permute-start.12 = (bf16[128,1024]{1,0:T(8,128)(2,1)}, bf16[128,1024]{1,0:T(8,128)(2,1)}, u32[]{:S(2)}, u32[]{:S(2)}) collective-permute-start(bf16[128,1024]{1,0:T(8,128)(2,1)} %get-tuple-element.141), channel_id=1, source_target_pairs={{0,24},{2,26},{4,28},{6,30},{8,0},{10,2},{12,4},{14,6},{16,8},{18,... | collective-permute-start | bytes 786440 | tf_op jit(solution)/shard_map/ppermute | solution.py:657
  323.8 28.4 %collective-permute-start.11 = (bf16[128,1024]{1,0:T(8,128)(2,1)}, bf16[128,1024]{1,0:T(8,128)(2,1)}, u32[]{:S(2)}, u32[]{:S(2)}) collective-permute-start(bf16[128,1024]{1,0:T(8,128)(2,1)} %get-tuple-element.142), channel_id=1, source_target_pairs={{0,16},{2,18},{4,20},{6,22},{8,24},{10,26},{12,28},{14,30},{16,0},... | collective-permute-start | bytes 786440 | tf_op jit(solution)/shard_map/ppermute | solution.py:657
  328.6 23.6 %collective-permute-start.10 = (bf16[128,1024]{1,0:T(8,128)(2,1)S(1)}, bf16[128,1024]{1,0:T(8,128)(2,1)}, u32[]{:S(2)}, u32[]{:S(2)}) collective-permute-start(bf16[128,1024]{1,0:T(8,128)(2,1)S(1)} %get-tuple-element.140), channel_id=1, source_target_pairs={{0,8},{2,10},{4,12},{6,14},{8,16},{10,18},{12,20},{14,22},{16,24},... | collective-permute-start | bytes 786440 | tf_op jit(solution)/shard_map/ppermute | solution.py:657
  334.9 12.4 %copy-start.19 = (bf16[512]{0:T(512)(128)(2,1)S(1)}, bf16[512]{0:T(512)(128)(2,1)}, u32[]{:S(2)}) copy-start(bf16[512]{0:T(512)(128)(2,1)} %param.29) | copy-start | bytes 3076
  334.9 13.0 %copy-start.20 = (bf16[512]{0:T(512)(128)(2,1)S(1)}, bf16[512]{0:T(512)(128)(2,1)}, u32[]{:S(2)}) copy-start(bf16[512]{0:T(512)(128)(2,1)} %param.25) | copy-start | bytes 3076
  344.5 13.3 %copy-start = (bf16[3072,512]{1,0:T(8,128)(2,1)S(1)}, bf16[3072,512]{1,0:T(8,128)(2,1)}, u32[]{:S(2)}) copy-start(bf16[3072,512]{1,0:T(8,128)(2,1)} %refs_0_.3) | copy-start | bytes 9437188
  347.3 27.0 %collective-permute-start.6 = (bf16[1536,256]{1,0:T(8,128)(2,1)}, bf16[1536,256]{1,0:T(8,128)(2,1)}, u32[]{:S(2)}, u32[]{:S(2)}) collective-permute-start(bf16[1536,256]{1,0:T(8,128)(2,1)} %pick_half.5), channel_id=1, source_target_pairs={{0,2},{2,0},{4,6},{6,4},{8,10},{10,8},{12,14},{14,12},{16,18},{18,... | collective-permute-start | bytes 2359304 | tf_op jit(solution)/shard_map/ppermute | solution.py:614
  355.7 22.1 %collective-permute-start.27 = (bf16[128,1024]{1,0:T(8,128)(2,1)}, bf16[128,1024]{1,0:T(8,128)(2,1)}, u32[]{:S(2)}, u32[]{:S(2)}) collective-permute-start(bf16[128,1024]{1,0:T(8,128)(2,1)} %get-tuple-element.134), channel_id=1, source_target_pairs={{0,8},{2,10},{4,12},{6,14},{8,16},{10,18},{12,20},{14,22},{16,24},... | collective-permute-start | bytes 786440 | tf_op jit(solution)/shard_map/ppermute | solution.py:668
  355.7 23.7 %collective-permute-start.28 = (bf16[128,1024]{1,0:T(8,128)(2,1)}, bf16[128,1024]{1,0:T(8,128)(2,1)}, u32[]{:S(2)}, u32[]{:S(2)}) collective-permute-start(bf16[128,1024]{1,0:T(8,128)(2,1)} %get-tuple-element.134), channel_id=1, source_target_pairs={{0,16},{2,18},{4,20},{6,22},{8,24},{10,26},{12,28},{14,30},{16,0},... | collective-permute-start | bytes 786440 | tf_op jit(solution)/shard_map/ppermute | solution.py:668
  355.7 38.5 %collective-permute-start.8 = (bf16[768,256]{1,0:T(8,128)(2,1)}, bf16[768,256]{1,0:T(8,128)(2,1)S(1)}, u32[]{:S(2)}, u32[]{:S(2)}) collective-permute-start(bf16[768,256]{1,0:T(8,128)(2,1)} %get-tuple-element.111), channel_id=1, source_target_pairs={{0,4},{2,6},{4,0},{6,2},{8,12},{10,14},{12,8},{14,10},{16,20},{18,... | collective-permute-start | bytes 1179656 | tf_op jit(solution)/shard_map/ppermute | solution.py:637
  370.6 52.2 %collective-permute-start.29 = (bf16[128,1024]{1,0:T(8,128)(2,1)}, bf16[128,1024]{1,0:T(8,128)(2,1)}, u32[]{:S(2)}, u32[]{:S(2)}) collective-permute-start(bf16[128,1024]{1,0:T(8,128)(2,1)} %get-tuple-element.134), channel_id=1, source_target_pairs={{0,24},{2,26},{4,28},{6,30},{8,0},{10,2},{12,4},{14,6},{16,8},{18,... | collective-permute-start | bytes 786440 | tf_op jit(solution)/shard_map/ppermute | solution.py:668
  377.8 17.7 %collective-permute-start.9 = (bf16[768,256]{1,0:T(8,128)(2,1)}, bf16[768,256]{1,0:T(8,128)(2,1)}, u32[]{:S(2)}, u32[]{:S(2)}) collective-permute-start(bf16[768,256]{1,0:T(8,128)(2,1)} %get-tuple-element.112), channel_id=1, source_target_pairs={{0,4},{2,6},{4,0},{6,2},{8,12},{10,14},{12,8},{14,10},{16,20},{18,... | collective-permute-start | bytes 1179656 | tf_op jit(solution)/shard_map/ppermute | solution.py:637
  392.6 27.9 %collective-permute-start.7 = (bf16[1024,512]{1,0:T(8,128)(2,1)}, bf16[1024,512]{1,0:T(8,128)(2,1)}, u32[]{:S(2)}, u32[]{:S(2)}) collective-permute-start(bf16[1024,512]{1,0:T(8,128)(2,1)} %get-tuple-element.110), channel_id=1, source_target_pairs={{0,1},{1,0},{2,3},{3,2},{4,5},{5,4},{6,7},{7,6},{8,9},{9,8},{10,11... | collective-permute-start | bytes 3145736 | tf_op jit(solution)/shard_map/ppermute | solution.py:571
  395.4 1.6 copy-start.2
  398.1 21.1 %collective-permute-start.16 = (bf16[192,512]{1,0:T(8,128)(2,1)}, bf16[192,512]{1,0:T(8,128)(2,1)S(1)}, u32[]{:S(2)}, u32[]{:S(2)}) collective-permute-start(bf16[192,512]{1,0:T(8,128)(2,1)} %get-tuple-element.145), channel_id=1, source_target_pairs={{0,24},{2,26},{4,28},{6,30},{8,0},{10,2},{12,4},{14,6},{16,8},{18,... | collective-permute-start | bytes 589832 | tf_op jit(solution)/shard_map/ppermute | solution.py:657
  398.6 20.5 %collective-permute-start.15 = (bf16[192,512]{1,0:T(8,128)(2,1)}, bf16[192,512]{1,0:T(8,128)(2,1)}, u32[]{:S(2)}, u32[]{:S(2)}) collective-permute-start(bf16[192,512]{1,0:T(8,128)(2,1)} %get-tuple-element.144), channel_id=1, source_target_pairs={{0,16},{2,18},{4,20},{6,22},{8,24},{10,26},{12,28},{14,30},{16,0},... | collective-permute-start | bytes 589832 | tf_op jit(solution)/shard_map/ppermute | solution.py:657
  400.1 19.0 %collective-permute-start.14 = (bf16[192,512]{1,0:T(8,128)(2,1)S(1)}, bf16[192,512]{1,0:T(8,128)(2,1)}, u32[]{:S(2)}, u32[]{:S(2)}) collective-permute-start(bf16[192,512]{1,0:T(8,128)(2,1)S(1)} %get-tuple-element.143), channel_id=1, source_target_pairs={{0,8},{2,10},{4,12},{6,14},{8,16},{10,18},{12,20},{14,22},{16,24},... | collective-permute-start | bytes 589832 | tf_op jit(solution)/shard_map/ppermute | solution.py:657
  404.8 17.8 %copy-start.13 = (f32[1024]{0:T(1024)S(1)}, f32[1024]{0:T(1024)}, u32[]{:S(2)}) copy-start(f32[1024]{0:T(1024)} %reduce_sum.128) | copy-start | bytes 12292
  404.8 17.8 %copy-start.12 = (f32[1024]{0:T(1024)S(1)}, f32[1024]{0:T(1024)}, u32[]{:S(2)}) copy-start(f32[1024]{0:T(1024)} %reduce_sum.129) | copy-start | bytes 12292
  418.4 8.2 %copy-start.15 = (f32[512]{0:T(512)S(1)}, f32[512]{0:T(512)}, u32[]{:S(2)}) copy-start(f32[512]{0:T(512)} %convert_element_type.125) | copy-start | bytes 6148
  418.4 8.2 %copy-start.16 = (f32[512]{0:T(512)S(1)}, f32[512]{0:T(512)}, u32[]{:S(2)}) copy-start(f32[512]{0:T(512)} %convert_element_type.124) | copy-start | bytes 6148
  422.7 3.8 collective-permute-start.17
  424.5 26.8 %collective-permute-start.30 = (bf16[512,1024]{1,0:T(8,128)(2,1)}, bf16[512,1024]{1,0:T(8,128)(2,1)S(1)}, u32[]{:S(2)}, u32[]{:S(2)}) collective-permute-start(bf16[512,1024]{1,0:T(8,128)(2,1)} %constant_dynamic-update-slice_fusion), channel_id=1, source_target_pairs={{0,4},{2,6},{4,0},{6,2},{8,12},{10,14},{12,8},{14,10},{16,20},{18,... | collective-permute-start | bytes 3145736 | tf_op jit(solution)/shard_map/ppermute | solution.py:642
  426.5 24.7 %collective-permute-start.18 = (f32[64,128]{1,0:T(8,128)S(1)}, f32[64,128]{1,0:T(8,128)S(1)}, u32[]{:S(2)}, u32[]{:S(2)}) collective-permute-start(f32[64,128]{1,0:T(8,128)S(1)} %bitcast_add_fusion), channel_id=1, source_target_pairs={{0,4},{2,6},{4,0},{6,2},{8,12},{10,14},{12,8},{14,10},{16,20},{18,... | collective-permute-start | bytes 98312 | tf_op jit(solution)/shard_map/ppermute | solution.py:578
  451.2 7.5 %collective-permute-start.19 = (f32[64,128]{1,0:T(8,128)S(1)}, f32[64,128]{1,0:T(8,128)S(1)}, u32[]{:S(2)}, u32[]{:S(2)}) collective-permute-start(f32[64,128]{1,0:T(8,128)S(1)} %fusion.15), channel_id=1, source_target_pairs={{0,8},{2,10},{4,12},{6,14},{8,0},{10,2},{12,4},{14,6},{16,24},{18,... | collective-permute-start | bytes 98312 | tf_op jit(solution)/shard_map/ppermute | solution.py:578
  455.3 55.5 %collective-permute-start.31 = (bf16[1024,1024]{1,0:T(8,128)(2,1)}, bf16[1024,1024]{1,0:T(8,128)(2,1)}, u32[]{:S(2)}, u32[]{:S(2)}) collective-permute-start(bf16[1024,1024]{1,0:T(8,128)(2,1)} %maximum_select_fusion.2), channel_id=1, source_target_pairs={{0,2},{2,0},{4,6},{6,4},{8,10},{10,8},{12,14},{14,12},{16,18},{18,... | collective-permute-start | bytes 6291464 | tf_op jit(solution)/shard_map/ppermute | solution.py:642
  455.3 36.8 %collective-permute-start.13 = (bf16[1024,512]{1,0:T(8,128)(2,1)}, bf16[1024,512]{1,0:T(8,128)(2,1)}, u32[]{:S(2)}, u32[]{:S(2)}) collective-permute-start(bf16[1024,512]{1,0:T(8,128)(2,1)} %get-tuple-element.115), channel_id=1, source_target_pairs={{0,1},{1,0},{2,3},{3,2},{4,5},{5,4},{6,7},{7,6},{8,9},{9,8},{10,11... | collective-permute-start | bytes 3145736 | tf_op jit(solution)/shard_map/ppermute | solution.py:571
  455.8 30.2 %collective-permute-start.22 = (bf16[192,512]{1,0:T(8,128)(2,1)S(1)}, bf16[192,512]{1,0:T(8,128)(2,1)}, u32[]{:S(2)}, u32[]{:S(2)}) collective-permute-start(bf16[192,512]{1,0:T(8,128)(2,1)S(1)} %fusion.6), channel_id=1, source_target_pairs={{0,8},{2,10},{4,12},{6,14},{8,16},{10,18},{12,20},{14,22},{16,24},... | collective-permute-start | bytes 589832 | tf_op jit(solution)/shard_map/ppermute | solution.py:668
  457.8 29.8 %collective-permute-start.23 = (bf16[192,512]{1,0:T(8,128)(2,1)S(1)}, bf16[192,512]{1,0:T(8,128)(2,1)S(1)}, u32[]{:S(2)}, u32[]{:S(2)}) collective-permute-start(bf16[192,512]{1,0:T(8,128)(2,1)S(1)} %fusion.6), channel_id=1, source_target_pairs={{0,16},{2,18},{4,20},{6,22},{8,24},{10,26},{12,28},{14,30},{16,0},... | collective-permute-start | bytes 589832 | tf_op jit(solution)/shard_map/ppermute | solution.py:668
  458.7 15.7 %collective-permute-start.20 = (f32[64,128]{1,0:T(8,128)S(1)}, f32[64,128]{1,0:T(8,128)S(1)}, u32[]{:S(2)}, u32[]{:S(2)}) collective-permute-start(f32[64,128]{1,0:T(8,128)S(1)} %add.232), channel_id=1, source_target_pairs={{0,16},{2,18},{4,20},{6,22},{8,24},{10,26},{12,28},{14,30},{16,0},... | collective-permute-start | bytes 98312 | tf_op jit(solution)/shard_map/ppermute | solution.py:578
  476.4 6.7 %collective-permute-start.21 = (f32[4,1024]{1,0:T(4,128)S(1)}, f32[4,1024]{1,0:T(4,128)}, u32[]{:S(2)}, u32[]{:S(2)}) collective-permute-start(f32[4,1024]{1,0:T(4,128)S(1)} %reshape.183), channel_id=1, source_target_pairs={{0,1},{1,0},{2,3},{3,2},{4,5},{5,4},{6,7},{7,6},{8,9},{9,8},{10,11... | collective-permute-start | bytes 49160 | tf_op jit(solution)/shard_map/ppermute | solution.py:578
  483.1 6.5 %collective-permute-start.24 = (bf16[192,512]{1,0:T(8,128)(2,1)S(1)}, bf16[192,512]{1,0:T(8,128)(2,1)S(1)}, u32[]{:S(2)}, u32[]{:S(2)}) collective-permute-start(bf16[192,512]{1,0:T(8,128)(2,1)S(1)} %fusion.6), channel_id=1, source_target_pairs={{0,24},{2,26},{4,28},{6,30},{8,0},{10,2},{12,4},{14,6},{16,8},{18,... | collective-permute-start | bytes 589832 | tf_op jit(solution)/shard_map/ppermute | solution.py:668
  490.3 18.5 %collective-permute-start.25 = (bf16[768,512]{1,0:T(8,128)(2,1)}, bf16[768,512]{1,0:T(8,128)(2,1)S(1)}, u32[]{:S(2)}, u32[]{:S(2)}) collective-permute-start(bf16[768,512]{1,0:T(8,128)(2,1)} %constant_dynamic-update-slice_fusion.4), channel_id=1, source_target_pairs={{0,4},{2,6},{4,0},{6,2},{8,12},{10,14},{12,8},{14,10},{16,20},{18,... | collective-permute-start | bytes 2359304 | tf_op jit(solution)/shard_map/ppermute | solution.py:642
  510.7 15.2 %collective-permute-start.26 = (bf16[1536,512]{1,0:T(8,128)(2,1)S(1)}, bf16[1536,512]{1,0:T(8,128)(2,1)S(1)}, u32[]{:S(2)}, u32[]{:S(2)}) collective-permute-start(bf16[1536,512]{1,0:T(8,128)(2,1)S(1)} %maximum_select_fusion.3), channel_id=1, source_target_pairs={{0,2},{2,0},{4,6},{6,4},{8,10},{10,8},{12,14},{14,12},{16,18},{18,... | collective-permute-start | bytes 4718600 | tf_op jit(solution)/shard_map/ppermute | solution.py:642
  517.0 4.4 copy-start.6
  526.9 3.6 copy-start.14
  (6 other events, 6.1 us)
Sparse Core Ops, SparseCore 0:
  156.9 127.2 all-reduce.2

commit v4 on v3

--- a/solution.py
+++ b/solution.py
@@ -691,16 +691,15 @@
     for part in range(parts):
         made.append(feedforward(part, parts, me, inputs, n2, n2t, w_fc1, row(b_fc1), w_fc2, w_dense, mixed, pieces, carried))
         carried = made[-1].get("carried")
-    early = lax.psum((made[0]["w1g"], made[0]["w2g"], made[0]["wdg"]), "dp")
     place = lax.axis_index("dp").astype(jnp.int32)
     bits = jnp.stack([place % 2, (place // 2) % 2])
-    late = [m["both"].reshape(2 * width, width) for m in made[1:]]
-    picked = [pick_half(bits, v) for v in late]
-    swapped = [swap_pair(v, packs) for v in picked]
+    both = [m["both"].reshape(2 * width, width) for m in made[1:]]
+    early = lax.psum((made[0]["w1g"], made[0]["w2g"], made[0]["wdg"], *both), "dp")
+    late = early[3:]
     own = lax.dynamic_slice_in_dim(inputs, me[0] * local, local, 1).astype(F32)
     total, out_came = send_pieces(made[-1]["outs"])
     outputs = (total + own + b_dense.astype(F32) + b_fc2.astype(F32)).astype(BF)
-    mixed_grad = tie(made[0]["mixed_grad"], made[-1]["n2g"], *picked)
+    mixed_grad = tie(made[0]["mixed_grad"], made[-1]["n2g"])
     grads = attn_bwd(min(GB * PAIR, local), 0, lowest, starts, query, key, value, mixed, mixed_grad, totals, cosine, sine)
     group = min(2 * PAIR, local)
     groups = local // group
@@ -716,32 +715,27 @@
         norms.append(jnp.stack([jnp.sum(v, axis=0) for v in got[ranks:]]))
         return got[0]
 
-    late = [merge_halves(bits, tie(v, grads[0], *early), s) for v, s in zip(late, swapped)]
-    normed2_grad = tie(made[-1]["n2g"], grads[0], *early, *[v[1] for v in late])
-    late = [cross_sum(*v, packs) for v in late]
+    normed2_grad = tie(made[-1]["n2g"], grads[0])
     done = chunk(0, normed2_grad)
     n1t = tie(n1t, done)
     for c in range(groups):
         wg, bg = weights_backward(c, group, n1t, *grads)
-        wg = tie(wg, *out_came, *late) if c == 0 else tie(wg, *arrived[0])
+        wg = tie(wg, *out_came) if c == 0 else tie(wg, *arrived[0])
         wg = wg.reshape(3 * width, group)
         halves = merge_halves(bits, wg, swap_pair(pick_half(bits, wg), packs))
         n1t = tie(n1t, halves[1])
-        if c == 0:
-            late = [far_sum(v, packs, 4).astype(BF) for v in late]
         biases.append(jnp.sum(bg, axis=1))
         weights.append(cross_sum(*halves, packs))
     normed2_grad = tie(normed2_grad, halves[1], *arrived[0])
     for c in range(1, count):
         done = chunk(c, normed2_grad)
         if c == 1:
-            normed2_grad = tie(normed2_grad, done, *weights, *late)
-    late = [far_gather(v, packs, 4) for v in late]
+            normed2_grad = tie(normed2_grad, done, *weights)
     wg = far_sum(jnp.concatenate(weights, axis=1), packs, 4).astype(BF)
     ready = lax.optimization_barrier((done, wg, norms[-1], *[p for came in arrived[:2] for p in came]))
     wg, norms[-1] = ready[1], ready[2]
     wg = far_gather(wg, packs, 4)
-    late = [double(double(v, packs, 2), packs, 1) for v in late]
+    norms[-1] = tie(norms[-1], *[p for came in arrived for p in came])
     input_grad = jnp.concatenate(input_grad, axis=0)
     wg = double(double(wg, packs, 2), packs, 1).astype(F32)
     qkv_weight_grad = wg.reshape(3, width, local).transpose(1, 0, 2)

time: 545 us -> 527 us (0.967)
  waiting for transfers between devices: 44.3 us -> 75.6 us
  other arithmetic: 81.1 us -> 63.7 us
  local copies, waits for them, and re-layouts: 36.7 us -> 22.3 us
  Pallas kernels: 320 us -> 309 us
  starting transfers between devices: 41.6 us -> 33.8 us
    psum x1, waiting for transfers between devices: 1.95 us -> 54 us  [on_device(): lax.psum((made[0]['w1g'], made[0]['w2g'], made[0]['wdg'], *both), 'dp')]
    ppermute x5, waiting for transfers between devices: 28.7 us -> 11.4 us  [swap_sum(): lax.ppermute(value, axis, [(i, i ^ step) for i in range(ranks)])]
    ppermute x4 -> x2, waiting for transfers between devices: 8.37 us -> 0.01 us  [double(): other = lax.ppermute(value, 'dp', [(i, i ^ step) for i in range(packs)])]
    dynamic_update_slice x6 -> x3, local copies, waits for them, and re-layouts: 8.02 us -> 0.05 us  [far_gather(): lax.dynamic_update_slice_in_dim(whole, came, (place + count - d) % count...]
    ppermute x6 -> x3, waiting for transfers between devices: 1.42 us -> 7.87 us  [far_gather(): came = lax.ppermute(value, 'dp', far_shift(packs, far, d))]
    select_n x4 -> x2, other arithmetic: 11.4 us -> 5.1 us  [double(): jnp.where(bit == 0, jnp.concatenate([value, other], axis=0), jnp.concaten...]
    ppermute x3 -> x2, starting transfers between devices: 7.47 us -> 2.02 us  [cross_sum(): lax.ppermute(sent, 'dp', [(i, i ^ 2) for i in range(packs)]).astype(F32)]
    pallas_call x3 -> x2, Pallas kernels: 12.2 us -> 6.82 us  [merge_halves(): pl.pallas_call(merge_kernel, grid_spec=pltpu.PrefetchScalarGridSpec(num_s...]
  transfers between devices with their start and end apart: 33 -> 23, of which waited for: 6 -> 5; matrix products, arithmetic and copies ran while one was open for 20% -> 15% of each run, Pallas kernels for 48% -> 36%
where the time goes in v4:
time: 527 us; the launch traced here: 519 us
  Pallas kernels  309 us (59%)
  waiting for transfers between devices  75.6 us (14%)
  other arithmetic  63.7 us (12%)
  starting transfers between devices  33.8 us (6%)
  local copies, waits for them, and re-layouts  22.3 us (4%)
  between operations  14.7 us (3%)
    pallas_call x2, Pallas kernels, feedforward(): pl.pallas_call(functools.partial(feedforward_kernel, ranks, part, parts),...  120 us
    pallas_call x1, Pallas kernels, attn_bwd(): pl.pallas_call(bwd_kernel, grid_spec=pltpu.PrefetchScalarGridSpec(num_sca...  62.1 us
    psum x1, waiting for transfers between devices, on_device(): lax.psum((made[0]['w1g'], made[0]['w2g'], made[0]['wdg'], *both), 'dp')  54 us
    pallas_call x1, Pallas kernels, attn_fwd(): pl.pallas_call(fwd_kernel, grid_spec=pltpu.PrefetchScalarGridSpec(num_sca...  43 us
    pallas_call x3, Pallas kernels, input_backward(): pl.pallas_call(functools.partial(input_kernel, ranks, len(grads) // 3), g...  32.1 us
    pallas_call x1, Pallas kernels, project(): pl.pallas_call(project_kernel, grid=(length // T,), in_specs=[tokens(T, w...  20.3 us
    pallas_call x2, Pallas kernels, weights_backward(): pl.pallas_call(weights_kernel, grid=(length // rows,), in_specs=[across(w...  18.6 us
    ppermute x5, waiting for transfers between devices, swap_sum(): lax.ppermute(value, axis, [(i, i ^ step) for i in range(ranks)])  11.4 us
  transfers between devices with their start and end apart: 23, of which 5 were waited for; matrix products, arithmetic and copies ran while one was open for 15% of the time, Pallas kernels for 36%

profile of v4, /device:TPU:0, one launch (start us, length us, event | category | flops | bytes accessed | tf_op | source)
XLA Modules:
  0.0 519.0 jit_solution(13214204867645161387)
XLA Ops:
  7.2 3.0 collective-permute-start
  11.6 4.6 copy.30
  16.3 4.7 copy.31.w_ref
  25.3 20.3 %project_qkv.1 = (bf16[3072,512]{1,0:T(8,128)(2,1)}, bf16[3072,512]{1,0:T(8,128)(2,1)}, bf16[3072,512]{1,0:T(8,128)(2,1)}, bf16[1024,3072]{1,0:T(8,128)(2,1)}, b...) custom-call(bf16[3072,1024]{1,0:T(8,128)(2,1)} %x_ref.7, f32[1,1024]{1,0:T(1,128)} %bitcast.63, f32[1,1024]{1,0:T(1,128)} %bitcast.76, ...), custom_call_target="tpu_custom_call" | custom-call | flops 1 | bytes 1 | tf_op jit(solution)/shard_map/project_qkv/pallas_call | solution.py:273
  46.5 43.0 %attention_forward.1 = (bf16[3072,512]{1,0:T(8,128)(2,1)}, f32[8,12,256]{2,1,0:T(8,128)}) custom-call(s32[12]{0:T(128)} %and_select_fusion.lo_ref, s32[12,256]{1,0:T(8,128)} %copy-done.10, bf16[3072,512]{1,0:T(8,128)(2,1)} %get-tuple-element.72.q_ref, bf16[3072,512]{1,0:T(8,128)(2,1)} %get-tuple-element.73.k_ref, bf16[3072,512]{1,0:T(8,128)(2,1)} %get-tuple-element.74.v_ref), custom_call_target="tpu_custom_call" | custom-call | flops 1 | bytes 1 | tf_op jit(solution)/shard_map/attention_forward/pallas_call | solution.py:111
  90.1 1.6 copy-done.1
  91.7 61.9 %feedforward_both_ways.2 = (f32[3072,1024]{1,0:T(8,128)}, f32[3072,1024]{1,0:T(8,128)}, bf16[1024,1024]{1,0:T(8,128)(2,1)}, bf16[1024,1024]{1,0:T(8,128)(2,1)}, ...) custom-call(s32[1]{0:T(128)} %bitcast.me_ref, ...), custom_call_target="tpu_custom_call" | custom-call | flops 1 | bytes 1 | tf_op jit(solution)/shard_map/feedforward_both_ways/pallas_call | solution.py:439
  153.6 58.2 %feedforward_both_ways.3 = (f32[3072,512]{1,0:T(8,128)}, bf16[3072,512]{1,0:T(8,128)(2,1)}, bf16[3072,1024]{1,0:T(8,128)(2,1)}, f32[8,1024]{1,0:T(8,128)}, f32[8...) custom-call(s32[1]{0:T(128)} %bitcast.me_ref, bf16[3072,1024]{1,0:T(8,128)(2,1)} %get-tuple-element.70.n2_ref, ...), custom_call_target="tpu_custom_call" | custom-call | flops 1 | bytes 1 | tf_op jit(solution)/shard_map/feedforward_both_ways/pallas_call | solution.py:439
  211.9 62.1 %attention_backward.1 = (bf16[3072,512]{1,0:T(8,128)(2,1)}, bf16[3072,512]{1,0:T(8,128)(2,1)}, bf16[3072,512]{1,0:T(8,128)(2,1)}) custom-call(s32[12]{0:T(128)} %and_select_fusion.lo_ref, s32[12,256]{1,0:T(8,128)} %copy-done.10, bf16[3072,512]{1,0:T(8,128)(2,1)} %get-tuple-element.72.q_ref, bf16[3072,512]{1,0:T(8,128)(2,1)} %get-tuple-element.73.k_ref, ...), custom_call_target="tpu_custom_call" | custom-call | flops 1 | bytes 1 | tf_op jit(solution)/shard_map/attention_backward/pallas_call | solution.py:207
  274.1 10.8 %input_backward.3 = (f32[1024,512]{1,0:T(8,128)}, bf16[1024,512]{1,0:T(8,128)(2,1)}, f32[8,1024]{1,0:T(8,128)}, f32[8,1024]{1,0:T(8,128)}) custom-call(s32[1]{0:T(128)} %bitcast.me_ref, bf16[3072,1024]{1,0:T(8,128)(2,1)} %x_ref.7, f32[1,1024]{1,0:T(1,128)} %bitcast.64, f32[1,1024]{1,0:T(1,128)} %bitcast.68, bf16[1024,1536]{1,0:T(8,128)(2,1)} %copy.31.w_ref, ...), custom_call_target="tpu_custom_call" | custom-call | flops 1 | bytes 1 | tf_op jit(solution)/shard_map/input_backward/pallas_call | solution.py:534
  284.8 2.1 collective-permute-start.2
  287.5 9.1 %qkv_weights_backward.2 = (bf16[3,1024,256]{2,1,0:T(8,128)(2,1)}, f32[3,8,256]{2,1,0:T(8,128)}) custom-call(bf16[1024,3072]{1,0:T(8,128)(2,1)} %get-tuple-element.95.n1t_ref, bf16[3072,512]{1,0:T(8,128)(2,1)} %get-tuple-element.84.refs_0_.dq_ref, bf16[3072,512]{1,0:T(8,128)(2,1)} %get-tuple-element.86.refs_1_.dk_ref, ...), custom_call_target="tpu_custom_call" | custom-call | flops 1 | bytes 1 | tf_op jit(solution)/shard_map/qkv_weights_backward/pallas_call | solution.py:489
  296.6 3.0 pick_half.2
  299.6 1.5 collective-permute-start.3
  301.1 2.3 collective-permute-done.3.came_ref
  303.4 3.4 merge_halves.2
  306.8 9.5 %qkv_weights_backward.3 = (bf16[3,1024,256]{2,1,0:T(8,128)(2,1)}, f32[3,8,256]{2,1,0:T(8,128)}) custom-call(bf16[1024,3072]{1,0:T(8,128)(2,1)} %get-tuple-element.95.n1t_ref, bf16[3072,512]{1,0:T(8,128)(2,1)} %get-tuple-element.84.refs_0_.dq_ref, bf16[3072,512]{1,0:T(8,128)(2,1)} %get-tuple-element.86.refs_1_.dk_ref, ...), custom_call_target="tpu_custom_call" | custom-call | flops 1 | bytes 1 | tf_op jit(solution)/shard_map/qkv_weights_backward/pallas_call | solution.py:489
  316.4 2.9 pick_half.3
  324.4 3.4 merge_halves.3
  327.8 2.0 collective-permute-start.7
  329.9 7.8 %add_convert_fusion = bf16[3072,512]{1,0:T(8,128)(2,1)} fusion(f32[3072,512]{1,0:T(8,128)} %get-tuple-element.78, bf16[3072,512]{1,0:T(8,128)(2,1)} %copy-done.5, f32[512]{0:T(512)S(1)} %convert_element_type.101, f32[512]{0:T(512)S(1)} %convert_element_type.100, bf16[3072,1024]{1,0:T(8,128)(2,1)} %x_ref.7, s32[]{:T(128)S(6)} %select_n.92), kind=kLoop, calls=%fused_computation.3 | loop fusion | flops 11010048 | bytes 15732740 | tf_op jit(solution)/shard_map/convert_element_type | solution.py:701
  338.5 2.4 convert_add_fusion.4
  340.9 10.7 %input_backward.4 = (f32[1024,512]{1,0:T(8,128)}, bf16[1024,512]{1,0:T(8,128)(2,1)}, f32[8,1024]{1,0:T(8,128)}, f32[8,1024]{1,0:T(8,128)}) custom-call(s32[1]{0:T(128)} %bitcast.me_ref, bf16[3072,1024]{1,0:T(8,128)(2,1)} %x_ref.7, f32[1,1024]{1,0:T(1,128)} %bitcast.65, f32[1,1024]{1,0:T(1,128)} %bitcast.69, bf16[1024,1536]{1,0:T(8,128)(2,1)} %copy.31.w_ref, ...), custom_call_target="tpu_custom_call" | custom-call | flops 1 | bytes 1 | tf_op jit(solution)/shard_map/input_backward/pallas_call | solution.py:534
  354.1 2.0 fusion.8
  356.1 4.1 collective-permute-start.10
  362.2 54.0 %all-reduce.3.cloned.1.call-done = (bf16[512,1024]{1,0:T(8,128)(2,1)}, bf16[2048,1024]{1,0:T(8,128)(2,1)}, bf16[1024,1024]{1,0:T(8,128)(2,1)}, bf16[1024,1024]{1,0:T(8,128)(2,1)}) async-done(((bf16[512,1024]{1,0:T(8,128)(2,1)}, bf16[2048,1024]{1,0:T(8,128)(2,1)}, bf16[1024,1024]{1,0:T(8,128)(2,1)}, bf16[1024,1024]{1,0:T(8,128)(2,1)}), (bf16[512,1024]{1,0:T(8,128)(2,1)}, bf16[2048,1024]{1,0:T(8,128)(2,1)}, ...) | async-done | bytes 9437200 | tf_op jit(solution)/shard_map/psum | solution.py:697
  416.2 4.7 fusion.13
  420.9 10.7 %input_backward.5 = (f32[1024,512]{1,0:T(8,128)}, bf16[1024,512]{1,0:T(8,128)(2,1)}, f32[8,1024]{1,0:T(8,128)}, f32[8,1024]{1,0:T(8,128)}) custom-call(s32[1]{0:T(128)} %bitcast.me_ref, bf16[3072,1024]{1,0:T(8,128)(2,1)} %x_ref.7, f32[1,1024]{1,0:T(1,128)} %bitcast.66, f32[1,1024]{1,0:T(1,128)} %bitcast.70, bf16[1024,1536]{1,0:T(8,128)(2,1)} %copy.31.w_ref, ...), custom_call_target="tpu_custom_call" | custom-call | flops 1 | bytes 1 | tf_op jit(solution)/shard_map/input_backward/pallas_call | solution.py:534
  431.5 1.4 reduce_sum.121
  432.9 1.4 reduce_sum.122
  437.0 5.3 %collective-permute-start.17 = (bf16[192,512]{1,0:T(8,128)(2,1)S(1)}, bf16[192,512]{1,0:T(8,128)(2,1)S(1)}, u32[]{:S(2)}, u32[]{:S(2)}) collective-permute-start(bf16[192,512]{1,0:T(8,128)(2,1)S(1)} %fusion.6), channel_id=1, source_target_pairs={{0,8},{2,10},{4,12},{6,14},{8,16},{10,18},{12,20},{14,22},{16,24},... | collective-permute-start | bytes 589832 | tf_op jit(solution)/shard_map/ppermute | solution.py:668
  442.3 6.1 %maximum_convert_fusion.1 = f32[2048,1024]{1,0:T(8,128)} fusion(bf16[1024,1024]{1,0:T(8,128)(2,1)S(1)} %copy-done.3, bf16[1024,1024]{1,0:T(8,128)(2,1)} %get-tuple-element.129), kind=kLoop, calls=%fused_computation.5 | loop fusion | flops 8388608 | bytes 12582912 | tf_op jit(solution)/shard_map/concatenate | solution.py:767
  448.4 1.4 reduce_sum.119
  449.8 1.4 reduce_sum.120
  451.1 2.9 collective-permute-start.19
  454.2 7.9 %collective-permute-done.18 = bf16[192,512]{1,0:T(8,128)(2,1)S(1)} collective-permute-done((bf16[192,512]{1,0:T(8,128)(2,1)S(1)}, bf16[192,512]{1,0:T(8,128)(2,1)S(1)}, u32[]{:S(2)}, u32[]{:S(2)}) %collective-permute-start.18) | collective-permute-done | bytes 196640 | tf_op jit(solution)/shard_map/ppermute | solution.py:668
  465.7 1.5 collective-permute-start.20
  468.3 6.1 %maximum_convert_fusion = f32[1024,2048]{1,0:T(8,128)} fusion(bf16[1024,1024]{1,0:T(8,128)(2,1)S(1)} %copy-done.2, bf16[1024,1024]{1,0:T(8,128)(2,1)} %get-tuple-element.128), kind=kLoop, calls=%fused_computation.4 | loop fusion | flops 8388608 | bytes 12582912 | tf_op jit(solution)/shard_map/concatenate | solution.py:765
  474.4 1.6 convert_element_type.120
  476.0 10.4 %collective-permute-done.13 = f32[64,128]{1,0:T(8,128)S(1)} collective-permute-done((f32[64,128]{1,0:T(8,128)S(1)}, f32[64,128]{1,0:T(8,128)S(1)}, u32[]{:S(2)}, u32[]{:S(2)}) %collective-permute-start.13) | collective-permute-done | bytes 32800 | tf_op jit(solution)/shard_map/ppermute | solution.py:578
  486.4 2.6 collective-permute-start.14
  489.0 1.8 maximum_select_fusion.1
  490.8 3.2 convert_add_fusion.2
  494.0 2.5 collective-permute-start.15
  496.5 3.4 pad_maximum_fusion
  500.0 1.5 collective-permute-start.16
  504.4 3.3 maximum_select_fusion
  507.7 3.6 convert_bitcast_fusion
  (151 shorter events, 29.3 us)
Async XLA Ops:
  7.2 409.0 %all-reduce.3.cloned.1.call-start = ((), (), s32[]{:S(2)}) async-start(), calls=%async_computation | async-start | bytes 18874368 | tf_op jit(solution)/shard_map/psum | solution.py:697
  7.2 82.9 %collective-permute-start = (bf16[3072,512]{1,0:T(8,128)(2,1)}, bf16[3072,512]{1,0:T(8,128)(2,1)S(1)}, u32[]{:S(2)}, u32[]{:S(2)}) collective-permute-start(bf16[3072,512]{1,0:T(8,128)(2,1)} %refs_0_.3), channel_id=1, source_target_pairs={{0,1},{1,0},{2,3},{3,2},{4,5},{5,4},{6,7},{7,6},{8,9},{9,8},{10,11... | collective-permute-start | bytes 9437192 | tf_op jit(solution)/shard_map/ppermute | solution.py:679
  16.3 4.7 copy-start.21
  16.3 5.3 %copy-start.22 = (bf16[1024]{0:T(1024)(128)(2,1)S(1)}, bf16[1024]{0:T(1024)(128)(2,1)}, u32[]{:S(2)}) copy-start(bf16[1024]{0:T(1024)(128)(2,1)} %param.20) | copy-start | bytes 6148
  16.3 5.9 %copy-start.19 = (bf16[3,512]{1,0:T(4,128)(2,1)S(1)}, bf16[3,512]{1,0:T(4,128)(2,1)}, u32[]{:S(2)}) copy-start(bf16[3,512]{1,0:T(4,128)(2,1)} %param.23) | copy-start | bytes 9220
  16.3 6.5 %copy-start.23 = (bf16[1024]{0:T(1024)(128)(2,1)S(1)}, bf16[1024]{0:T(1024)(128)(2,1)}, u32[]{:S(2)}) copy-start(bf16[1024]{0:T(1024)(128)(2,1)} %param.19) | copy-start | bytes 6148
  16.3 7.1 %copy-start.24 = (bf16[1024]{0:T(1024)(128)(2,1)S(1)}, bf16[1024]{0:T(1024)(128)(2,1)}, u32[]{:S(2)}) copy-start(bf16[1024]{0:T(1024)(128)(2,1)} %param.21) | copy-start | bytes 6148
  46.5 43.0 %copy-start.20 = (bf16[2048]{0:T(1024)(128)(2,1)S(1)}, bf16[2048]{0:T(1024)(128)(2,1)}, u32[]{:S(2)}) copy-start(bf16[2048]{0:T(1024)(128)(2,1)} %param.27) | copy-start | bytes 12292
  90.1 1.6 copy-start.1
  211.8 84.8 %collective-permute-start.1 = (bf16[3072,512]{1,0:T(8,128)(2,1)}, bf16[3072,512]{1,0:T(8,128)(2,1)S(1)}, u32[]{:S(2)}, u32[]{:S(2)}) collective-permute-start(bf16[3072,512]{1,0:T(8,128)(2,1)} %get-tuple-element.79), channel_id=1, source_target_pairs={{0,1},{1,0},{2,3},{3,2},{4,5},{5,4},{6,7},{7,6},{8,9},{9,8},{10,11... | collective-permute-start | bytes 9437192 | tf_op jit(solution)/shard_map/ppermute | solution.py:571
  284.8 31.5 %collective-permute-start.2 = (bf16[1024,512]{1,0:T(8,128)(2,1)}, bf16[1024,512]{1,0:T(8,128)(2,1)}, u32[]{:S(2)}, u32[]{:S(2)}) collective-permute-start(bf16[1024,512]{1,0:T(8,128)(2,1)} %get-tuple-element.89), channel_id=1, source_target_pairs={{0,1},{1,0},{2,3},{3,2},{4,5},{5,4},{6,7},{7,6},{8,9},{9,8},{10,11... | collective-permute-start | bytes 3145736 | tf_op jit(solution)/shard_map/ppermute | solution.py:571
  296.6 10.2 %copy-start.5 = (bf16[3072,512]{1,0:T(8,128)(2,1)}, bf16[3072,512]{1,0:T(8,128)(2,1)S(1)}, u32[]{:S(2)}) copy-start(bf16[3072,512]{1,0:T(8,128)(2,1)S(1)} %collective-permute-done.1) | copy-start | bytes 9437188
  299.6 3.8 collective-permute-start.3
  306.8 12.8 %copy-start.25 = (bf16[512]{0:T(512)(128)(2,1)S(1)}, bf16[512]{0:T(512)(128)(2,1)}, u32[]{:S(2)}) copy-start(bf16[512]{0:T(512)(128)(2,1)} %param.25) | copy-start | bytes 3076
  306.8 12.9 %copy-start.26 = (bf16[512]{0:T(512)(128)(2,1)S(1)}, bf16[512]{0:T(512)(128)(2,1)}, u32[]{:S(2)}) copy-start(bf16[512]{0:T(512)(128)(2,1)} %param.29) | copy-start | bytes 3076
  306.8 12.9 %copy-start = (bf16[3072,512]{1,0:T(8,128)(2,1)S(1)}, bf16[3072,512]{1,0:T(8,128)(2,1)}, u32[]{:S(2)}) copy-start(bf16[3072,512]{1,0:T(8,128)(2,1)} %refs_0_.3) | copy-start | bytes 9437188
  316.3 4.5 copy-start.17
  316.3 4.5 copy-start.16
  316.3 5.1 copy-start.15
  316.3 5.7 %copy-start.14 = (f32[8,1024]{1,0:T(8,128)S(1)}, f32[8,1024]{1,0:T(8,128)}, u32[]{:S(2)}) copy-start(f32[8,1024]{1,0:T(8,128)} %get-tuple-element.115) | copy-start | bytes 98308
  316.3 6.3 %copy-start.13 = (f32[8,1024]{1,0:T(8,128)S(1)}, f32[8,1024]{1,0:T(8,128)}, u32[]{:S(2)}) copy-start(f32[8,1024]{1,0:T(8,128)} %get-tuple-element.116) | copy-start | bytes 98308
  316.3 6.9 %copy-start.11 = (f32[8,1024]{1,0:T(8,128)S(1)}, f32[8,1024]{1,0:T(8,128)}, u32[]{:S(2)}) copy-start(f32[8,1024]{1,0:T(8,128)} %get-tuple-element.119) | copy-start | bytes 98308
  316.3 7.5 %copy-start.12 = (f32[8,1024]{1,0:T(8,128)S(1)}, f32[8,1024]{1,0:T(8,128)}, u32[]{:S(2)}) copy-start(f32[8,1024]{1,0:T(8,128)} %get-tuple-element.120) | copy-start | bytes 98308
  319.2 5.2 %collective-permute-start.4 = (bf16[1536,256]{1,0:T(8,128)(2,1)}, bf16[1536,256]{1,0:T(8,128)(2,1)}, u32[]{:S(2)}, u32[]{:S(2)}) collective-permute-start(bf16[1536,256]{1,0:T(8,128)(2,1)} %pick_half.3), channel_id=1, source_target_pairs={{0,2},{2,0},{4,6},{6,4},{8,10},{10,8},{12,14},{14,12},{16,18},{18,... | collective-permute-start | bytes 2359304 | tf_op jit(solution)/shard_map/ppermute | solution.py:614
  324.4 14.1 %collective-permute-start.6 = (bf16[768,256]{1,0:T(8,128)(2,1)}, bf16[768,256]{1,0:T(8,128)(2,1)}, u32[]{:S(2)}, u32[]{:S(2)}) collective-permute-start(bf16[768,256]{1,0:T(8,128)(2,1)} %get-tuple-element.102), channel_id=1, source_target_pairs={{0,4},{2,6},{4,0},{6,2},{8,12},{10,14},{12,8},{14,10},{16,20},{18,... | collective-permute-start | bytes 1179656 | tf_op jit(solution)/shard_map/ppermute | solution.py:637
  327.8 24.1 %collective-permute-start.7 = (bf16[768,256]{1,0:T(8,128)(2,1)}, bf16[768,256]{1,0:T(8,128)(2,1)S(1)}, u32[]{:S(2)}, u32[]{:S(2)}) collective-permute-start(bf16[768,256]{1,0:T(8,128)(2,1)} %get-tuple-element.103), channel_id=1, source_target_pairs={{0,4},{2,6},{4,0},{6,2},{8,12},{10,14},{12,8},{14,10},{16,20},{18,... | collective-permute-start | bytes 1179656 | tf_op jit(solution)/shard_map/ppermute | solution.py:637
  351.6 85.4 %collective-permute-start.5 = (bf16[1024,512]{1,0:T(8,128)(2,1)}, bf16[1024,512]{1,0:T(8,128)(2,1)}, u32[]{:S(2)}, u32[]{:S(2)}) collective-permute-start(bf16[1024,512]{1,0:T(8,128)(2,1)} %get-tuple-element.101), channel_id=1, source_target_pairs={{0,1},{1,0},{2,3},{3,2},{4,5},{5,4},{6,7},{7,6},{8,9},{9,8},{10,11... | collective-permute-start | bytes 3145736 | tf_op jit(solution)/shard_map/ppermute | solution.py:571
  356.1 79.5 %collective-permute-start.10 = (bf16[192,512]{1,0:T(8,128)(2,1)}, bf16[192,512]{1,0:T(8,128)(2,1)S(1)}, u32[]{:S(2)}, u32[]{:S(2)}) collective-permute-start(bf16[192,512]{1,0:T(8,128)(2,1)} %get-tuple-element.136), channel_id=1, source_target_pairs={{0,16},{2,18},{4,20},{6,22},{8,24},{10,26},{12,28},{14,30},{16,0},... | collective-permute-start | bytes 589832 | tf_op jit(solution)/shard_map/ppermute | solution.py:657
  360.2 75.4 %collective-permute-start.11 = (bf16[192,512]{1,0:T(8,128)(2,1)}, bf16[192,512]{1,0:T(8,128)(2,1)}, u32[]{:S(2)}, u32[]{:S(2)}) collective-permute-start(bf16[192,512]{1,0:T(8,128)(2,1)} %get-tuple-element.137), channel_id=1, source_target_pairs={{0,24},{2,26},{4,28},{6,30},{8,0},{10,2},{12,4},{14,6},{16,8},{18,... | collective-permute-start | bytes 589832 | tf_op jit(solution)/shard_map/ppermute | solution.py:657
  361.4 74.2 %collective-permute-start.9 = (bf16[192,512]{1,0:T(8,128)(2,1)S(1)}, bf16[192,512]{1,0:T(8,128)(2,1)}, u32[]{:S(2)}, u32[]{:S(2)}) collective-permute-start(bf16[192,512]{1,0:T(8,128)(2,1)S(1)} %get-tuple-element.135), channel_id=1, source_target_pairs={{0,8},{2,10},{4,12},{6,14},{8,16},{10,18},{12,20},{14,22},{16,24},... | collective-permute-start | bytes 589832 | tf_op jit(solution)/shard_map/ppermute | solution.py:657
  434.3 8.0 %copy-start.3 = (bf16[1024,1024]{1,0:T(8,128)(2,1)S(1)}, bf16[1024,1024]{1,0:T(8,128)(2,1)}, u32[]{:S(2)}) copy-start(bf16[1024,1024]{1,0:T(8,128)(2,1)} %get-tuple-element.130) | copy-start | bytes 6291460
  434.3 27.8 %collective-permute-start.8 = (bf16[1024,512]{1,0:T(8,128)(2,1)}, bf16[1024,512]{1,0:T(8,128)(2,1)}, u32[]{:S(2)}, u32[]{:S(2)}) collective-permute-start(bf16[1024,512]{1,0:T(8,128)(2,1)} %get-tuple-element.106), channel_id=1, source_target_pairs={{0,1},{1,0},{2,3},{3,2},{4,5},{5,4},{6,7},{7,6},{8,9},{9,8},{10,11... | collective-permute-start | bytes 3145736 | tf_op jit(solution)/shard_map/ppermute | solution.py:571
  437.0 17.2 %collective-permute-start.17 = (bf16[192,512]{1,0:T(8,128)(2,1)S(1)}, bf16[192,512]{1,0:T(8,128)(2,1)S(1)}, u32[]{:S(2)}, u32[]{:S(2)}) collective-permute-start(bf16[192,512]{1,0:T(8,128)(2,1)S(1)} %fusion.6), channel_id=1, source_target_pairs={{0,8},{2,10},{4,12},{6,14},{8,16},{10,18},{12,20},{14,22},{16,24},... | collective-permute-start | bytes 589832 | tf_op jit(solution)/shard_map/ppermute | solution.py:668
  451.1 17.2 %copy-start.2 = (bf16[1024,1024]{1,0:T(8,128)(2,1)S(1)}, bf16[1024,1024]{1,0:T(8,128)(2,1)}, u32[]{:S(2)}) copy-start(bf16[1024,1024]{1,0:T(8,128)(2,1)} %get-tuple-element.131) | copy-start | bytes 6291460
  451.1 10.9 %collective-permute-start.18 = (bf16[192,512]{1,0:T(8,128)(2,1)S(1)}, bf16[192,512]{1,0:T(8,128)(2,1)S(1)}, u32[]{:S(2)}, u32[]{:S(2)}) collective-permute-start(bf16[192,512]{1,0:T(8,128)(2,1)S(1)} %fusion.6), channel_id=1, source_target_pairs={{0,16},{2,18},{4,20},{6,22},{8,24},{10,26},{12,28},{14,30},{16,0},... | collective-permute-start | bytes 589832 | tf_op jit(solution)/shard_map/ppermute | solution.py:668
  451.1 14.5 %collective-permute-start.19 = (bf16[192,512]{1,0:T(8,128)(2,1)S(1)}, bf16[192,512]{1,0:T(8,128)(2,1)S(1)}, u32[]{:S(2)}, u32[]{:S(2)}) collective-permute-start(bf16[192,512]{1,0:T(8,128)(2,1)S(1)} %fusion.6), channel_id=1, source_target_pairs={{0,24},{2,26},{4,28},{6,30},{8,0},{10,2},{12,4},{14,6},{16,8},{18,... | collective-permute-start | bytes 589832 | tf_op jit(solution)/shard_map/ppermute | solution.py:668
  465.6 1.6 collective-permute-start.12
  465.7 23.3 %collective-permute-start.20 = (bf16[768,512]{1,0:T(8,128)(2,1)S(1)}, bf16[768,512]{1,0:T(8,128)(2,1)S(1)}, u32[]{:S(2)}, u32[]{:S(2)}) collective-permute-start(bf16[768,512]{1,0:T(8,128)(2,1)S(1)} %constant_dynamic-update-slice_fusion.4), channel_id=1, source_target_pairs={{0,4},{2,6},{4,0},{6,2},{8,12},{10,14},{12,8},{14,10},{16,20},{18,... | collective-permute-start | bytes 2359304 | tf_op jit(solution)/shard_map/ppermute | solution.py:642
  467.2 19.2 %collective-permute-start.13 = (f32[64,128]{1,0:T(8,128)S(1)}, f32[64,128]{1,0:T(8,128)S(1)}, u32[]{:S(2)}, u32[]{:S(2)}) collective-permute-start(f32[64,128]{1,0:T(8,128)S(1)} %bitcast_add_fusion), channel_id=1, source_target_pairs={{0,4},{2,6},{4,0},{6,2},{8,12},{10,14},{12,8},{14,10},{16,20},{18,... | collective-permute-start | bytes 98312 | tf_op jit(solution)/shard_map/ppermute | solution.py:578
  468.3 6.1 %copy-start.9 = (bf16[512,1024]{1,0:T(8,128)(2,1)S(1)}, bf16[512,1024]{1,0:T(8,128)(2,1)}, u32[]{:S(2)}) copy-start(bf16[512,1024]{1,0:T(8,128)(2,1)} %get-tuple-element.126) | copy-start | bytes 3145732
  474.4 16.4 %copy-start.6 = (f32[1024,512]{1,0:T(8,128)S(1)}, f32[1024,512]{1,0:T(8,128)}, u32[]{:S(2)}) copy-start(f32[1024,512]{1,0:T(8,128)} %get-tuple-element.88) | copy-start | bytes 6291460
  474.4 16.4 %copy-start.7 = (f32[1024,512]{1,0:T(8,128)S(1)}, f32[1024,512]{1,0:T(8,128)}, u32[]{:S(2)}) copy-start(f32[1024,512]{1,0:T(8,128)} %get-tuple-element.100) | copy-start | bytes 6291460
  474.4 16.4 %copy-start.8 = (f32[1024,512]{1,0:T(8,128)S(1)}, f32[1024,512]{1,0:T(8,128)}, u32[]{:S(2)}) copy-start(f32[1024,512]{1,0:T(8,128)} %get-tuple-element.105) | copy-start | bytes 6291460
  486.4 7.6 %collective-permute-start.14 = (f32[64,128]{1,0:T(8,128)S(1)}, f32[64,128]{1,0:T(8,128)S(1)}, u32[]{:S(2)}, u32[]{:S(2)}) collective-permute-start(f32[64,128]{1,0:T(8,128)S(1)} %fusion.15), channel_id=1, source_target_pairs={{0,8},{2,10},{4,12},{6,14},{8,0},{10,2},{12,4},{14,6},{16,24},{18,... | collective-permute-start | bytes 98312 | tf_op jit(solution)/shard_map/ppermute | solution.py:578
  490.8 13.6 %collective-permute-start.21 = (bf16[1536,512]{1,0:T(8,128)(2,1)}, bf16[1536,512]{1,0:T(8,128)(2,1)}, u32[]{:S(2)}, u32[]{:S(2)}) collective-permute-start(bf16[1536,512]{1,0:T(8,128)(2,1)} %maximum_select_fusion.1), channel_id=1, source_target_pairs={{0,2},{2,0},{4,6},{6,4},{8,10},{10,8},{12,14},{14,12},{16,18},{18,... | collective-permute-start | bytes 4718600 | tf_op jit(solution)/shard_map/ppermute | solution.py:642
  494.0 5.9 %collective-permute-start.15 = (f32[64,128]{1,0:T(8,128)S(1)}, f32[64,128]{1,0:T(8,128)S(1)}, u32[]{:S(2)}, u32[]{:S(2)}) collective-permute-start(f32[64,128]{1,0:T(8,128)S(1)} %add.184), channel_id=1, source_target_pairs={{0,16},{2,18},{4,20},{6,22},{8,24},{10,26},{12,28},{14,30},{16,0},... | collective-permute-start | bytes 98312 | tf_op jit(solution)/shard_map/ppermute | solution.py:578
  500.0 3.8 collective-permute-start.16
  502.1 9.2 %copy-start.18 = (f32[512]{0:T(512)}, f32[512]{0:T(512)S(1)}, u32[]{:S(2)}) copy-start(f32[512]{0:T(512)S(1)} %slice_bitcast_fusion.1) | copy-start | bytes 6148
  (2 other events, 1.6 us)
Sparse Core Ops, SparseCore 0:
  212.0 204.1 all-reduce.2
